TPU v7x, 512 devices: a whole 4x4x16 slice. The times are simulated.
512 devices in a mesh: section: 16 (over x_lo, y, core), seq: 32 (over x_hi, z).
Axes of the slice: x: 4 (x_hi: 2, x_lo: 2; x = x_hi * 2 + x_lo), y: 4, z: 16, core: 2. Of those that a mesh axis runs over, the one named last changes fastest.
Arguments:
- queries: bfloat16 [32768, 4096], P(('section', 'seq')), may hold values from -120 to 120
- keys: bfloat16 [32768, 4096], P(('section', 'seq')), may hold values from -6 to 6
- values: bfloat16 [32768, 4096], P(('section', 'seq')), may hold values from -6 to 6
- queue_state: bfloat16 [32768, 4096], P(('section', 'seq')), may hold values from -6 to 6
- fresh_state: bfloat16 [2048, 4096], P('seq'), may hold values from -6 to 6
- timestep: int32 [16], P('section'), may hold values from 1 to 15
- window_start: int32 [16, 2], P('section'), may hold values from -1 to 0, as said below
- modulation: float32 [16, 4096], replicated, may hold values from 0.1 to 1.9
Outputs:
- velocity: bfloat16 [32768, 4096], P(('section', 'seq'))
- advanced: bfloat16 [32768, 4096], P(('section', 'seq'))
Inputs may be any that keep to these rules, and one draw needn't show every extreme that they name: `window_start`: each offset is -1 or 0.
All inputs are finite; a program needn't handle non-finite values.
Results may differ from a plain program's by a relative error of at most 0.0057.
Values may be sent and summed in bfloat16 or wider, within the bound.
No kernel may reach another device: no remote copies, remote signals or barrier semaphores. Data moves between devices by JAX's collectives and lax.ppermute only.
A program may use at most 64 MiB of HBM per device.

v0:
```python
import math

import jax
import jax.numpy as jnp
from jax import lax
from jax.sharding import PartitionSpec as P

HEAD_DIM = 128
FRAMES = 2
NSTEPS = 16


def with_halo(shard, sides, width):
    for axis, dim in sides:
        devices, length = (lax.axis_size(axis), shard.shape[dim])
        up = [(i, (i + 1) % devices) for i in range(devices - 1)]
        down = [(j, i) for i, j in up]
        last = lax.slice_in_dim(shard, length - width, length, axis=dim)
        leading = lax.slice_in_dim(shard, 0, width, axis=dim)
        before = lax.ppermute(last, axis, up)
        after = lax.ppermute(leading, axis, down)
        shard = jnp.concatenate([before, shard, after], axis=dim)
    return shard


def passed_along(value, axis, steps):
    count = lax.axis_size(axis)
    leading, last = (max(0, -steps), min(count, count - steps))
    return lax.ppermute(value, axis, [(source, source + steps) for source in range(leading, last)])


def level(step):
    share = step.astype(jnp.float32) / NSTEPS
    return 5.0 * share / (1.0 + 4.0 * share)


def attend(query_block, key_window, value_window, valid):
    scores = jnp.einsum(
        "qhd,khd->hqk", query_block, key_window, preferred_element_type=jnp.float32
    ) / jnp.sqrt(jnp.float32(HEAD_DIM))
    scores = jnp.where(valid[None, None, :], scores, -jnp.inf)
    peak = jnp.max(scores, axis=-1, keepdims=True)
    expo = jnp.exp(scores - peak)
    total = jnp.sum(expo, axis=-1)
    weights = expo.astype(jnp.bfloat16)
    mixed = jnp.einsum("hqk,khd->qhd", weights, value_window, preferred_element_type=jnp.float32)
    return (mixed / jnp.transpose(total)[:, :, None]).astype(jnp.bfloat16)


def per_device(queries, keys, values, queue_state, fresh_state, timestep, window_start, modulation):
    tok_dev, feat = queries.shape
    group_size = lax.axis_size("seq")
    section_tok = tok_dev * group_size
    frame_tok = section_tok // FRAMES
    head_cols = feat // group_size
    head_count = head_cols // HEAD_DIM
    position = lax.axis_index("section")
    final = lax.axis_size("section") - 1
    query_heads, key_heads, value_heads = (
        lax.all_to_all(queries, "seq", split_axis=1, concat_axis=0, tiled=True),
        lax.all_to_all(keys, "seq", split_axis=1, concat_axis=0, tiled=True),
        lax.all_to_all(values, "seq", split_axis=1, concat_axis=0, tiled=True),
    )
    paired = jnp.concatenate([key_heads, value_heads], axis=1)
    extended = with_halo(paired, (("section", 0),), frame_tok)
    query_split = query_heads.reshape(section_tok, head_count, HEAD_DIM)
    key_split = extended[:, :head_cols].reshape(-1, head_count, HEAD_DIM)
    value_split = extended[:, head_cols:].reshape(-1, head_count, HEAD_DIM)
    block = math.gcd(frame_tok, 512)
    pieces = []
    for frame in range(FRAMES):
        lead = frame + window_start[0, frame]
        first = (lead + 1) * frame_tok
        key_window = lax.dynamic_slice_in_dim(key_split, first, 2 * frame_tok, 0)
        value_window = lax.dynamic_slice_in_dim(value_split, first, 2 * frame_tok, 0)
        key_frame = lead + jnp.arange(2 * frame_tok, dtype=jnp.int32) // frame_tok
        valid = ((key_frame >= 0) | (position > 0)) & ((key_frame < FRAMES) | (position < final))
        for index_block in range(frame_tok // block):
            begin = frame * frame_tok + index_block * block
            pieces.append(
                attend(query_split[begin : begin + block], key_window, value_window, valid)
            )
    attended_heads = jnp.concatenate(pieces, axis=0).reshape(section_tok, head_cols)
    attended = lax.all_to_all(
        attended_heads, "seq", split_axis=0, concat_axis=1, tiled=True
    ).astype(jnp.float32)
    scale = jnp.sqrt(jnp.mean(attended * attended, axis=-1, keepdims=True) + 1e-06)
    step = timestep[0]
    gain = lax.dynamic_index_in_dim(modulation, step, 0, keepdims=False)
    moving = attended / scale * gain[None, :]
    delta = level(step - 1) - level(step)
    updated = (queue_state.astype(jnp.float32) + delta * moving).astype(jnp.bfloat16)
    shifted = passed_along(updated, "section", 1)
    advanced = jnp.where(position == 0, fresh_state, shifted)
    return (moving.astype(jnp.bfloat16), advanced)


def solution(mesh):
    return jax.shard_map(
        per_device,
        mesh=mesh,
        in_specs=(
            P(("section", "seq"), None),
            P(("section", "seq"), None),
            P(("section", "seq"), None),
            P(("section", "seq"), None),
            P("seq", None),
            P("section"),
            P("section", None),
            P(),
        ),
        out_specs=(P(("section", "seq"), None), P(("section", "seq"), None)),
        check_vma=False,
    )
```

profile of v0, /device:TPU:34, one launch (start us, length us, event | category | flops | bytes accessed | tf_op | source)
XLA Modules:
  0.0 197.6 jit_solution(9542367396306694937)
XLA Ops:
  0.6 0.0 copy-start
  0.6 0.0 copy-start.1
  0.7 0.0 copy-start.4
  0.7 1.0 copy-done
  1.7 0.9 copy_bitcast_fusion.2
  2.6 16.9 %all-to-all-start = ((bf16[64,32,128]{2,0,1:T(8,128)(2,1)}), bf16[64,32,128]{2,0,1:T(8,128)(2,1)S(1)}, u32[]{:S(2)}, u32[]{:S(2)}) async-start(bf16[64,32,128]{2,0,1:T(8,128)(2,1)} %copy_bitcast_fusion.2), calls=%async_computation | async-start | bytes 1048576 | tf_op jit(solution)/shard_map/all_to_all | solution.py:61
  19.5 2.0 %copy_bitcast_fusion.1 = bf16[64,32,128]{2,0,1:T(8,128)(2,1)} fusion(bf16[64,4096]{1,0:T(8,128)(2,1)} %param.10), kind=kLoop, calls=%fused_computation.55 | loop fusion | bytes 1048576 | tf_op jit(solution)/shard_map/all_to_all | solution.py:62
  21.5 31.8 %all-to-all-done = bf16[64,32,128]{2,0,1:T(8,128)(2,1)S(1)} async-done(((bf16[64,32,128]{2,0,1:T(8,128)(2,1)}), bf16[64,32,128]{2,0,1:T(8,128)(2,1)S(1)}, u32[]{:S(2)}, u32[]{:S(2)}) %all-to-all-start) | async-done | bytes 524320 | tf_op jit(solution)/shard_map/all_to_all | solution.py:61
  53.3 4.2 %all-to-all-start.1 = ((bf16[64,32,128]{2,0,1:T(8,128)(2,1)}), bf16[64,32,128]{2,0,1:T(8,128)(2,1)S(1)}, u32[]{:S(2)}, u32[]{:S(2)}) async-start(bf16[64,32,128]{2,0,1:T(8,128)(2,1)} %copy_bitcast_fusion.1), calls=%async_computation.1 | async-start | bytes 1048576 | tf_op jit(solution)/shard_map/all_to_all | solution.py:62
  57.4 0.0 copy-done.1
  57.5 0.9 copy_bitcast_fusion
  58.4 32.9 %all-to-all-done.1 = bf16[64,32,128]{2,0,1:T(8,128)(2,1)S(1)} async-done(((bf16[64,32,128]{2,0,1:T(8,128)(2,1)}), bf16[64,32,128]{2,0,1:T(8,128)(2,1)S(1)}, u32[]{:S(2)}, u32[]{:S(2)}) %all-to-all-start.1) | async-done | bytes 524320 | tf_op jit(solution)/shard_map/all_to_all | solution.py:62
  91.3 4.1 %all-to-all-start.2 = ((bf16[64,32,128]{2,0,1:T(8,128)(2,1)}), bf16[64,32,128]{2,0,1:T(8,128)(2,1)S(1)}, u32[]{:S(2)}, u32[]{:S(2)}) async-start(bf16[64,32,128]{2,0,1:T(8,128)(2,1)} %copy_bitcast_fusion), calls=%async_computation.2 | async-start | bytes 1048576 | tf_op jit(solution)/shard_map/all_to_all | solution.py:60
  95.5 0.1 fusion.74
  95.6 1.9 collective-permute-start
  97.5 5.8 %collective-permute-start.1 = (bf16[1024,256]{1,0:T(8,128)(2,1)S(1)}, bf16[1024,256]{1,0:T(8,128)(2,1)}, u32[]{:S(2)}, u32[]{:S(2)}) collective-permute-start(bf16[1024,256]{1,0:T(8,128)(2,1)S(1)} %get-tuple-element.11), channel_id=1, source_target_pairs={{32,0},{64,32},{96,64},{128,96},{160,128},{192,160},{224,192},{256... | collective-permute-start | bytes 1572872 | tf_op jit(solution)/shard_map/ppermute | solution.py:21
  103.3 0.0 copy-done.4
  103.3 0.7 fusion.121
  106.0 0.7 fusion.97
  106.7 22.7 %all-to-all-done.2 = bf16[64,32,128]{2,0,1:T(8,128)(2,1)S(1)} async-done(((bf16[64,32,128]{2,0,1:T(8,128)(2,1)}), bf16[64,32,128]{2,0,1:T(8,128)(2,1)S(1)}, u32[]{:S(2)}, u32[]{:S(2)}) %all-to-all-start.2) | async-done | bytes 524320 | tf_op jit(solution)/shard_map/all_to_all | solution.py:60
  129.4 0.0 collective-permute-done
  129.4 0.0 collective-permute-done.1
  129.4 1.4 pad_maximum_fusion
  130.8 0.1 fusion.119
  130.9 1.6 fusion
  132.5 1.4 fusion.4
  133.9 1.2 fusion.69
  135.1 1.0 fusion.6
  136.1 1.2 fusion.60
  137.3 1.5 fusion.2
  138.9 1.4 fusion.8
  140.3 1.2 fusion.51
  141.5 1.0 fusion.10
  142.6 0.0 copy-start.3
  142.6 1.2 fusion.42
  143.8 0.0 copy-start.2
  143.8 1.0 copy.23
  144.8 4.1 %all-to-all-start.3 = ((bf16[32,64,128]{2,1,0:T(8,128)(2,1)}), bf16[32,64,128]{2,1,0:T(8,128)(2,1)S(1)}, u32[]{:S(2)}, u32[]{:S(2)}) async-start(bf16[32,64,128]{2,1,0:T(8,128)(2,1)} %bitcast.20), calls=%async_computation.3 | async-start | bytes 1048576 | tf_op jit(solution)/shard_map/all_to_all | solution.py:84
  149.7 0.9 constant_dynamic-slice_fusion
  150.7 32.2 %all-to-all-done.3 = bf16[32,64,128]{2,1,0:T(8,128)(2,1)S(1)} async-done(((bf16[32,64,128]{2,1,0:T(8,128)(2,1)}), bf16[32,64,128]{2,1,0:T(8,128)(2,1)S(1)}, u32[]{:S(2)}, u32[]{:S(2)}) %all-to-all-start.3) | async-done | bytes 524320 | tf_op jit(solution)/shard_map/all_to_all | solution.py:84
  182.8 0.2 fusion.72
  183.1 0.0 copy-done.3
  183.1 1.1 add_convert_fusion
  184.2 1.9 collective-permute-start.2
  186.1 10.7 %collective-permute-done.2 = bf16[64,4096]{1,0:T(8,128)(2,1)S(1)} collective-permute-done((bf16[64,4096]{1,0:T(8,128)(2,1)S(1)}, bf16[64,4096]{1,0:T(8,128)(2,1)S(1)}, u32[]{:S(2)}, u32[]{:S(2)}) %collective-permute-start.2) | collective-permute-done | bytes 524320 | tf_op jit(solution)/shard_map/ppermute | solution.py:29
  196.8 0.0 copy-done.2
  196.8 0.8 broadcast_select_fusion
  (3 shorter events, 0.1 us)
Async XLA Ops:
  0.6 1.0 copy-start
  0.6 56.8 %copy-start.1 = (bf16[64,4096]{1,0:T(8,128)(2,1)S(1)}, bf16[64,4096]{1,0:T(8,128)(2,1)}, u32[]{:S(2)}) copy-start(bf16[64,4096]{1,0:T(8,128)(2,1)} %param.8) | copy-start | bytes 1572868
  0.7 102.6 %copy-start.4 = (s32[1,2]{1,0:T(1,128)S(1)}, s32[1,2]{1,0:T(1,128)}, u32[]{:S(2)}) copy-start(s32[1,2]{1,0:T(1,128)} %param.14) | copy-start | bytes 28
  2.6 50.7 %all-to-all-start = ((bf16[64,32,128]{2,0,1:T(8,128)(2,1)}), bf16[64,32,128]{2,0,1:T(8,128)(2,1)S(1)}, u32[]{:S(2)}, u32[]{:S(2)}) async-start(bf16[64,32,128]{2,0,1:T(8,128)(2,1)} %copy_bitcast_fusion.2), calls=%async_computation | async-start | bytes 1048576 | tf_op jit(solution)/shard_map/all_to_all | solution.py:61
  53.3 38.0 %all-to-all-start.1 = ((bf16[64,32,128]{2,0,1:T(8,128)(2,1)}), bf16[64,32,128]{2,0,1:T(8,128)(2,1)S(1)}, u32[]{:S(2)}, u32[]{:S(2)}) async-start(bf16[64,32,128]{2,0,1:T(8,128)(2,1)} %copy_bitcast_fusion.1), calls=%async_computation.1 | async-start | bytes 1048576 | tf_op jit(solution)/shard_map/all_to_all | solution.py:62
  91.3 38.0 %all-to-all-start.2 = ((bf16[64,32,128]{2,0,1:T(8,128)(2,1)}), bf16[64,32,128]{2,0,1:T(8,128)(2,1)S(1)}, u32[]{:S(2)}, u32[]{:S(2)}) async-start(bf16[64,32,128]{2,0,1:T(8,128)(2,1)} %copy_bitcast_fusion), calls=%async_computation.2 | async-start | bytes 1048576 | tf_op jit(solution)/shard_map/all_to_all | solution.py:60
  95.6 33.8 %collective-permute-start = (bf16[1024,256]{1,0:T(8,128)(2,1)S(1)}, bf16[1024,256]{1,0:T(8,128)(2,1)}, u32[]{:S(2)}, u32[]{:S(2)}) collective-permute-start(bf16[1024,256]{1,0:T(8,128)(2,1)S(1)} %get-tuple-element.10), channel_id=1, source_target_pairs={{0,32},{32,64},{64,96},{96,128},{128,160},{160,192},{192,224},{224... | collective-permute-start | bytes 1572872 | tf_op jit(solution)/shard_map/ppermute | solution.py:20
  97.5 31.9 %collective-permute-start.1 = (bf16[1024,256]{1,0:T(8,128)(2,1)S(1)}, bf16[1024,256]{1,0:T(8,128)(2,1)}, u32[]{:S(2)}, u32[]{:S(2)}) collective-permute-start(bf16[1024,256]{1,0:T(8,128)(2,1)S(1)} %get-tuple-element.11), channel_id=1, source_target_pairs={{32,0},{64,32},{96,64},{128,96},{160,128},{192,160},{224,192},{256... | collective-permute-start | bytes 1572872 | tf_op jit(solution)/shard_map/ppermute | solution.py:21
  142.6 40.5 %copy-start.3 = (bf16[64,4096]{1,0:T(8,128)(2,1)S(1)}, bf16[64,4096]{1,0:T(8,128)(2,1)}, u32[]{:S(2)}) copy-start(bf16[64,4096]{1,0:T(8,128)(2,1)} %param.11) | copy-start | bytes 1572868
  143.8 53.0 %copy-start.2 = (bf16[64,4096]{1,0:T(8,128)(2,1)S(1)}, bf16[64,4096]{1,0:T(8,128)(2,1)}, u32[]{:S(2)}) copy-start(bf16[64,4096]{1,0:T(8,128)(2,1)} %param.12) | copy-start | bytes 1572868
  144.8 38.0 %all-to-all-start.3 = ((bf16[32,64,128]{2,1,0:T(8,128)(2,1)}), bf16[32,64,128]{2,1,0:T(8,128)(2,1)S(1)}, u32[]{:S(2)}, u32[]{:S(2)}) async-start(bf16[32,64,128]{2,1,0:T(8,128)(2,1)} %bitcast.20), calls=%async_computation.3 | async-start | bytes 1048576 | tf_op jit(solution)/shard_map/all_to_all | solution.py:84
  184.2 12.6 %collective-permute-start.2 = (bf16[64,4096]{1,0:T(8,128)(2,1)S(1)}, bf16[64,4096]{1,0:T(8,128)(2,1)S(1)}, u32[]{:S(2)}, u32[]{:S(2)}) collective-permute-start(bf16[64,4096]{1,0:T(8,128)(2,1)S(1)} %get-tuple-element.8), channel_id=1, source_target_pairs={{0,32},{32,64},{64,96},{96,128},{128,160},{160,192},{192,224},{224... | collective-permute-start | bytes 1572872 | tf_op jit(solution)/shard_map/ppermute | solution.py:29
where the time goes:
time: 198 us
  waiting for transfers between devices  130 us (66%)
  starting transfers between devices  38.9 us (20%)
  matrix products  10.7 us (5%)
  local copies, waits for them, and re-layouts  7.65 us (4%)
  other arithmetic  6.44 us (3%)
  between operations  3.67 us (2%)
    all_to_all x1, waiting for transfers between devices, per_device(): lax.all_to_all(values, 'seq', split_axis=1, concat_axis=0, tiled=True)  32.9 us
    all_to_all x1, waiting for transfers between devices, per_device(): lax.all_to_all(attended_heads, 'seq', split_axis=0, concat_axis=1, tiled=...  32.2 us
    all_to_all x1, waiting for transfers between devices, per_device(): lax.all_to_all(keys, 'seq', split_axis=1, concat_axis=0, tiled=True)  31.8 us
    all_to_all x1, waiting for transfers between devices, per_device(): lax.all_to_all(queries, 'seq', split_axis=1, concat_axis=0, tiled=True)  22.7 us
    all_to_all x1, starting transfers between devices, per_device(): lax.all_to_all(keys, 'seq', split_axis=1, concat_axis=0, tiled=True)  16.9 us
    ppermute x1, waiting for transfers between devices, passed_along(): lax.ppermute(value, axis, [(source, source + steps) for source in range(l...  10.7 us
    dot_general x4, matrix products, attend(): jnp.einsum('qhd,khd->hqk', query_block, key_window, preferred_element_typ...  5.94 us
    ppermute x1, starting transfers between devices, with_halo(): after = lax.ppermute(leading, axis, down)  5.75 us
  transfers between devices with their start and end apart: 7, of which 5 were waited for; matrix products, arithmetic and copies ran while one was open for 3% of the time, Pallas kernels for 0%

commit v1 on v0

v1 whole, which is shorter than its diff:
```python
import functools

import jax
import jax.numpy as jnp
from jax import lax
from jax.experimental import pallas as pl
from jax.experimental.pallas import tpu as pltpu
from jax.sharding import PartitionSpec as P

HEAD_DIM = 128
FRAMES = 2
NSTEPS = 16
LOG2E = 1.4426950408889634
VMEM = pl.BlockSpec(memory_space=pltpu.VMEM)
SMEM = pl.BlockSpec(memory_space=pltpu.SMEM)
BIG = 48 * 1024 * 1024


def level(step):
    share = step / NSTEPS
    return 5.0 * share / (1.0 + 4.0 * share)


def pack_kernel(q_ref, k_ref, v_ref, out_ref):
    for head in range(out_ref.shape[0]):
        cols = slice(head * HEAD_DIM, (head + 1) * HEAD_DIM)
        for part, ref in enumerate((q_ref, k_ref, v_ref)):
            out_ref[head, :, part * HEAD_DIM : (part + 1) * HEAD_DIM] = ref[:, cols]


def pack(queries, keys, values):
    tok, feat = queries.shape
    heads = feat // HEAD_DIM
    group = 8
    block = pl.BlockSpec((tok, group * HEAD_DIM), lambda i: (0, i))
    return pl.pallas_call(
        pack_kernel,
        grid=(heads // group,),
        in_specs=[block] * 3,
        out_specs=pl.BlockSpec((group, tok, 3 * HEAD_DIM), lambda i: (i, 0, 0)),
        out_shape=jax.ShapeDtypeStruct((heads, tok, 3 * HEAD_DIM), queries.dtype),
    )(queries, keys, values)


def attend_kernel(final, ws_ref, qkv_ref, before_ref, after_ref, out_ref, key_ref, value_ref):
    frame_tok = qkv_ref.shape[0] // FRAMES
    position = lax.axis_index("section")
    block = 256
    k_cols, v_cols = slice(HEAD_DIM, 2 * HEAD_DIM), slice(2 * HEAD_DIM, 3 * HEAD_DIM)
    ones = jnp.ones((2 * frame_tok, HEAD_DIM), jnp.bfloat16)
    value_ref[:, HEAD_DIM:] = ones

    def run(frame, length):
        keys, vals = key_ref[:length], value_ref[:length]
        for index in range(frame_tok // block):
            rows = pl.ds(frame * frame_tok + index * block, block)
            q = qkv_ref[rows, :HEAD_DIM]
            s = lax.dot_general(q, keys, (((1,), (1,)), ((), ())), preferred_element_type=jnp.float32)
            peak = jnp.max(s, axis=-1, keepdims=True)
            w = jnp.exp2((s - peak) * (LOG2E / HEAD_DIM**0.5)).astype(jnp.bfloat16)
            mixed = jnp.dot(w, vals, preferred_element_type=jnp.float32)
            out_ref[rows, :] = (mixed[:, :HEAD_DIM] / mixed[:, HEAD_DIM:]).astype(jnp.bfloat16)

    for frame in range(FRAMES):
        own = pl.ds(frame * frame_tok, frame_tok)
        key_ref[:frame_tok] = qkv_ref[own, k_cols]
        value_ref[:frame_tok, :HEAD_DIM] = qkv_ref[own, v_cols]
        start = ws_ref[0, frame]
        outside = (start == -1) if frame == 0 else (start == 0)
        halo = before_ref if frame == 0 else after_ref
        exists = (position > 0) if frame == 0 else (position < final)

        @pl.when(outside)
        def _():
            key_ref[frame_tok:] = halo[:, :HEAD_DIM]
            value_ref[frame_tok:, :HEAD_DIM] = halo[:, HEAD_DIM:]

        @pl.when(jnp.logical_not(outside))
        def _():
            other = pl.ds((1 - frame) * frame_tok, frame_tok)
            key_ref[frame_tok:] = qkv_ref[other, k_cols]
            value_ref[frame_tok:, :HEAD_DIM] = qkv_ref[other, v_cols]

        both = jnp.logical_or(jnp.logical_not(outside), exists)
        pl.when(both)(functools.partial(run, frame, 2 * frame_tok))
        pl.when(jnp.logical_not(both))(functools.partial(run, frame, frame_tok))


def attend(window_start, qkv, before, after, final):
    tok = qkv.shape[0]
    return pl.pallas_call(
        functools.partial(attend_kernel, final),
        in_specs=[SMEM, VMEM, VMEM, VMEM],
        out_specs=VMEM,
        out_shape=jax.ShapeDtypeStruct((tok, HEAD_DIM), qkv.dtype),
        scratch_shapes=[
            pltpu.VMEM((tok, HEAD_DIM), jnp.bfloat16),
            pltpu.VMEM((tok, 2 * HEAD_DIM), jnp.bfloat16),
        ],
        compiler_params=pltpu.CompilerParams(vmem_limit_bytes=BIG),
    )(window_start, qkv, before, after)


def finish_kernel(final, step_ref, att_ref, state_ref, fresh_ref, mod_ref, velocity_ref, passed_ref):
    heads, tok, _ = att_ref.shape
    position = lax.axis_index("section")
    step = step_ref[0]
    squares = jnp.zeros((tok, HEAD_DIM), jnp.float32)
    for head in range(heads):
        a = att_ref[head].astype(jnp.float32)
        squares += a * a
    mean = jnp.sum(squares, axis=-1, keepdims=True) / (heads * HEAD_DIM)
    scale = jnp.sqrt(mean + 1e-06)
    inverse = jnp.broadcast_to(1.0 / scale, (tok, HEAD_DIM))
    now = jnp.full((1, HEAD_DIM), step, jnp.int32)
    delta = level((now - 1).astype(jnp.float32)) - level(now.astype(jnp.float32))
    delta = jnp.broadcast_to(delta, (tok, HEAD_DIM))
    chosen = lax.broadcasted_iota(jnp.int32, (NSTEPS, HEAD_DIM), 0) == step
    for head in range(heads):
        cols = slice(head * HEAD_DIM, (head + 1) * HEAD_DIM)
        gain = jnp.sum(jnp.where(chosen, mod_ref[:, cols], 0.0), axis=0, keepdims=True)
        moving = att_ref[head].astype(jnp.float32) * inverse * gain
        velocity_ref[:, cols] = moving.astype(jnp.bfloat16)
        updated = state_ref[:, cols].astype(jnp.float32) + delta * moving
        passed_ref[:, cols] = updated.astype(jnp.bfloat16)

    @pl.when(position == final)
    def _():
        passed_ref[...] = fresh_ref[...]


def finish(timestep, attended, state, fresh, modulation, final):
    return pl.pallas_call(
        functools.partial(finish_kernel, final),
        in_specs=[SMEM, VMEM, VMEM, VMEM, VMEM],
        out_specs=[VMEM, VMEM],
        out_shape=[jax.ShapeDtypeStruct(state.shape, state.dtype)] * 2,
        compiler_params=pltpu.CompilerParams(vmem_limit_bytes=BIG),
    )(timestep, attended, state, fresh, modulation)


def per_device(queries, keys, values, queue_state, fresh_state, timestep, window_start, modulation):
    tok_dev, feat = queries.shape
    sections = lax.axis_size("section")
    frame_tok = tok_dev * lax.axis_size("seq") // FRAMES
    packed = pack(queries, keys, values)
    qkv = lax.all_to_all(packed, "seq", split_axis=0, concat_axis=0, tiled=True)
    qkv = qkv.reshape(FRAMES * frame_tok, 3 * HEAD_DIM)
    up = [(i, i + 1) for i in range(sections - 1)]
    down = [(j, i) for i, j in up]
    before = lax.ppermute(qkv[frame_tok:, HEAD_DIM:], "section", up)
    after = lax.ppermute(qkv[:frame_tok, HEAD_DIM:], "section", down)
    attended = attend(window_start, qkv, before, after, sections - 1)
    attended = attended.reshape(feat // HEAD_DIM, tok_dev, HEAD_DIM)
    attended = lax.all_to_all(attended, "seq", split_axis=0, concat_axis=0, tiled=True)
    velocity, passed = finish(timestep, attended, queue_state, fresh_state, modulation, sections - 1)
    ring = [(i, (i + 1) % sections) for i in range(sections)]
    return velocity, lax.ppermute(passed, "section", ring)


def solution(mesh):
    return jax.shard_map(
        per_device,
        mesh=mesh,
        in_specs=(
            P(("section", "seq"), None),
            P(("section", "seq"), None),
            P(("section", "seq"), None),
            P(("section", "seq"), None),
            P("seq", None),
            P("section"),
            P("section", None),
            P(),
        ),
        out_specs=(P(("section", "seq"), None), P(("section", "seq"), None)),
        check_vma=False,
    )
```

time: 198 us -> 176 us (0.89)
  blocking collectives: 0 us -> 95.6 us
  waiting for transfers between devices: 130 us -> 50.4 us
  starting transfers between devices: 38.9 us -> 13.9 us
  Pallas kernels: 0 us -> 13.1 us
  matrix products: 10.7 us -> 0 us
  local copies, waits for them, and re-layouts: 7.65 us -> 0.88 us
  other arithmetic: 6.44 us -> 0 us
  between operations: 3.67 us -> 1.35 us
    all_to_all x0 -> x1, blocking collectives: none -> 95.6 us  [per_device(): qkv = lax.all_to_all(packed, 'seq', split_axis=0, concat_axis=0, tiled=True)]
    all_to_all x4 -> x1, waiting for transfers between devices: 120 us -> 33 us  [per_device(): lax.all_to_all(attended, 'seq', split_axis=0, concat_axis=0, tiled=True)]
    all_to_all x4 -> x1, starting transfers between devices: 29.4 us -> 4.2 us  [per_device(): lax.all_to_all(attended, 'seq', split_axis=0, concat_axis=0, tiled=True)]
    pallas_call x0 -> x3, Pallas kernels: none -> 13.1 us  [the longest x1 8.08 us: attend(): pl.pallas_call(functools.partial(attend_kernel, final), in_specs=[SMEM, V...]
    dot_general x8 -> x0, matrix products: 10.7 us -> none  [the longest x4 5.94 us: attend(): jnp.einsum('qhd,khd->hqk', query_block, key_window, preferred_element_typ...]
    ppermute x3, waiting for transfers between devices: 10.7 us -> 17.4 us  [the longest x1 10.7 us: per_device(): return (velocity, lax.ppermute(passed, 'section', ring))]
    all_to_all x3 -> x0, local copies, waits for them, and re-layouts: 3.85 us -> none  [the longest x1 1.98 us: per_device(): lax.all_to_all(values, 'seq', split_axis=1, concat_axis=0, tiled=True)]
    reduce_sum x3 -> x0, other arithmetic: 2.26 us -> none  [the longest x2 2.05 us: attend(): total = jnp.sum(expo, axis=-1)]
  transfers between devices with their start and end apart: 7 -> 4, of which waited for: 5 -> 4; matrix products, arithmetic and copies ran while one was open for 3% -> 0% of each run, Pallas kernels for 0% -> 0%
where the time goes in v1:
time: 176 us; the launch traced here: 175 us
  blocking collectives  95.6 us (54%)
  waiting for transfers between devices  50.4 us (29%)
  starting transfers between devices  13.9 us (8%)
  Pallas kernels  13.1 us (7%)
    all_to_all x1, blocking collectives, per_device(): qkv = lax.all_to_all(packed, 'seq', split_axis=0, concat_axis=0, tiled=True)  95.6 us
    all_to_all x1, waiting for transfers between devices, per_device(): lax.all_to_all(attended, 'seq', split_axis=0, concat_axis=0, tiled=True)  33 us
    ppermute x1, waiting for transfers between devices, per_device(): return (velocity, lax.ppermute(passed, 'section', ring))  10.7 us
    pallas_call x1, Pallas kernels, attend(): pl.pallas_call(functools.partial(attend_kernel, final), in_specs=[SMEM, V...  8.08 us
    ppermute x1, starting transfers between devices, per_device(): after = lax.ppermute(qkv[:frame_tok, HEAD_DIM:], 'section', down)  5.88 us
    ppermute x1, waiting for transfers between devices, per_device(): before = lax.ppermute(qkv[frame_tok:, HEAD_DIM:], 'section', up)  4.75 us
    all_to_all x1, starting transfers between devices, per_device(): lax.all_to_all(attended, 'seq', split_axis=0, concat_axis=0, tiled=True)  4.2 us
    pallas_call x1, Pallas kernels, pack(): pl.pallas_call(pack_kernel, grid=(heads // group,), in_specs=[block] * 3,...  3.76 us
  transfers between devices with their start and end apart: 4, of which 4 were waited for; matrix products, arithmetic and copies ran while one was open for 0% of the time, Pallas kernels for 0%

profile of v1, /device:TPU:34, one launch (start us, length us, event | category | flops | bytes accessed | tf_op | source)
XLA Modules:
  0.0 175.1 jit_solution(11073394689586755874)
XLA Ops:
  0.6 3.8 %shard_map.95 = bf16[32,64,384]{2,1,0:T(8,128)(2,1)} custom-call(bf16[64,4096]{1,0:T(8,128)(2,1)} %q_ref.1, bf16[64,4096]{1,0:T(8,128)(2,1)} %k_ref.1, bf16[64,4096]{1,0:T(8,128)(2,1)} %v_ref.1), custom_call_target="tpu_custom_call" | custom-call | tf_op jit(solution)/shard_map/pallas_call | solution.py:36
  4.4 95.6 %all_to_all.10 = bf16[32,64,384]{2,1,0:T(8,128)(2,1)S(1)} all-to-all(bf16[32,64,384]{2,1,0:T(8,128)(2,1)} %shard_map.95), channel_id=1, replica_groups=mesh['section'=16,'seq'=32] {'seq'}, dimensions={0} | all-to-all | bytes 3145728 | tf_op jit(solution)/shard_map/all_to_all | solution.py:147
  99.9 0.0 copy-start.3
  99.9 0.1 fusion
  100.0 1.9 %collective-permute-start = (bf16[1024,256]{1,0:T(8,128)(2,1)S(1)}, bf16[1024,256]{1,0:T(8,128)(2,1)S(1)}, u32[]{:S(2)}, u32[]{:S(2)}) collective-permute-start(bf16[1024,256]{1,0:T(8,128)(2,1)S(1)} %get-tuple-element.7), channel_id=1, source_target_pairs={{0,32},{32,64},{64,96},{96,128},{128,160},{160,192},{192,224},{224... | collective-permute-start | bytes 1572872 | tf_op jit(solution)/shard_map/ppermute | solution.py:151
  101.9 0.0 copy-start
  102.0 0.0 copy-start.1
  102.0 0.0 copy-start.2
  102.0 5.9 %collective-permute-start.1 = (bf16[1024,256]{1,0:T(8,128)(2,1)S(1)}, bf16[1024,256]{1,0:T(8,128)(2,1)S(1)}, u32[]{:S(2)}, u32[]{:S(2)}) collective-permute-start(bf16[1024,256]{1,0:T(8,128)(2,1)S(1)} %get-tuple-element.6), channel_id=1, source_target_pairs={{32,0},{64,32},{96,64},{128,96},{160,128},{192,160},{224,192},{256... | collective-permute-start | bytes 1572872 | tf_op jit(solution)/shard_map/ppermute | solution.py:152
  107.9 4.8 %collective-permute-done.before_ref = bf16[1024,256]{1,0:T(8,128)(2,1)S(1)} collective-permute-done((bf16[1024,256]{1,0:T(8,128)(2,1)S(1)}, bf16[1024,256]{1,0:T(8,128)(2,1)S(1)}, u32[]{:S(2)}, u32[]{:S(2)}) %collective-permute-start) | collective-permute-done | bytes 524320 | tf_op jit(solution)/shard_map/ppermute | solution.py:151
  112.6 1.9 %collective-permute-done.1.after_ref = bf16[1024,256]{1,0:T(8,128)(2,1)S(1)} collective-permute-done((bf16[1024,256]{1,0:T(8,128)(2,1)S(1)}, bf16[1024,256]{1,0:T(8,128)(2,1)S(1)}, u32[]{:S(2)}, u32[]{:S(2)}) %collective-permute-start.1) | collective-permute-done | bytes 524320 | tf_op jit(solution)/shard_map/ppermute | solution.py:152
  114.6 0.0 copy-done.3
  114.6 8.1 %shard_map.96 = bf16[2048,128]{1,0:T(8,128)(2,1)} custom-call(s32[1,2]{1,0:T(1,128)S(1)} %copy-done.3, bf16[2048,384]{1,0:T(8,128)(2,1)S(1)} %bitcast.3, bf16[1024,256]{1,0:T(8,128)(2,1)S(1)} %collective-permute-done.before_ref, bf16[1024,256]{1,0:T(8,128)(2,1)S(1)} %collective-permute-done.1.after_ref), custom_call_target="tpu_custom_call" | custom-call | tf_op jit(solution)/shard_map/pallas_call | solution.py:91
  122.6 4.2 %all-to-all-start.1 = ((bf16[32,64,128]{2,1,0:T(8,128)(2,1)}), bf16[32,64,128]{2,1,0:T(8,128)(2,1)S(1)}, u32[]{:S(2)}, u32[]{:S(2)}) async-start(bf16[32,64,128]{2,1,0:T(8,128)(2,1)} %bitcast.1), calls=%async_computation.1 | async-start | bytes 1048576 | tf_op jit(solution)/shard_map/all_to_all | solution.py:155
  127.5 33.0 %all-to-all-done.1.att_ref = bf16[32,64,128]{2,1,0:T(8,128)(2,1)S(1)} async-done(((bf16[32,64,128]{2,1,0:T(8,128)(2,1)}), bf16[32,64,128]{2,1,0:T(8,128)(2,1)S(1)}, u32[]{:S(2)}, u32[]{:S(2)}) %all-to-all-start.1) | async-done | bytes 524320 | tf_op jit(solution)/shard_map/all_to_all | solution.py:155
  160.5 0.0 copy-done
  160.5 0.0 copy-done.1
  160.5 0.0 copy-done.2
  160.5 1.2 shard_map.97
  161.7 1.9 %collective-permute-start.2 = (bf16[64,4096]{1,0:T(8,128)(2,1)S(1)}, bf16[64,4096]{1,0:T(8,128)(2,1)S(1)}, u32[]{:S(2)}, u32[]{:S(2)}) collective-permute-start(bf16[64,4096]{1,0:T(8,128)(2,1)S(1)} %get-tuple-element.5), channel_id=1, source_target_pairs={{0,32},{32,64},{64,96},{96,128},{128,160},{160,192},{192,224},{224... | collective-permute-start | bytes 1572872 | tf_op jit(solution)/shard_map/ppermute | solution.py:158
  163.7 10.7 %collective-permute-done.2 = bf16[64,4096]{1,0:T(8,128)(2,1)S(1)} collective-permute-done((bf16[64,4096]{1,0:T(8,128)(2,1)S(1)}, bf16[64,4096]{1,0:T(8,128)(2,1)S(1)}, u32[]{:S(2)}, u32[]{:S(2)}) %collective-permute-start.2) | collective-permute-done | bytes 524320 | tf_op jit(solution)/shard_map/ppermute | solution.py:158
  174.3 0.8 copy.12
Async XLA Ops:
  99.9 14.6 %copy-start.3 = (s32[1,2]{1,0:T(1,128)S(1)}, s32[1,2]{1,0:T(1,128)}, u32[]{:S(2)}) copy-start(s32[1,2]{1,0:T(1,128)} %ws_ref.1) | copy-start | bytes 28
  100.0 12.6 %collective-permute-start = (bf16[1024,256]{1,0:T(8,128)(2,1)S(1)}, bf16[1024,256]{1,0:T(8,128)(2,1)S(1)}, u32[]{:S(2)}, u32[]{:S(2)}) collective-permute-start(bf16[1024,256]{1,0:T(8,128)(2,1)S(1)} %get-tuple-element.7), channel_id=1, source_target_pairs={{0,32},{32,64},{64,96},{96,128},{128,160},{160,192},{192,224},{224... | collective-permute-start | bytes 1572872 | tf_op jit(solution)/shard_map/ppermute | solution.py:151
  101.9 58.5 %copy-start = (bf16[64,4096]{1,0:T(8,128)(2,1)S(1)}, bf16[64,4096]{1,0:T(8,128)(2,1)}, u32[]{:S(2)}) copy-start(bf16[64,4096]{1,0:T(8,128)(2,1)} %state_ref.1) | copy-start | bytes 1572868
  102.0 58.5 %copy-start.1 = (bf16[64,4096]{1,0:T(8,128)(2,1)S(1)}, bf16[64,4096]{1,0:T(8,128)(2,1)}, u32[]{:S(2)}) copy-start(bf16[64,4096]{1,0:T(8,128)(2,1)} %fresh_ref.1) | copy-start | bytes 1572868
  102.0 58.5 %copy-start.2 = (f32[16,4096]{1,0:T(8,128)S(1)}, f32[16,4096]{1,0:T(8,128)}, u32[]{:S(2)}) copy-start(f32[16,4096]{1,0:T(8,128)} %mod_ref.1) | copy-start | bytes 786436
  102.0 12.6 %collective-permute-start.1 = (bf16[1024,256]{1,0:T(8,128)(2,1)S(1)}, bf16[1024,256]{1,0:T(8,128)(2,1)S(1)}, u32[]{:S(2)}, u32[]{:S(2)}) collective-permute-start(bf16[1024,256]{1,0:T(8,128)(2,1)S(1)} %get-tuple-element.6), channel_id=1, source_target_pairs={{32,0},{64,32},{96,64},{128,96},{160,128},{192,160},{224,192},{256... | collective-permute-start | bytes 1572872 | tf_op jit(solution)/shard_map/ppermute | solution.py:152
  122.6 37.9 %all-to-all-start.1 = ((bf16[32,64,128]{2,1,0:T(8,128)(2,1)}), bf16[32,64,128]{2,1,0:T(8,128)(2,1)S(1)}, u32[]{:S(2)}, u32[]{:S(2)}) async-start(bf16[32,64,128]{2,1,0:T(8,128)(2,1)} %bitcast.1), calls=%async_computation.1 | async-start | bytes 1048576 | tf_op jit(solution)/shard_map/all_to_all | solution.py:155
  161.7 12.6 %collective-permute-start.2 = (bf16[64,4096]{1,0:T(8,128)(2,1)S(1)}, bf16[64,4096]{1,0:T(8,128)(2,1)S(1)}, u32[]{:S(2)}, u32[]{:S(2)}) collective-permute-start(bf16[64,4096]{1,0:T(8,128)(2,1)S(1)} %get-tuple-element.5), channel_id=1, source_target_pairs={{0,32},{32,64},{64,96},{96,128},{128,160},{160,192},{192,224},{224... | collective-permute-start | bytes 1572872 | tf_op jit(solution)/shard_map/ppermute | solution.py:158

commit v2 on v1

v2 whole, which is shorter than its diff:
```python
import functools

import jax
import jax.numpy as jnp
from jax import lax
from jax.experimental import pallas as pl
from jax.experimental.pallas import tpu as pltpu
from jax.sharding import PartitionSpec as P

HEAD_DIM = 128
FRAMES = 2
NSTEPS = 16
SCALE = 1.4426950408889634 / HEAD_DIM**0.5
BLOCK = 256
VMEM = pl.BlockSpec(memory_space=pltpu.VMEM)
SMEM = pl.BlockSpec(memory_space=pltpu.SMEM)
LIMIT = 24 * 1024 * 1024


def level(step):
    share = step / NSTEPS
    return 5.0 * share / (1.0 + 4.0 * share)


def pack_kernel(q_ref, k_ref, v_ref, out_ref):
    for head in range(out_ref.shape[0]):
        cols = slice(head * HEAD_DIM, (head + 1) * HEAD_DIM)
        for part, ref in enumerate((q_ref, k_ref, v_ref)):
            out_ref[head, :, part * HEAD_DIM : (part + 1) * HEAD_DIM] = ref[:, cols]


def pack(queries, keys, values):
    tok, feat = queries.shape
    heads = feat // HEAD_DIM
    return pl.pallas_call(
        pack_kernel,
        in_specs=[VMEM] * 3,
        out_specs=VMEM,
        out_shape=jax.ShapeDtypeStruct((heads, tok, 3 * HEAD_DIM), queries.dtype),
        compiler_params=pltpu.CompilerParams(vmem_limit_bytes=LIMIT),
    )(queries, keys, values)


def scores_of(q, keys):
    return lax.dot_general(q, keys, (((1,), (1,)), ((), ())), preferred_element_type=jnp.float32)


def own_kernel(qkv_ref, sums_ref, peak_ref, value_ref):
    frame_tok = qkv_ref.shape[0] // FRAMES
    value_ref[:, :HEAD_DIM] = qkv_ref[:, 2 * HEAD_DIM :]
    value_ref[:, HEAD_DIM:] = jnp.ones((FRAMES * frame_tok, HEAD_DIM), jnp.bfloat16)
    for frame in range(FRAMES):
        own = pl.ds(frame * frame_tok, frame_tok)
        for index in range(frame_tok // BLOCK):
            rows = pl.ds(frame * frame_tok + index * BLOCK, BLOCK)
            scores = scores_of(qkv_ref[rows, :HEAD_DIM], qkv_ref[own, HEAD_DIM : 2 * HEAD_DIM])
            peak = jnp.max(scores, axis=-1, keepdims=True)
            weights = jnp.exp2((scores - peak) * SCALE).astype(jnp.bfloat16)
            sums_ref[rows, :] = jnp.dot(weights, value_ref[own, :], preferred_element_type=jnp.float32)
            peak_ref[rows, :] = jnp.broadcast_to(peak, (BLOCK, HEAD_DIM))


def own_part(qkv):
    tok = qkv.shape[0]
    return pl.pallas_call(
        own_kernel,
        in_specs=[VMEM],
        out_specs=[VMEM, VMEM],
        out_shape=[
            jax.ShapeDtypeStruct((tok, 2 * HEAD_DIM), jnp.float32),
            jax.ShapeDtypeStruct((tok, HEAD_DIM), jnp.float32),
        ],
        scratch_shapes=[pltpu.VMEM((tok, 2 * HEAD_DIM), jnp.bfloat16)],
        compiler_params=pltpu.CompilerParams(vmem_limit_bytes=LIMIT),
        cost_estimate=pl.CostEstimate(
            flops=6 * tok * tok // FRAMES * HEAD_DIM,
            bytes_accessed=10 * tok * HEAD_DIM,
            transcendentals=tok * tok // FRAMES,
        ),
    )(qkv)


def other_kernel(final, ws_ref, qkv_ref, near_ref, far_ref, sums_ref, peak_ref, out_ref, key_ref, value_ref):
    frame_tok = qkv_ref.shape[0] // FRAMES
    position = lax.axis_index("section")
    odd = lax.rem(position, 2) == 1
    k_cols, v_cols = slice(HEAD_DIM, 2 * HEAD_DIM), slice(2 * HEAD_DIM, 3 * HEAD_DIM)
    for frame in range(FRAMES):
        start = ws_ref[0, frame]
        outside = (start == -1) if frame == 0 else (start == 0)
        exists = (position > 0) if frame == 0 else (position < final)
        by_near = odd if frame == 0 else jnp.logical_not(odd)
        own = pl.ds(frame * frame_tok, frame_tok)
        other = pl.ds((1 - frame) * frame_tok, frame_tok)

        @pl.when(jnp.logical_not(outside))
        def _():
            key_ref[frame] = qkv_ref[other, k_cols]
            value_ref[frame, :, :HEAD_DIM] = qkv_ref[other, v_cols]

        for ref, chosen in ((near_ref, by_near), (far_ref, jnp.logical_not(by_near))):

            @pl.when(jnp.logical_and(outside, jnp.logical_and(exists, chosen)))
            def _():
                key_ref[frame] = ref[:, :HEAD_DIM]
                value_ref[frame, :, :HEAD_DIM] = ref[:, HEAD_DIM:]

        missing = jnp.logical_and(outside, jnp.logical_not(exists))

        @pl.when(jnp.logical_not(missing))
        def _():
            value_ref[frame, :, HEAD_DIM:] = jnp.ones((frame_tok, HEAD_DIM), jnp.bfloat16)

        @pl.when(missing)
        def _():
            key_ref[frame] = qkv_ref[own, k_cols]
            value_ref[frame] = jnp.zeros((frame_tok, 2 * HEAD_DIM), jnp.bfloat16)

    for frame in range(FRAMES):
        for index in range(frame_tok // BLOCK):
            rows = pl.ds(frame * frame_tok + index * BLOCK, BLOCK)
            scores = scores_of(qkv_ref[rows, :HEAD_DIM], key_ref[frame])
            before = peak_ref[rows, :]
            peak = jnp.maximum(jnp.max(scores, axis=-1, keepdims=True), before[:, :1])
            weights = jnp.exp2((scores - peak) * SCALE).astype(jnp.bfloat16)
            sums = jnp.dot(weights, value_ref[frame], preferred_element_type=jnp.float32)
            share = jnp.exp2((before - peak) * SCALE)
            mixed = sums[:, :HEAD_DIM] + sums_ref[rows, :HEAD_DIM] * share
            total = sums[:, HEAD_DIM:] + sums_ref[rows, HEAD_DIM:] * share
            out_ref[rows, :] = (mixed / total).astype(jnp.bfloat16)


def other_part(window_start, qkv, near, far, sums, peak, final):
    tok = qkv.shape[0]
    return pl.pallas_call(
        functools.partial(other_kernel, final),
        in_specs=[SMEM] + [VMEM] * 5,
        out_specs=VMEM,
        out_shape=jax.ShapeDtypeStruct((tok, HEAD_DIM), qkv.dtype),
        scratch_shapes=[
            pltpu.VMEM((FRAMES, tok // FRAMES, HEAD_DIM), jnp.bfloat16),
            pltpu.VMEM((FRAMES, tok // FRAMES, 2 * HEAD_DIM), jnp.bfloat16),
        ],
        compiler_params=pltpu.CompilerParams(vmem_limit_bytes=LIMIT),
    )(window_start, qkv, near, far, sums, peak)


def finish_kernel(final, step_ref, att_ref, state_ref, fresh_ref, mod_ref, velocity_ref, passed_ref):
    heads, tok, _ = att_ref.shape
    position = lax.axis_index("section")
    step = step_ref[0]
    squares = jnp.zeros((tok, HEAD_DIM), jnp.float32)
    for head in range(heads):
        a = att_ref[head].astype(jnp.float32)
        squares += a * a
    mean = jnp.sum(squares, axis=-1, keepdims=True) / (heads * HEAD_DIM)
    scale = jnp.sqrt(mean + 1e-06)
    inverse = jnp.broadcast_to(1.0 / scale, (tok, HEAD_DIM))
    now = jnp.full((1, HEAD_DIM), step, jnp.int32)
    delta = level((now - 1).astype(jnp.float32)) - level(now.astype(jnp.float32))
    delta = jnp.broadcast_to(delta, (tok, HEAD_DIM))
    chosen = lax.broadcasted_iota(jnp.int32, (NSTEPS, HEAD_DIM), 0) == step
    for head in range(heads):
        cols = slice(head * HEAD_DIM, (head + 1) * HEAD_DIM)
        gain = jnp.sum(jnp.where(chosen, mod_ref[:, cols], 0.0), axis=0, keepdims=True)
        moving = att_ref[head].astype(jnp.float32) * inverse * gain
        velocity_ref[:, cols] = moving.astype(jnp.bfloat16)
        updated = state_ref[:, cols].astype(jnp.float32) + delta * moving
        passed_ref[:, cols] = updated.astype(jnp.bfloat16)

    @pl.when(position == final)
    def _():
        passed_ref[...] = fresh_ref[...]


def finish(timestep, attended, state, fresh, modulation, final):
    return pl.pallas_call(
        functools.partial(finish_kernel, final),
        in_specs=[SMEM, VMEM, VMEM, VMEM, VMEM],
        out_specs=[VMEM, VMEM],
        out_shape=[jax.ShapeDtypeStruct(state.shape, state.dtype)] * 2,
        compiler_params=pltpu.CompilerParams(vmem_limit_bytes=LIMIT),
    )(timestep, attended, state, fresh, modulation)


def per_device(queries, keys, values, queue_state, fresh_state, timestep, window_start, modulation):
    tok_dev, feat = queries.shape
    sections = lax.axis_size("section")
    frame_tok = tok_dev * lax.axis_size("seq") // FRAMES
    packed = pack(queries, keys, values)
    qkv = lax.all_to_all(packed, "seq", split_axis=0, concat_axis=0, tiled=True)
    qkv = qkv.reshape(FRAMES * frame_tok, 3 * HEAD_DIM)
    odd = lax.rem(lax.axis_index("section"), 2)
    facing = [lax.dynamic_slice(qkv, (f * frame_tok, HEAD_DIM), (frame_tok, 2 * HEAD_DIM)) for f in (odd, 1 - odd)]
    pairs = [(i, i + 1) for i in range(1, sections - 1, 2)]
    far = lax.ppermute(facing[0], "section", pairs + [(j, i) for i, j in pairs])
    pairs = [(i, i + 1) for i in range(0, sections - 1, 2)]
    near = lax.ppermute(facing[1], "section", pairs + [(j, i) for i, j in pairs])
    sums, peak = own_part(qkv)
    attended = other_part(window_start, qkv, near, far, sums, peak, sections - 1)
    attended = attended.reshape(feat // HEAD_DIM, tok_dev, HEAD_DIM)
    attended = lax.all_to_all(attended, "seq", split_axis=0, concat_axis=0, tiled=True)
    velocity, passed = finish(timestep, attended, queue_state, fresh_state, modulation, sections - 1)
    ring = [(i, (i + 1) % sections) for i in range(sections)]
    return velocity, lax.ppermute(passed, "section", ring)


def solution(mesh):
    return jax.shard_map(
        per_device,
        mesh=mesh,
        in_specs=(
            P(("section", "seq"), None),
            P(("section", "seq"), None),
            P(("section", "seq"), None),
            P(("section", "seq"), None),
            P("seq", None),
            P("section"),
            P("section", None),
            P(),
        ),
        out_specs=(P(("section", "seq"), None), P(("section", "seq"), None)),
        check_vma=False,
    )
```

time: 176 us -> 172 us (0.977)
  blocking collectives: 95.6 us -> 0 us
  waiting for transfers between devices: 50.4 us -> 125 us
  starting transfers between devices: 13.9 us -> 30.9 us
  local copies, waits for them, and re-layouts: 0.88 us -> 4 us
  Pallas kernels: 13.1 us -> 10.5 us
    all_to_all x1 -> x0, blocking collectives: 95.6 us -> none  [per_device(): qkv = lax.all_to_all(packed, 'seq', split_axis=0, concat_axis=0, tiled=True)]
    all_to_all x0 -> x1, waiting for transfers between devices: none -> 78.6 us  [per_device(): qkv = lax.all_to_all(packed, 'seq', split_axis=0, concat_axis=0, tiled=True)]
    all_to_all x0 -> x1, starting transfers between devices: none -> 16.9 us  [per_device(): qkv = lax.all_to_all(packed, 'seq', split_axis=0, concat_axis=0, tiled=True)]
    unnamed x9 -> x15, local copies, waits for them, and re-layouts: 0.82 us -> 3.93 us
    ppermute x2, waiting for transfers between devices: 6.68 us -> 3.87 us  [the longest x1 3.86 us: per_device(): far = lax.ppermute(facing[0], 'section', pairs + [(j, i) for i, j in pairs])]
    pallas_call x2 -> x3, Pallas kernels: 11.8 us -> 9.25 us  [the longest x1 4.83 us: other_part(): pl.pallas_call(functools.partial(other_kernel, final), in_specs=[SMEM] +...]
  transfers between devices with their start and end apart: 4 -> 5, of which waited for: 4 -> 4; matrix products, arithmetic and copies ran while one was open for 0% -> 0% of each run, Pallas kernels for 0% -> 2%
where the time goes in v2:
time: 172 us
  waiting for transfers between devices  125 us (73%)
  starting transfers between devices  30.9 us (18%)
  Pallas kernels  10.5 us (6%)
  local copies, waits for them, and re-layouts  4 us (2%)
    all_to_all x1, waiting for transfers between devices, per_device(): qkv = lax.all_to_all(packed, 'seq', split_axis=0, concat_axis=0, tiled=True)  78.6 us
    all_to_all x1, waiting for transfers between devices, per_device(): lax.all_to_all(attended, 'seq', split_axis=0, concat_axis=0, tiled=True)  31.8 us
    all_to_all x1, starting transfers between devices, per_device(): qkv = lax.all_to_all(packed, 'seq', split_axis=0, concat_axis=0, tiled=True)  16.9 us
    ppermute x1, waiting for transfers between devices, per_device(): return (velocity, lax.ppermute(passed, 'section', ring))  10.7 us
    ppermute x1, starting transfers between devices, per_device(): far = lax.ppermute(facing[0], 'section', pairs + [(j, i) for i, j in pairs])  5.9 us
    pallas_call x1, Pallas kernels, other_part(): pl.pallas_call(functools.partial(other_kernel, final), in_specs=[SMEM] +...  4.83 us
    all_to_all x1, starting transfers between devices, per_device(): lax.all_to_all(attended, 'seq', split_axis=0, concat_axis=0, tiled=True)  4.26 us
    unnamed x15, local copies, waits for them, and re-layouts  3.93 us
  transfers between devices with their start and end apart: 5, of which 4 were waited for; matrix products, arithmetic and copies ran while one was open for 0% of the time, Pallas kernels for 2%

profile of v2, /device:TPU:34, one launch (start us, length us, event | category | flops | bytes accessed | tf_op | source)
XLA Modules:
  0.0 171.7 jit_solution(1792328121461344583)
XLA Ops:
  0.6 0.0 copy-start
  0.6 1.0 copy-done
  1.7 0.0 copy-start.1
  1.7 1.0 copy-done.1
  2.7 0.0 copy-start.2
  2.7 1.0 copy-done.2
  3.8 1.4 shard_map.95
  5.2 16.9 %all-to-all-start = ((bf16[32,64,384]{2,1,0:T(8,128)(2,1)}), bf16[32,64,384]{2,1,0:T(8,128)(2,1)S(1)}, u32[]{:S(2)}, u32[]{:S(2)}) async-start(bf16[32,64,384]{2,1,0:T(8,128)(2,1)} %shard_map.95), calls=%async_computation | async-start | bytes 3145728 | tf_op jit(solution)/shard_map/all_to_all | solution.py:191
  22.1 78.6 %all-to-all-done = bf16[32,64,384]{2,1,0:T(8,128)(2,1)S(1)} async-done(((bf16[32,64,384]{2,1,0:T(8,128)(2,1)}), bf16[32,64,384]{2,1,0:T(8,128)(2,1)S(1)}, u32[]{:S(2)}, u32[]{:S(2)}) %all-to-all-start) | async-done | bytes 1572896 | tf_op jit(solution)/shard_map/all_to_all | solution.py:191
  100.7 0.1 constant_dynamic-slice_fusion
  100.8 1.9 %collective-permute-start = (bf16[1024,256]{1,0:T(8,128)(2,1)S(1)}, bf16[1024,256]{1,0:T(8,128)(2,1)S(1)}, u32[]{:S(2)}, u32[]{:S(2)}) collective-permute-start(bf16[1024,256]{1,0:T(8,128)(2,1)S(1)} %get-tuple-element.11), channel_id=1, source_target_pairs={{0,32},{64,96},{128,160},{192,224},{256,288},{320,352},{384,416},{... | collective-permute-start | bytes 1572872 | tf_op jit(solution)/shard_map/ppermute | solution.py:198
  102.7 0.0 copy-start.6
  102.7 5.9 %collective-permute-start.1 = (bf16[1024,256]{1,0:T(8,128)(2,1)S(1)}, bf16[1024,256]{1,0:T(8,128)(2,1)S(1)}, u32[]{:S(2)}, u32[]{:S(2)}) collective-permute-start(bf16[1024,256]{1,0:T(8,128)(2,1)S(1)} %get-tuple-element.10), channel_id=1, source_target_pairs={{32,64},{96,128},{160,192},{224,256},{288,320},{352,384},{416,448}... | collective-permute-start | bytes 1572872 | tf_op jit(solution)/shard_map/ppermute | solution.py:196
  108.6 3.0 %shard_map.96 = (f32[2048,256]{1,0:T(8,128)S(1)}, f32[2048,128]{1,0:T(8,128)S(1)}) custom-call(bf16[2048,384]{1,0:T(8,128)(2,1)S(1)} %bitcast.3), custom_call_target="tpu_custom_call" | custom-call | flops 1610612736 | bytes 2621440 | tf_op jit(solution)/shard_map/pallas_call | solution.py:65
  111.6 0.0 collective-permute-done.near_ref
  111.6 3.9 %collective-permute-done.1.far_ref = bf16[1024,256]{1,0:T(8,128)(2,1)S(1)} collective-permute-done((bf16[1024,256]{1,0:T(8,128)(2,1)S(1)}, bf16[1024,256]{1,0:T(8,128)(2,1)S(1)}, u32[]{:S(2)}, u32[]{:S(2)}) %collective-permute-start.1) | collective-permute-done | bytes 524320 | tf_op jit(solution)/shard_map/ppermute | solution.py:196
  115.5 0.0 copy-done.6
  115.5 0.0 copy-start.3
  115.5 0.0 copy-start.4
  115.5 0.0 copy-start.5
  115.5 4.8 %shard_map.97 = bf16[2048,128]{1,0:T(8,128)(2,1)} custom-call(s32[1,2]{1,0:T(1,128)S(1)} %copy-done.6, bf16[2048,384]{1,0:T(8,128)(2,1)S(1)} %bitcast.4, bf16[1024,256]{1,0:T(8,128)(2,1)S(1)} %collective-permute-done.near_ref, bf16[1024,256]{1,0:T(8,128)(2,1)S(1)} %collective-permute-done.1.far_ref, f32[2048,256]{1,0:T(8,128)S(1)} %get-tuple-element.6.sums_ref, ...), custom_call_target="tpu_custom_call" | custom-call | tf_op jit(solution)/shard_map/pallas_call | solution.py:135
  120.3 4.3 %all-to-all-start.1 = ((bf16[32,64,128]{2,1,0:T(8,128)(2,1)}), bf16[32,64,128]{2,1,0:T(8,128)(2,1)S(1)}, u32[]{:S(2)}, u32[]{:S(2)}) async-start(bf16[32,64,128]{2,1,0:T(8,128)(2,1)} %bitcast.1), calls=%async_computation.1 | async-start | bytes 1048576 | tf_op jit(solution)/shard_map/all_to_all | solution.py:202
  125.2 31.8 %all-to-all-done.1.att_ref = bf16[32,64,128]{2,1,0:T(8,128)(2,1)S(1)} async-done(((bf16[32,64,128]{2,1,0:T(8,128)(2,1)}), bf16[32,64,128]{2,1,0:T(8,128)(2,1)S(1)}, u32[]{:S(2)}, u32[]{:S(2)}) %all-to-all-start.1) | async-done | bytes 524320 | tf_op jit(solution)/shard_map/all_to_all | solution.py:202
  157.1 0.0 copy-done.3
  157.1 0.0 copy-done.4
  157.1 0.0 copy-done.5
  157.1 1.2 shard_map.98
  158.3 1.9 %collective-permute-start.2 = (bf16[64,4096]{1,0:T(8,128)(2,1)S(1)}, bf16[64,4096]{1,0:T(8,128)(2,1)S(1)}, u32[]{:S(2)}, u32[]{:S(2)}) collective-permute-start(bf16[64,4096]{1,0:T(8,128)(2,1)S(1)} %get-tuple-element.9), channel_id=1, source_target_pairs={{0,32},{32,64},{64,96},{96,128},{128,160},{160,192},{192,224},{224... | collective-permute-start | bytes 1572872 | tf_op jit(solution)/shard_map/ppermute | solution.py:205
  160.2 10.7 %collective-permute-done.2 = bf16[64,4096]{1,0:T(8,128)(2,1)S(1)} collective-permute-done((bf16[64,4096]{1,0:T(8,128)(2,1)S(1)}, bf16[64,4096]{1,0:T(8,128)(2,1)S(1)}, u32[]{:S(2)}, u32[]{:S(2)}) %collective-permute-start.2) | collective-permute-done | bytes 524320 | tf_op jit(solution)/shard_map/ppermute | solution.py:205
  170.9 0.8 copy.12
Async XLA Ops:
  0.6 1.0 copy-start
  1.7 1.0 copy-start.1
  2.7 1.0 copy-start.2
  5.2 95.5 %all-to-all-start = ((bf16[32,64,384]{2,1,0:T(8,128)(2,1)}), bf16[32,64,384]{2,1,0:T(8,128)(2,1)S(1)}, u32[]{:S(2)}, u32[]{:S(2)}) async-start(bf16[32,64,384]{2,1,0:T(8,128)(2,1)} %shard_map.95), calls=%async_computation | async-start | bytes 3145728 | tf_op jit(solution)/shard_map/all_to_all | solution.py:191
  100.8 10.8 %collective-permute-start = (bf16[1024,256]{1,0:T(8,128)(2,1)S(1)}, bf16[1024,256]{1,0:T(8,128)(2,1)S(1)}, u32[]{:S(2)}, u32[]{:S(2)}) collective-permute-start(bf16[1024,256]{1,0:T(8,128)(2,1)S(1)} %get-tuple-element.11), channel_id=1, source_target_pairs={{0,32},{64,96},{128,160},{192,224},{256,288},{320,352},{384,416},{... | collective-permute-start | bytes 1572872 | tf_op jit(solution)/shard_map/ppermute | solution.py:198
  102.7 12.8 %copy-start.6 = (s32[1,2]{1,0:T(1,128)S(1)}, s32[1,2]{1,0:T(1,128)}, u32[]{:S(2)}) copy-start(s32[1,2]{1,0:T(1,128)} %ws_ref.1) | copy-start | bytes 28
  102.7 12.8 %collective-permute-start.1 = (bf16[1024,256]{1,0:T(8,128)(2,1)S(1)}, bf16[1024,256]{1,0:T(8,128)(2,1)S(1)}, u32[]{:S(2)}, u32[]{:S(2)}) collective-permute-start(bf16[1024,256]{1,0:T(8,128)(2,1)S(1)} %get-tuple-element.10), channel_id=1, source_target_pairs={{32,64},{96,128},{160,192},{224,256},{288,320},{352,384},{416,448}... | collective-permute-start | bytes 1572872 | tf_op jit(solution)/shard_map/ppermute | solution.py:196
  115.5 41.6 %copy-start.3 = (bf16[64,4096]{1,0:T(8,128)(2,1)S(1)}, bf16[64,4096]{1,0:T(8,128)(2,1)}, u32[]{:S(2)}) copy-start(bf16[64,4096]{1,0:T(8,128)(2,1)} %state_ref.1) | copy-start | bytes 1572868
  115.5 41.6 %copy-start.4 = (bf16[64,4096]{1,0:T(8,128)(2,1)S(1)}, bf16[64,4096]{1,0:T(8,128)(2,1)}, u32[]{:S(2)}) copy-start(bf16[64,4096]{1,0:T(8,128)(2,1)} %fresh_ref.1) | copy-start | bytes 1572868
  115.5 41.6 %copy-start.5 = (f32[16,4096]{1,0:T(8,128)S(1)}, f32[16,4096]{1,0:T(8,128)}, u32[]{:S(2)}) copy-start(f32[16,4096]{1,0:T(8,128)} %mod_ref.1) | copy-start | bytes 786436
  120.3 36.7 %all-to-all-start.1 = ((bf16[32,64,128]{2,1,0:T(8,128)(2,1)}), bf16[32,64,128]{2,1,0:T(8,128)(2,1)S(1)}, u32[]{:S(2)}, u32[]{:S(2)}) async-start(bf16[32,64,128]{2,1,0:T(8,128)(2,1)} %bitcast.1), calls=%async_computation.1 | async-start | bytes 1048576 | tf_op jit(solution)/shard_map/all_to_all | solution.py:202
  158.3 12.6 %collective-permute-start.2 = (bf16[64,4096]{1,0:T(8,128)(2,1)S(1)}, bf16[64,4096]{1,0:T(8,128)(2,1)S(1)}, u32[]{:S(2)}, u32[]{:S(2)}) collective-permute-start(bf16[64,4096]{1,0:T(8,128)(2,1)S(1)} %get-tuple-element.9), channel_id=1, source_target_pairs={{0,32},{32,64},{64,96},{96,128},{128,160},{160,192},{192,224},{224... | collective-permute-start | bytes 1572872 | tf_op jit(solution)/shard_map/ppermute | solution.py:205

commit v3 on v2

--- a/solution.py
+++ b/solution.py
@@ -12,9 +12,12 @@
 NSTEPS = 16
 SCALE = 1.4426950408889634 / HEAD_DIM**0.5
 BLOCK = 256
+CHUNKS = 4
 VMEM = pl.BlockSpec(memory_space=pltpu.VMEM)
+HBM = pl.BlockSpec(memory_space=pltpu.HBM)
 SMEM = pl.BlockSpec(memory_space=pltpu.SMEM)
 LIMIT = 24 * 1024 * 1024
+WHOLE = 63 * 1024 * 1024
 
 
 def level(step):
@@ -22,22 +25,46 @@
     return 5.0 * share / (1.0 + 4.0 * share)
 
 
-def pack_kernel(q_ref, k_ref, v_ref, out_ref):
-    for head in range(out_ref.shape[0]):
-        cols = slice(head * HEAD_DIM, (head + 1) * HEAD_DIM)
+def pack_kernel(q_ref, k_ref, v_ref, out_ref, held_ref, packed_ref, in_sem, out_sem):
+    heads = out_ref.shape[0]
+    group = heads // CHUNKS
+    copies = []
+    for chunk in range(CHUNKS):
+        cols = slice(chunk * group * HEAD_DIM, (chunk + 1) * group * HEAD_DIM)
         for part, ref in enumerate((q_ref, k_ref, v_ref)):
-            out_ref[head, :, part * HEAD_DIM : (part + 1) * HEAD_DIM] = ref[:, cols]
+            copy = pltpu.make_async_copy(ref.at[:, cols], held_ref.at[part, :, cols], in_sem.at[chunk, part])
+            copy.start()
+            copies.append(copy)
+    for chunk in range(CHUNKS):
+        mine = slice(chunk * group, (chunk + 1) * group)
+        for part in range(3):
+            copies[3 * chunk + part].wait()
+            for head in range(chunk * group, (chunk + 1) * group):
+                cols = slice(head * HEAD_DIM, (head + 1) * HEAD_DIM)
+                packed_ref[head, :, part * HEAD_DIM : (part + 1) * HEAD_DIM] = held_ref[part, :, cols]
+        copy = pltpu.make_async_copy(packed_ref.at[mine], out_ref.at[mine], out_sem.at[chunk])
+        copy.start()
+        copies.append(copy)
+    for copy in copies[3 * CHUNKS :]:
+        copy.wait()
 
 
 def pack(queries, keys, values):
     tok, feat = queries.shape
     heads = feat // HEAD_DIM
+    shape = (heads, tok, 3 * HEAD_DIM)
     return pl.pallas_call(
         pack_kernel,
-        in_specs=[VMEM] * 3,
-        out_specs=VMEM,
-        out_shape=jax.ShapeDtypeStruct((heads, tok, 3 * HEAD_DIM), queries.dtype),
-        compiler_params=pltpu.CompilerParams(vmem_limit_bytes=LIMIT),
+        in_specs=[HBM] * 3,
+        out_specs=HBM,
+        out_shape=jax.ShapeDtypeStruct(shape, queries.dtype),
+        scratch_shapes=[
+            pltpu.VMEM((3, tok, feat), queries.dtype),
+            pltpu.VMEM(shape, queries.dtype),
+            pltpu.SemaphoreType.DMA((CHUNKS, 3)),
+            pltpu.SemaphoreType.DMA((CHUNKS,)),
+        ],
+        compiler_params=pltpu.CompilerParams(vmem_limit_bytes=WHOLE),
     )(queries, keys, values)
 
 
@@ -80,7 +107,7 @@
     )(qkv)
 
 
-def other_kernel(final, ws_ref, qkv_ref, near_ref, far_ref, sums_ref, peak_ref, out_ref, key_ref, value_ref):
+def other_kernel(final, ws_ref, qkv_ref, far_ref, near_ref, sums_ref, peak_ref, out_ref, key_ref, value_ref):
     frame_tok = qkv_ref.shape[0] // FRAMES
     position = lax.axis_index("section")
     odd = lax.rem(position, 2) == 1
@@ -130,7 +157,7 @@
             out_ref[rows, :] = (mixed / total).astype(jnp.bfloat16)
 
 
-def other_part(window_start, qkv, near, far, sums, peak, final):
+def other_part(window_start, qkv, far, near, sums, peak, final):
     tok = qkv.shape[0]
     return pl.pallas_call(
         functools.partial(other_kernel, final),
@@ -142,45 +169,50 @@
             pltpu.VMEM((FRAMES, tok // FRAMES, 2 * HEAD_DIM), jnp.bfloat16),
         ],
         compiler_params=pltpu.CompilerParams(vmem_limit_bytes=LIMIT),
-    )(window_start, qkv, near, far, sums, peak)
-
-
-def finish_kernel(final, step_ref, att_ref, state_ref, fresh_ref, mod_ref, velocity_ref, passed_ref):
+    )(window_start, qkv, far, near, sums, peak)
+
+
+def velocity_of(step_ref, att_ref, mod_ref):
     heads, tok, _ = att_ref.shape
-    position = lax.axis_index("section")
-    step = step_ref[0]
     squares = jnp.zeros((tok, HEAD_DIM), jnp.float32)
     for head in range(heads):
         a = att_ref[head].astype(jnp.float32)
         squares += a * a
     mean = jnp.sum(squares, axis=-1, keepdims=True) / (heads * HEAD_DIM)
-    scale = jnp.sqrt(mean + 1e-06)
-    inverse = jnp.broadcast_to(1.0 / scale, (tok, HEAD_DIM))
-    now = jnp.full((1, HEAD_DIM), step, jnp.int32)
-    delta = level((now - 1).astype(jnp.float32)) - level(now.astype(jnp.float32))
-    delta = jnp.broadcast_to(delta, (tok, HEAD_DIM))
-    chosen = lax.broadcasted_iota(jnp.int32, (NSTEPS, HEAD_DIM), 0) == step
+    inverse = jnp.broadcast_to(1.0 / jnp.sqrt(mean + 1e-06), (tok, HEAD_DIM))
+    chosen = lax.broadcasted_iota(jnp.int32, (NSTEPS, HEAD_DIM), 0) == step_ref[0]
     for head in range(heads):
         cols = slice(head * HEAD_DIM, (head + 1) * HEAD_DIM)
         gain = jnp.sum(jnp.where(chosen, mod_ref[:, cols], 0.0), axis=0, keepdims=True)
-        moving = att_ref[head].astype(jnp.float32) * inverse * gain
-        velocity_ref[:, cols] = moving.astype(jnp.bfloat16)
-        updated = state_ref[:, cols].astype(jnp.float32) + delta * moving
-        passed_ref[:, cols] = updated.astype(jnp.bfloat16)
-
-    @pl.when(position == final)
+        yield cols, att_ref[head].astype(jnp.float32) * inverse * gain
+
+
+def update_kernel(final, step_ref, att_ref, mod_ref, state_ref, fresh_ref, passed_ref):
+    now = jnp.full((1, HEAD_DIM), step_ref[0], jnp.int32)
+    delta = level((now - 1).astype(jnp.float32)) - level(now.astype(jnp.float32))
+    for cols, moving in velocity_of(step_ref, att_ref, mod_ref):
+        passed_ref[:, cols] = (state_ref[:, cols].astype(jnp.float32) + delta * moving).astype(jnp.bfloat16)
+
+    @pl.when(lax.axis_index("section") == final)
     def _():
         passed_ref[...] = fresh_ref[...]
 
 
-def finish(timestep, attended, state, fresh, modulation, final):
-    return pl.pallas_call(
-        functools.partial(finish_kernel, final),
-        in_specs=[SMEM, VMEM, VMEM, VMEM, VMEM],
-        out_specs=[VMEM, VMEM],
-        out_shape=[jax.ShapeDtypeStruct(state.shape, state.dtype)] * 2,
+def velocity_kernel(step_ref, att_ref, mod_ref, velocity_ref):
+    for cols, moving in velocity_of(step_ref, att_ref, mod_ref):
+        velocity_ref[:, cols] = moving.astype(jnp.bfloat16)
+
+
+def finish(kernel, timestep, attended, modulation, *others):
+    heads, tok, _ = attended.shape
+    return pl.pallas_call(
+        kernel,
+        in_specs=[SMEM] + [VMEM] * (2 + len(others)),
+        out_specs=VMEM,
+        out_shape=jax.ShapeDtypeStruct((tok, heads * HEAD_DIM), attended.dtype),
         compiler_params=pltpu.CompilerParams(vmem_limit_bytes=LIMIT),
-    )(timestep, attended, state, fresh, modulation)
+        cost_estimate=pl.CostEstimate(flops=10 * tok * heads * HEAD_DIM, bytes_accessed=6 * tok * heads * HEAD_DIM, transcendentals=0),
+    )(timestep, attended, modulation, *others)
 
 
 def per_device(queries, keys, values, queue_state, fresh_state, timestep, window_start, modulation):
@@ -197,12 +229,14 @@
     pairs = [(i, i + 1) for i in range(0, sections - 1, 2)]
     near = lax.ppermute(facing[1], "section", pairs + [(j, i) for i, j in pairs])
     sums, peak = own_part(qkv)
-    attended = other_part(window_start, qkv, near, far, sums, peak, sections - 1)
+    attended = other_part(window_start, qkv, far, near, sums, peak, sections - 1)
     attended = attended.reshape(feat // HEAD_DIM, tok_dev, HEAD_DIM)
     attended = lax.all_to_all(attended, "seq", split_axis=0, concat_axis=0, tiled=True)
-    velocity, passed = finish(timestep, attended, queue_state, fresh_state, modulation, sections - 1)
-    ring = [(i, (i + 1) % sections) for i in range(sections)]
-    return velocity, lax.ppermute(passed, "section", ring)
+    update = functools.partial(update_kernel, sections - 1)
+    passed = finish(update, timestep, attended, modulation, queue_state, fresh_state)
+    advanced = lax.ppermute(passed, "section", [(i, (i + 1) % sections) for i in range(sections)])
+    velocity = finish(velocity_kernel, timestep, attended, modulation)
+    return velocity, advanced
 
 
 def solution(mesh):

time: 172 us -> 167 us (0.971)
  local copies, waits for them, and re-layouts: 4 us -> 0.88 us
  starting transfers between devices: 30.9 us -> 28.6 us
    unnamed x15 -> x9, local copies, waits for them, and re-layouts: 3.93 us -> 0.82 us
    ppermute x1, starting transfers between devices: 5.9 us -> 3.6 us  [per_device(): far = lax.ppermute(facing[0], 'section', pairs + [(j, i) for i, j in pairs])]
    pallas_call x2 -> x3, Pallas kernels: 2.69 us -> 3.88 us  [the longest x1 2.39 us: pack(): pl.pallas_call(pack_kernel, in_specs=[HBM] * 3, out_specs=HBM, out_shape=...]
where the time goes in v3:
time: 167 us; the launch traced here: 166 us
  waiting for transfers between devices  124 us (74%)
  starting transfers between devices  28.6 us (17%)
  Pallas kernels  11.7 us (7%)
    all_to_all x1, waiting for transfers between devices, per_device(): qkv = lax.all_to_all(packed, 'seq', split_axis=0, concat_axis=0, tiled=True)  78.6 us
    all_to_all x1, waiting for transfers between devices, per_device(): lax.all_to_all(attended, 'seq', split_axis=0, concat_axis=0, tiled=True)  31.4 us
    all_to_all x1, starting transfers between devices, per_device(): qkv = lax.all_to_all(packed, 'seq', split_axis=0, concat_axis=0, tiled=True)  16.9 us
    ppermute x1, waiting for transfers between devices, per_device(): lax.ppermute(passed, 'section', [(i, (i + 1) % sections) for i in range(s...  9.77 us
    pallas_call x1, Pallas kernels, other_part(): pl.pallas_call(functools.partial(other_kernel, final), in_specs=[SMEM] +...  4.83 us
    all_to_all x1, starting transfers between devices, per_device(): lax.all_to_all(attended, 'seq', split_axis=0, concat_axis=0, tiled=True)  4.26 us
    ppermute x1, waiting for transfers between devices, per_device(): far = lax.ppermute(facing[0], 'section', pairs + [(j, i) for i, j in pairs])  4.09 us
    ppermute x1, starting transfers between devices, per_device(): far = lax.ppermute(facing[0], 'section', pairs + [(j, i) for i, j in pairs])  3.6 us
  transfers between devices with their start and end apart: 5, of which 4 were waited for; matrix products, arithmetic and copies ran while one was open for 0% of the time, Pallas kernels for 2%

profile of v3, /device:TPU:34, one launch (start us, length us, event | category | flops | bytes accessed | tf_op | source)
XLA Modules:
  0.0 166.4 jit_solution(9892371286567658907)
XLA Ops:
  0.6 2.4 %shard_map.95 = bf16[32,64,384]{2,1,0:T(8,128)(2,1)} custom-call(bf16[64,4096]{1,0:T(8,128)(2,1)} %q_ref.1, bf16[64,4096]{1,0:T(8,128)(2,1)} %k_ref.1, bf16[64,4096]{1,0:T(8,128)(2,1)} %v_ref.1), custom_call_target="tpu_custom_call" | custom-call | tf_op jit(solution)/shard_map/pallas_call | solution.py:56
  3.0 16.9 %all-to-all-start = ((bf16[32,64,384]{2,1,0:T(8,128)(2,1)}), bf16[32,64,384]{2,1,0:T(8,128)(2,1)S(1)}, u32[]{:S(2)}, u32[]{:S(2)}) async-start(bf16[32,64,384]{2,1,0:T(8,128)(2,1)} %shard_map.95), calls=%async_computation | async-start | bytes 3145728 | tf_op jit(solution)/shard_map/all_to_all | solution.py:223
  20.0 78.6 %all-to-all-done = bf16[32,64,384]{2,1,0:T(8,128)(2,1)S(1)} async-done(((bf16[32,64,384]{2,1,0:T(8,128)(2,1)}), bf16[32,64,384]{2,1,0:T(8,128)(2,1)S(1)}, u32[]{:S(2)}, u32[]{:S(2)}) %all-to-all-start) | async-done | bytes 1572896 | tf_op jit(solution)/shard_map/all_to_all | solution.py:223
  98.5 0.1 constant_dynamic-slice_fusion
  98.6 3.6 %collective-permute-start = (bf16[1024,256]{1,0:T(8,128)(2,1)S(1)}, bf16[1024,256]{1,0:T(8,128)(2,1)S(1)}, u32[]{:S(2)}, u32[]{:S(2)}) collective-permute-start(bf16[1024,256]{1,0:T(8,128)(2,1)S(1)} %get-tuple-element.7), channel_id=1, source_target_pairs={{32,64},{96,128},{160,192},{224,256},{288,320},{352,384},{416,448}... | collective-permute-start | bytes 1572872 | tf_op jit(solution)/shard_map/ppermute | solution.py:228
  102.2 0.0 copy-start.3
  102.2 1.9 %collective-permute-start.1 = (bf16[1024,256]{1,0:T(8,128)(2,1)S(1)}, bf16[1024,256]{1,0:T(8,128)(2,1)S(1)}, u32[]{:S(2)}, u32[]{:S(2)}) collective-permute-start(bf16[1024,256]{1,0:T(8,128)(2,1)S(1)} %get-tuple-element.6), channel_id=1, source_target_pairs={{0,32},{64,96},{128,160},{192,224},{256,288},{320,352},{384,416},{... | collective-permute-start | bytes 1572872 | tf_op jit(solution)/shard_map/ppermute | solution.py:230
  104.2 3.0 %shard_map.96 = (f32[2048,256]{1,0:T(8,128)S(1)}, f32[2048,128]{1,0:T(8,128)S(1)}) custom-call(bf16[2048,384]{1,0:T(8,128)(2,1)S(1)} %bitcast.3), custom_call_target="tpu_custom_call" | custom-call | flops 1610612736 | bytes 2621440 | tf_op jit(solution)/shard_map/pallas_call | solution.py:92
  107.1 4.1 %collective-permute-done.far_ref = bf16[1024,256]{1,0:T(8,128)(2,1)S(1)} collective-permute-done((bf16[1024,256]{1,0:T(8,128)(2,1)S(1)}, bf16[1024,256]{1,0:T(8,128)(2,1)S(1)}, u32[]{:S(2)}, u32[]{:S(2)}) %collective-permute-start) | collective-permute-done | bytes 524320 | tf_op jit(solution)/shard_map/ppermute | solution.py:228
  111.2 0.0 collective-permute-done.1.near_ref
  111.2 0.0 copy-done.3
  111.2 0.0 copy-start
  111.2 0.0 copy-start.1
  111.3 0.0 copy-start.2
  111.3 4.8 %shard_map.97 = bf16[2048,128]{1,0:T(8,128)(2,1)} custom-call(s32[1,2]{1,0:T(1,128)S(1)} %copy-done.3, bf16[2048,384]{1,0:T(8,128)(2,1)S(1)} %bitcast.4, bf16[1024,256]{1,0:T(8,128)(2,1)S(1)} %collective-permute-done.far_ref, bf16[1024,256]{1,0:T(8,128)(2,1)S(1)} %collective-permute-done.1.near_ref, f32[2048,256]{1,0:T(8,128)S(1)} %get-tuple-element.4.sums_ref, ...), custom_call_target="tpu_custom_call" | custom-call | tf_op jit(solution)/shard_map/pallas_call | solution.py:162
  116.1 4.3 %all-to-all-start.1 = ((bf16[32,64,128]{2,1,0:T(8,128)(2,1)}), bf16[32,64,128]{2,1,0:T(8,128)(2,1)S(1)}, u32[]{:S(2)}, u32[]{:S(2)}) async-start(bf16[32,64,128]{2,1,0:T(8,128)(2,1)} %bitcast.1), calls=%async_computation.1 | async-start | bytes 1048576 | tf_op jit(solution)/shard_map/all_to_all | solution.py:234
  121.0 31.4 %all-to-all-done.1.att_ref = bf16[32,64,128]{2,1,0:T(8,128)(2,1)S(1)} async-done(((bf16[32,64,128]{2,1,0:T(8,128)(2,1)}), bf16[32,64,128]{2,1,0:T(8,128)(2,1)S(1)}, u32[]{:S(2)}, u32[]{:S(2)}) %all-to-all-start.1) | async-done | bytes 524320 | tf_op jit(solution)/shard_map/all_to_all | solution.py:234
  152.4 0.0 copy-done
  152.4 0.0 copy-done.1
  152.4 0.0 copy-done.2
  152.4 0.4 shard_map.99
  152.9 1.9 %collective-permute-start.2 = (bf16[64,4096]{1,0:T(8,128)(2,1)S(1)}, bf16[64,4096]{1,0:T(8,128)(2,1)S(1)}, u32[]{:S(2)}, u32[]{:S(2)}) collective-permute-start(bf16[64,4096]{1,0:T(8,128)(2,1)S(1)} %shard_map.99), channel_id=1, source_target_pairs={{0,32},{32,64},{64,96},{96,128},{128,160},{160,192},{192,224},{224... | collective-permute-start | bytes 1572872 | tf_op jit(solution)/shard_map/ppermute | solution.py:237
  154.8 1.1 shard_map.98
  155.9 9.8 %collective-permute-done.2 = bf16[64,4096]{1,0:T(8,128)(2,1)S(1)} collective-permute-done((bf16[64,4096]{1,0:T(8,128)(2,1)S(1)}, bf16[64,4096]{1,0:T(8,128)(2,1)S(1)}, u32[]{:S(2)}, u32[]{:S(2)}) %collective-permute-start.2) | collective-permute-done | bytes 524320 | tf_op jit(solution)/shard_map/ppermute | solution.py:237
  165.6 0.8 copy.12
Async XLA Ops:
  3.0 95.5 %all-to-all-start = ((bf16[32,64,384]{2,1,0:T(8,128)(2,1)}), bf16[32,64,384]{2,1,0:T(8,128)(2,1)S(1)}, u32[]{:S(2)}, u32[]{:S(2)}) async-start(bf16[32,64,384]{2,1,0:T(8,128)(2,1)} %shard_map.95), calls=%async_computation | async-start | bytes 3145728 | tf_op jit(solution)/shard_map/all_to_all | solution.py:223
  98.6 12.6 %collective-permute-start = (bf16[1024,256]{1,0:T(8,128)(2,1)S(1)}, bf16[1024,256]{1,0:T(8,128)(2,1)S(1)}, u32[]{:S(2)}, u32[]{:S(2)}) collective-permute-start(bf16[1024,256]{1,0:T(8,128)(2,1)S(1)} %get-tuple-element.7), channel_id=1, source_target_pairs={{32,64},{96,128},{160,192},{224,256},{288,320},{352,384},{416,448}... | collective-permute-start | bytes 1572872 | tf_op jit(solution)/shard_map/ppermute | solution.py:228
  102.2 9.0 %copy-start.3 = (s32[1,2]{1,0:T(1,128)S(1)}, s32[1,2]{1,0:T(1,128)}, u32[]{:S(2)}) copy-start(s32[1,2]{1,0:T(1,128)} %ws_ref.1) | copy-start | bytes 28
  102.2 9.0 %collective-permute-start.1 = (bf16[1024,256]{1,0:T(8,128)(2,1)S(1)}, bf16[1024,256]{1,0:T(8,128)(2,1)S(1)}, u32[]{:S(2)}, u32[]{:S(2)}) collective-permute-start(bf16[1024,256]{1,0:T(8,128)(2,1)S(1)} %get-tuple-element.6), channel_id=1, source_target_pairs={{0,32},{64,96},{128,160},{192,224},{256,288},{320,352},{384,416},{... | collective-permute-start | bytes 1572872 | tf_op jit(solution)/shard_map/ppermute | solution.py:230
  111.2 41.2 %copy-start = (f32[16,4096]{1,0:T(8,128)S(1)}, f32[16,4096]{1,0:T(8,128)}, u32[]{:S(2)}) copy-start(f32[16,4096]{1,0:T(8,128)} %mod_ref.3) | copy-start | bytes 786436
  111.2 41.2 %copy-start.1 = (bf16[64,4096]{1,0:T(8,128)(2,1)S(1)}, bf16[64,4096]{1,0:T(8,128)(2,1)}, u32[]{:S(2)}) copy-start(bf16[64,4096]{1,0:T(8,128)(2,1)} %state_ref.1) | copy-start | bytes 1572868
  111.3 41.2 %copy-start.2 = (bf16[64,4096]{1,0:T(8,128)(2,1)S(1)}, bf16[64,4096]{1,0:T(8,128)(2,1)}, u32[]{:S(2)}) copy-start(bf16[64,4096]{1,0:T(8,128)(2,1)} %fresh_ref.1) | copy-start | bytes 1572868
  116.1 36.3 %all-to-all-start.1 = ((bf16[32,64,128]{2,1,0:T(8,128)(2,1)}), bf16[32,64,128]{2,1,0:T(8,128)(2,1)S(1)}, u32[]{:S(2)}, u32[]{:S(2)}) async-start(bf16[32,64,128]{2,1,0:T(8,128)(2,1)} %bitcast.1), calls=%async_computation.1 | async-start | bytes 1048576 | tf_op jit(solution)/shard_map/all_to_all | solution.py:234
  152.9 12.8 %collective-permute-start.2 = (bf16[64,4096]{1,0:T(8,128)(2,1)S(1)}, bf16[64,4096]{1,0:T(8,128)(2,1)S(1)}, u32[]{:S(2)}, u32[]{:S(2)}) collective-permute-start(bf16[64,4096]{1,0:T(8,128)(2,1)S(1)} %shard_map.99), channel_id=1, source_target_pairs={{0,32},{32,64},{64,96},{96,128},{128,160},{160,192},{192,224},{224... | collective-permute-start | bytes 1572872 | tf_op jit(solution)/shard_map/ppermute | solution.py:237

commit v4 on v3

--- a/solution.py
+++ b/solution.py
@@ -12,7 +12,8 @@
 NSTEPS = 16
 SCALE = 1.4426950408889634 / HEAD_DIM**0.5
 BLOCK = 256
-CHUNKS = 4
+CHUNKS = 2
+MORE = 16
 VMEM = pl.BlockSpec(memory_space=pltpu.VMEM)
 HBM = pl.BlockSpec(memory_space=pltpu.HBM)
 SMEM = pl.BlockSpec(memory_space=pltpu.SMEM)
@@ -72,104 +73,134 @@
     return lax.dot_general(q, keys, (((1,), (1,)), ((), ())), preferred_element_type=jnp.float32)
 
 
-def own_kernel(qkv_ref, sums_ref, peak_ref, value_ref):
-    frame_tok = qkv_ref.shape[0] // FRAMES
-    value_ref[:, :HEAD_DIM] = qkv_ref[:, 2 * HEAD_DIM :]
-    value_ref[:, HEAD_DIM:] = jnp.ones((FRAMES * frame_tok, HEAD_DIM), jnp.bfloat16)
-    for frame in range(FRAMES):
-        own = pl.ds(frame * frame_tok, frame_tok)
-        for index in range(frame_tok // BLOCK):
-            rows = pl.ds(frame * frame_tok + index * BLOCK, BLOCK)
-            scores = scores_of(qkv_ref[rows, :HEAD_DIM], qkv_ref[own, HEAD_DIM : 2 * HEAD_DIM])
-            peak = jnp.max(scores, axis=-1, keepdims=True)
-            weights = jnp.exp2((scores - peak) * SCALE).astype(jnp.bfloat16)
-            sums_ref[rows, :] = jnp.dot(weights, value_ref[own, :], preferred_element_type=jnp.float32)
-            peak_ref[rows, :] = jnp.broadcast_to(peak, (BLOCK, HEAD_DIM))
-
-
-def own_part(qkv):
-    tok = qkv.shape[0]
-    return pl.pallas_call(
-        own_kernel,
+def frame_of(far):
+    odd = lax.rem(lax.axis_index("section"), 2)
+    return odd if far else 1 - odd
+
+
+def own_kernel(far, qkv_ref, sums_ref, peak_ref, *refs):
+    value_ref = refs[-1]
+    frame_tok = peak_ref.shape[0]
+    first = pl.multiple_of(frame_of(far) * frame_tok, frame_tok)
+    own = pl.ds(first, frame_tok)
+    if not far:
+        refs[0][...] = qkv_ref[own, HEAD_DIM:]
+    value_ref[:, :HEAD_DIM] = qkv_ref[own, 2 * HEAD_DIM :]
+    value_ref[:, HEAD_DIM:] = jnp.ones((frame_tok, HEAD_DIM), jnp.bfloat16)
+    for index in range(frame_tok // BLOCK):
+        rows = pl.ds(index * BLOCK, BLOCK)
+        q = qkv_ref[pl.ds(pl.multiple_of(first + index * BLOCK, BLOCK), BLOCK), :HEAD_DIM]
+        scores = scores_of(q, qkv_ref[own, HEAD_DIM : 2 * HEAD_DIM])
+        peak = jnp.max(scores, axis=-1, keepdims=True)
+        weights = jnp.exp2((scores - peak) * SCALE).astype(jnp.bfloat16)
+        sums_ref[rows, :] = jnp.dot(weights, value_ref[...], preferred_element_type=jnp.float32)
+        peak_ref[rows, :] = jnp.broadcast_to(peak, (BLOCK, HEAD_DIM))
+
+
+def part_cost(frame_tok):
+    return pl.CostEstimate(flops=frame_tok, bytes_accessed=frame_tok, transcendentals=0)
+
+
+def own_part(far, qkv):
+    frame_tok = qkv.shape[0] // FRAMES
+    shapes = [
+        jax.ShapeDtypeStruct((frame_tok, 2 * HEAD_DIM), jnp.float32),
+        jax.ShapeDtypeStruct((frame_tok, HEAD_DIM), jnp.float32),
+    ]
+    if not far:
+        shapes.append(jax.ShapeDtypeStruct((frame_tok, 2 * HEAD_DIM), qkv.dtype))
+    return pl.pallas_call(
+        functools.partial(own_kernel, far),
         in_specs=[VMEM],
-        out_specs=[VMEM, VMEM],
-        out_shape=[
-            jax.ShapeDtypeStruct((tok, 2 * HEAD_DIM), jnp.float32),
-            jax.ShapeDtypeStruct((tok, HEAD_DIM), jnp.float32),
-        ],
-        scratch_shapes=[pltpu.VMEM((tok, 2 * HEAD_DIM), jnp.bfloat16)],
+        out_specs=[VMEM] * len(shapes),
+        out_shape=shapes,
+        scratch_shapes=[pltpu.VMEM((frame_tok, 2 * HEAD_DIM), jnp.bfloat16)],
         compiler_params=pltpu.CompilerParams(vmem_limit_bytes=LIMIT),
-        cost_estimate=pl.CostEstimate(
-            flops=6 * tok * tok // FRAMES * HEAD_DIM,
-            bytes_accessed=10 * tok * HEAD_DIM,
-            transcendentals=tok * tok // FRAMES,
-        ),
+        cost_estimate=part_cost(frame_tok),
     )(qkv)
 
 
-def other_kernel(final, ws_ref, qkv_ref, far_ref, near_ref, sums_ref, peak_ref, out_ref, key_ref, value_ref):
+def other_frame(final, far, ws_ref, qkv_ref, halo_ref, sums_ref, peak_ref, key_ref, value_ref, store):
     frame_tok = qkv_ref.shape[0] // FRAMES
     position = lax.axis_index("section")
-    odd = lax.rem(position, 2) == 1
+    frame = frame_of(far)
+    outside = ws_ref[0, frame] == frame - 1
+    exists = jnp.where(frame == 0, position > 0, position < final)
+    own = pl.multiple_of(frame * frame_tok, frame_tok)
+    other = pl.ds(pl.multiple_of((1 - frame) * frame_tok, frame_tok), frame_tok)
     k_cols, v_cols = slice(HEAD_DIM, 2 * HEAD_DIM), slice(2 * HEAD_DIM, 3 * HEAD_DIM)
-    for frame in range(FRAMES):
-        start = ws_ref[0, frame]
-        outside = (start == -1) if frame == 0 else (start == 0)
-        exists = (position > 0) if frame == 0 else (position < final)
-        by_near = odd if frame == 0 else jnp.logical_not(odd)
-        own = pl.ds(frame * frame_tok, frame_tok)
-        other = pl.ds((1 - frame) * frame_tok, frame_tok)
-
-        @pl.when(jnp.logical_not(outside))
-        def _():
-            key_ref[frame] = qkv_ref[other, k_cols]
-            value_ref[frame, :, :HEAD_DIM] = qkv_ref[other, v_cols]
-
-        for ref, chosen in ((near_ref, by_near), (far_ref, jnp.logical_not(by_near))):
-
-            @pl.when(jnp.logical_and(outside, jnp.logical_and(exists, chosen)))
-            def _():
-                key_ref[frame] = ref[:, :HEAD_DIM]
-                value_ref[frame, :, :HEAD_DIM] = ref[:, HEAD_DIM:]
-
-        missing = jnp.logical_and(outside, jnp.logical_not(exists))
-
-        @pl.when(jnp.logical_not(missing))
-        def _():
-            value_ref[frame, :, HEAD_DIM:] = jnp.ones((frame_tok, HEAD_DIM), jnp.bfloat16)
-
-        @pl.when(missing)
-        def _():
-            key_ref[frame] = qkv_ref[own, k_cols]
-            value_ref[frame] = jnp.zeros((frame_tok, 2 * HEAD_DIM), jnp.bfloat16)
-
-    for frame in range(FRAMES):
-        for index in range(frame_tok // BLOCK):
-            rows = pl.ds(frame * frame_tok + index * BLOCK, BLOCK)
-            scores = scores_of(qkv_ref[rows, :HEAD_DIM], key_ref[frame])
-            before = peak_ref[rows, :]
-            peak = jnp.maximum(jnp.max(scores, axis=-1, keepdims=True), before[:, :1])
-            weights = jnp.exp2((scores - peak) * SCALE).astype(jnp.bfloat16)
-            sums = jnp.dot(weights, value_ref[frame], preferred_element_type=jnp.float32)
-            share = jnp.exp2((before - peak) * SCALE)
-            mixed = sums[:, :HEAD_DIM] + sums_ref[rows, :HEAD_DIM] * share
-            total = sums[:, HEAD_DIM:] + sums_ref[rows, HEAD_DIM:] * share
-            out_ref[rows, :] = (mixed / total).astype(jnp.bfloat16)
-
-
-def other_part(window_start, qkv, far, near, sums, peak, final):
-    tok = qkv.shape[0]
-    return pl.pallas_call(
-        functools.partial(other_kernel, final),
-        in_specs=[SMEM] + [VMEM] * 5,
+    value_ref[:, HEAD_DIM:] = jnp.ones((frame_tok, HEAD_DIM), jnp.bfloat16)
+
+    @pl.when(jnp.logical_not(outside))
+    def _():
+        key_ref[...] = qkv_ref[other, k_cols]
+        value_ref[:, :HEAD_DIM] = qkv_ref[other, v_cols]
+
+    @pl.when(jnp.logical_and(outside, exists))
+    def _():
+        rows = pl.ds(pl.multiple_of((1 - frame) * MORE, MORE), frame_tok) if far else slice(None)
+        key_ref[...] = halo_ref[rows, :HEAD_DIM]
+        value_ref[:, :HEAD_DIM] = halo_ref[rows, HEAD_DIM:]
+
+    @pl.when(jnp.logical_and(outside, jnp.logical_not(exists)))
+    def _():
+        key_ref[...] = qkv_ref[pl.ds(own, frame_tok), k_cols]
+        value_ref[...] = jnp.zeros((frame_tok, 2 * HEAD_DIM), jnp.bfloat16)
+
+    def scores(index):
+        rows = pl.ds(pl.multiple_of(own + index * BLOCK, BLOCK), BLOCK)
+        return scores_of(qkv_ref[rows, :HEAD_DIM], key_ref[...])
+
+    blocks = frame_tok // BLOCK
+    after = scores(0)
+    for index in range(blocks):
+        here = after
+        if index + 1 < blocks:
+            after = scores(index + 1)
+        rows = pl.ds(index * BLOCK, BLOCK)
+        before = peak_ref[rows, :]
+        peak = jnp.maximum(jnp.broadcast_to(jnp.max(here, axis=-1, keepdims=True), before.shape), before)
+        spread = jnp.concatenate([peak] * (frame_tok // HEAD_DIM), axis=1)
+        weights = jnp.exp2((here - spread) * SCALE).astype(jnp.bfloat16)
+        sums = jnp.dot(weights, value_ref[...], preferred_element_type=jnp.float32)
+        share = jnp.exp2((before - peak) * SCALE)
+        mixed = sums[:, :HEAD_DIM] + sums_ref[rows, :HEAD_DIM] * share
+        total = sums[:, HEAD_DIM:] + sums_ref[rows, HEAD_DIM:] * share
+        store(index * BLOCK, (mixed / total).astype(jnp.bfloat16))
+
+
+def near_kernel(final, ws_ref, qkv_ref, halo_ref, sums_ref, peak_ref, out_ref, key_ref, value_ref):
+    def store(begin, result):
+        out_ref[pl.ds(begin, BLOCK), :] = result
+
+    other_frame(final, False, ws_ref, qkv_ref, halo_ref, sums_ref, peak_ref, key_ref, value_ref, store)
+
+
+def far_kernel(final, ws_ref, qkv_ref, halo_ref, sums_ref, peak_ref, near_ref, out_ref, key_ref, value_ref):
+    frame_tok = near_ref.shape[0]
+    first = frame_of(True) * frame_tok
+
+    def store(begin, result):
+        out_ref[pl.ds(pl.multiple_of(first + begin, BLOCK), BLOCK), :] = result
+
+    out_ref[pl.ds(pl.multiple_of(frame_of(False) * frame_tok, frame_tok), frame_tok), :] = near_ref[...]
+    other_frame(final, True, ws_ref, qkv_ref, halo_ref, sums_ref, peak_ref, key_ref, value_ref, store)
+
+
+def other_part(kernel, rows, window_start, qkv, *others):
+    frame_tok = qkv.shape[0] // FRAMES
+    return pl.pallas_call(
+        kernel,
+        in_specs=[SMEM] + [VMEM] * (1 + len(others)),
         out_specs=VMEM,
-        out_shape=jax.ShapeDtypeStruct((tok, HEAD_DIM), qkv.dtype),
+        out_shape=jax.ShapeDtypeStruct((rows, HEAD_DIM), qkv.dtype),
         scratch_shapes=[
-            pltpu.VMEM((FRAMES, tok // FRAMES, HEAD_DIM), jnp.bfloat16),
-            pltpu.VMEM((FRAMES, tok // FRAMES, 2 * HEAD_DIM), jnp.bfloat16),
+            pltpu.VMEM((frame_tok, HEAD_DIM), jnp.bfloat16),
+            pltpu.VMEM((frame_tok, 2 * HEAD_DIM), jnp.bfloat16),
         ],
         compiler_params=pltpu.CompilerParams(vmem_limit_bytes=LIMIT),
-    )(window_start, qkv, far, near, sums, peak)
+        cost_estimate=part_cost(frame_tok),
+    )(window_start, qkv, *others)
 
 
 def velocity_of(step_ref, att_ref, mod_ref):
@@ -222,14 +253,17 @@
     packed = pack(queries, keys, values)
     qkv = lax.all_to_all(packed, "seq", split_axis=0, concat_axis=0, tiled=True)
     qkv = qkv.reshape(FRAMES * frame_tok, 3 * HEAD_DIM)
-    odd = lax.rem(lax.axis_index("section"), 2)
-    facing = [lax.dynamic_slice(qkv, (f * frame_tok, HEAD_DIM), (frame_tok, 2 * HEAD_DIM)) for f in (odd, 1 - odd)]
+    start = frame_of(True) * (frame_tok - MORE)
+    facing = lax.dynamic_slice(qkv, (start, HEAD_DIM), (frame_tok + MORE, 2 * HEAD_DIM))
     pairs = [(i, i + 1) for i in range(1, sections - 1, 2)]
-    far = lax.ppermute(facing[0], "section", pairs + [(j, i) for i, j in pairs])
+    far = lax.ppermute(facing, "section", pairs + [(j, i) for i, j in pairs])
+    near_sums, near_peak, facing = own_part(False, qkv)
     pairs = [(i, i + 1) for i in range(0, sections - 1, 2)]
-    near = lax.ppermute(facing[1], "section", pairs + [(j, i) for i, j in pairs])
-    sums, peak = own_part(qkv)
-    attended = other_part(window_start, qkv, far, near, sums, peak, sections - 1)
+    near = lax.ppermute(facing, "section", pairs + [(j, i) for i, j in pairs])
+    far_sums, far_peak = own_part(True, qkv)
+    kernels = [functools.partial(kernel, sections - 1) for kernel in (near_kernel, far_kernel)]
+    near_out = other_part(kernels[0], frame_tok, window_start, qkv, near, near_sums, near_peak)
+    attended = other_part(kernels[1], FRAMES * frame_tok, window_start, qkv, far, far_sums, far_peak, near_out)
     attended = attended.reshape(feat // HEAD_DIM, tok_dev, HEAD_DIM)
     attended = lax.all_to_all(attended, "seq", split_axis=0, concat_axis=0, tiled=True)
     update = functools.partial(update_kernel, sections - 1)

time: 167 us -> 167 us (level)
    ppermute x2, waiting for transfers between devices: 4.09 us -> 1.46 us  [the longest x1 1.35 us: per_device(): far = lax.ppermute(facing, 'section', pairs + [(j, i) for i, j in pairs])]
    all_to_all x1, waiting for transfers between devices: 31.4 us -> 33.7 us  [per_device(): lax.all_to_all(attended, 'seq', split_axis=0, concat_axis=0, tiled=True)]
    pallas_call x2 -> x4, Pallas kernels: 7.8 us -> 8.66 us  [the longest x2 5.13 us: other_part(): pl.pallas_call(kernel, in_specs=[SMEM] + [VMEM] * (1 + len(others)), out_...]
  transfers between devices with their start and end apart: 5 -> 5, of which waited for: 4 -> 5; matrix products, arithmetic and copies ran while one was open for 0% -> 0% of each run, Pallas kernels for 2% -> 4%
where the time goes in v4:
time: 167 us
  waiting for transfers between devices  123 us (74%)
  starting transfers between devices  28.6 us (17%)
  Pallas kernels  12.5 us (7%)
    all_to_all x1, waiting for transfers between devices, per_device(): qkv = lax.all_to_all(packed, 'seq', split_axis=0, concat_axis=0, tiled=True)  78.6 us
    all_to_all x1, waiting for transfers between devices, per_device(): lax.all_to_all(attended, 'seq', split_axis=0, concat_axis=0, tiled=True)  33.7 us
    all_to_all x1, starting transfers between devices, per_device(): qkv = lax.all_to_all(packed, 'seq', split_axis=0, concat_axis=0, tiled=True)  16.9 us
    ppermute x1, waiting for transfers between devices, per_device(): lax.ppermute(passed, 'section', [(i, (i + 1) % sections) for i in range(s...  9.62 us
    pallas_call x2, Pallas kernels, other_part(): pl.pallas_call(kernel, in_specs=[SMEM] + [VMEM] * (1 + len(others)), out_...  5.13 us
    all_to_all x1, starting transfers between devices, per_device(): lax.all_to_all(attended, 'seq', split_axis=0, concat_axis=0, tiled=True)  4.26 us
    ppermute x1, starting transfers between devices, per_device(): far = lax.ppermute(facing, 'section', pairs + [(j, i) for i, j in pairs])  3.6 us
    pallas_call x2, Pallas kernels, own_part(): pl.pallas_call(functools.partial(own_kernel, far), in_specs=[VMEM], out_s...  3.52 us
  transfers between devices with their start and end apart: 5, of which 5 were waited for; matrix products, arithmetic and copies ran while one was open for 0% of the time, Pallas kernels for 4%

profile of v4, /device:TPU:34, one launch (start us, length us, event | category | flops | bytes accessed | tf_op | source)
XLA Modules:
  0.0 166.7 jit_solution(12543317811745532360)
XLA Ops:
  0.6 2.4 %shard_map.95 = bf16[32,64,384]{2,1,0:T(8,128)(2,1)} custom-call(bf16[64,4096]{1,0:T(8,128)(2,1)} %q_ref.1, bf16[64,4096]{1,0:T(8,128)(2,1)} %k_ref.1, bf16[64,4096]{1,0:T(8,128)(2,1)} %v_ref.1), custom_call_target="tpu_custom_call" | custom-call | tf_op jit(solution)/shard_map/pallas_call | solution.py:57
  3.0 16.9 %all-to-all-start = ((bf16[32,64,384]{2,1,0:T(8,128)(2,1)}), bf16[32,64,384]{2,1,0:T(8,128)(2,1)S(1)}, u32[]{:S(2)}, u32[]{:S(2)}) async-start(bf16[32,64,384]{2,1,0:T(8,128)(2,1)} %shard_map.95), calls=%async_computation | async-start | bytes 3145728 | tf_op jit(solution)/shard_map/all_to_all | solution.py:254
  20.0 78.6 %all-to-all-done = bf16[32,64,384]{2,1,0:T(8,128)(2,1)S(1)} async-done(((bf16[32,64,384]{2,1,0:T(8,128)(2,1)}), bf16[32,64,384]{2,1,0:T(8,128)(2,1)S(1)}, u32[]{:S(2)}, u32[]{:S(2)}) %all-to-all-start) | async-done | bytes 1572896 | tf_op jit(solution)/shard_map/all_to_all | solution.py:254
  98.6 0.0 copy-start.3
  98.6 3.6 %collective-permute-start = (bf16[1040,256]{1,0:T(8,128)(2,1)S(1)}, bf16[1040,256]{1,0:T(8,128)(2,1)S(1)}, u32[]{:S(2)}, u32[]{:S(2)}) collective-permute-start(bf16[1040,256]{1,0:T(8,128)(2,1)S(1)} %constant_dynamic-slice_fusion), channel_id=1, source_target_pairs={{32,64},{96,128},{160,192},{224,256},{288,320},{352,384},{416,448}... | collective-permute-start | bytes 1597448 | tf_op jit(solution)/shard_map/ppermute | solution.py:259
  102.2 1.8 %shard_map.97 = (f32[1024,256]{1,0:T(8,128)S(1)}, f32[1024,128]{1,0:T(8,128)S(1)}, bf16[1024,256]{1,0:T(8,128)(2,1)S(1)}) custom-call(bf16[2048,384]{1,0:T(8,128)(2,1)S(1)} %bitcast.3), custom_call_target="tpu_custom_call" | custom-call | flops 1024 | bytes 1024 | tf_op jit(solution)/shard_map/pallas_call | solution.py:112
  104.0 1.9 %collective-permute-start.1 = (bf16[1024,256]{1,0:T(8,128)(2,1)S(1)}, bf16[1024,256]{1,0:T(8,128)(2,1)S(1)}, u32[]{:S(2)}, u32[]{:S(2)}) collective-permute-start(bf16[1024,256]{1,0:T(8,128)(2,1)S(1)} %get-tuple-element.9), channel_id=1, source_target_pairs={{0,32},{64,96},{128,160},{192,224},{256,288},{320,352},{384,416},{... | collective-permute-start | bytes 1572872 | tf_op jit(solution)/shard_map/ppermute | solution.py:262
  105.9 1.8 %shard_map.96 = (f32[1024,256]{1,0:T(8,128)S(1)}, f32[1024,128]{1,0:T(8,128)S(1)}) custom-call(bf16[2048,384]{1,0:T(8,128)(2,1)S(1)} %bitcast.4), custom_call_target="tpu_custom_call" | custom-call | flops 1024 | bytes 1024 | tf_op jit(solution)/shard_map/pallas_call | solution.py:112
  107.7 0.1 collective-permute-done.1.halo_ref
  107.8 0.0 copy-done.3
  107.8 2.2 %shard_map.98.near_ref = bf16[1024,128]{1,0:T(8,128)(2,1)S(1)} custom-call(s32[1,2]{1,0:T(1,128)S(1)} %copy-done.3, bf16[2048,384]{1,0:T(8,128)(2,1)S(1)} %bitcast.5, bf16[1024,256]{1,0:T(8,128)(2,1)S(1)} %collective-permute-done.1.halo_ref, f32[1024,256]{1,0:T(8,128)S(1)} %get-tuple-element.10.sums_ref, f32[1024,128]{1,0:T(8,128)S(1)} %get-tuple-element.11.peak_ref), custom_call_target="tpu_custom_call" | custom-call | flops 1024 | bytes 1024 | tf_op jit(solution)/shard_map/pallas_call | solution.py:192
  109.9 1.4 collective-permute-done.halo_ref
  111.3 0.0 copy-start
  111.3 0.0 copy-start.1
  111.3 0.0 copy-start.2
  111.3 3.0 %shard_map.99 = bf16[2048,128]{1,0:T(8,128)(2,1)} custom-call(s32[1,2]{1,0:T(1,128)S(1)} %copy-done.3, bf16[2048,384]{1,0:T(8,128)(2,1)S(1)} %bitcast.6, bf16[1040,256]{1,0:T(8,128)(2,1)S(1)} %collective-permute-done.halo_ref, f32[1024,256]{1,0:T(8,128)S(1)} %get-tuple-element.7.sums_ref, f32[1024,128]{1,0:T(8,128)S(1)} %get-tuple-element.8.peak_ref, ...), custom_call_target="tpu_custom_call" | custom-call | flops 1024 | bytes 1024 | tf_op jit(solution)/shard_map/pallas_call | solution.py:192
  114.3 4.3 %all-to-all-start.1 = ((bf16[32,64,128]{2,1,0:T(8,128)(2,1)}), bf16[32,64,128]{2,1,0:T(8,128)(2,1)S(1)}, u32[]{:S(2)}, u32[]{:S(2)}) async-start(bf16[32,64,128]{2,1,0:T(8,128)(2,1)} %bitcast.1), calls=%async_computation.1 | async-start | bytes 1048576 | tf_op jit(solution)/shard_map/all_to_all | solution.py:268
  119.2 33.7 %all-to-all-done.1.att_ref = bf16[32,64,128]{2,1,0:T(8,128)(2,1)S(1)} async-done(((bf16[32,64,128]{2,1,0:T(8,128)(2,1)}), bf16[32,64,128]{2,1,0:T(8,128)(2,1)S(1)}, u32[]{:S(2)}, u32[]{:S(2)}) %all-to-all-start.1) | async-done | bytes 524320 | tf_op jit(solution)/shard_map/all_to_all | solution.py:268
  152.9 0.0 copy-done
  152.9 0.0 copy-done.1
  152.9 0.0 copy-done.2
  152.9 0.4 shard_map.101
  153.3 1.9 %collective-permute-start.2 = (bf16[64,4096]{1,0:T(8,128)(2,1)S(1)}, bf16[64,4096]{1,0:T(8,128)(2,1)S(1)}, u32[]{:S(2)}, u32[]{:S(2)}) collective-permute-start(bf16[64,4096]{1,0:T(8,128)(2,1)S(1)} %shard_map.101), channel_id=1, source_target_pairs={{0,32},{32,64},{64,96},{96,128},{128,160},{160,192},{192,224},{224... | collective-permute-start | bytes 1572872 | tf_op jit(solution)/shard_map/ppermute | solution.py:271
  155.2 1.1 shard_map.100
  156.3 9.6 %collective-permute-done.2 = bf16[64,4096]{1,0:T(8,128)(2,1)S(1)} collective-permute-done((bf16[64,4096]{1,0:T(8,128)(2,1)S(1)}, bf16[64,4096]{1,0:T(8,128)(2,1)S(1)}, u32[]{:S(2)}, u32[]{:S(2)}) %collective-permute-start.2) | collective-permute-done | bytes 524320 | tf_op jit(solution)/shard_map/ppermute | solution.py:271
  165.9 0.8 copy.12
  (1 shorter events, 0.0 us)
Async XLA Ops:
  3.0 95.5 %all-to-all-start = ((bf16[32,64,384]{2,1,0:T(8,128)(2,1)}), bf16[32,64,384]{2,1,0:T(8,128)(2,1)S(1)}, u32[]{:S(2)}, u32[]{:S(2)}) async-start(bf16[32,64,384]{2,1,0:T(8,128)(2,1)} %shard_map.95), calls=%async_computation | async-start | bytes 3145728 | tf_op jit(solution)/shard_map/all_to_all | solution.py:254
  98.6 9.2 %copy-start.3 = (s32[1,2]{1,0:T(1,128)S(1)}, s32[1,2]{1,0:T(1,128)}, u32[]{:S(2)}) copy-start(s32[1,2]{1,0:T(1,128)} %ws_ref.3) | copy-start | bytes 28
  98.6 12.7 %collective-permute-start = (bf16[1040,256]{1,0:T(8,128)(2,1)S(1)}, bf16[1040,256]{1,0:T(8,128)(2,1)S(1)}, u32[]{:S(2)}, u32[]{:S(2)}) collective-permute-start(bf16[1040,256]{1,0:T(8,128)(2,1)S(1)} %constant_dynamic-slice_fusion), channel_id=1, source_target_pairs={{32,64},{96,128},{160,192},{224,256},{288,320},{352,384},{416,448}... | collective-permute-start | bytes 1597448 | tf_op jit(solution)/shard_map/ppermute | solution.py:259
  104.0 3.8 %collective-permute-start.1 = (bf16[1024,256]{1,0:T(8,128)(2,1)S(1)}, bf16[1024,256]{1,0:T(8,128)(2,1)S(1)}, u32[]{:S(2)}, u32[]{:S(2)}) collective-permute-start(bf16[1024,256]{1,0:T(8,128)(2,1)S(1)} %get-tuple-element.9), channel_id=1, source_target_pairs={{0,32},{64,96},{128,160},{192,224},{256,288},{320,352},{384,416},{... | collective-permute-start | bytes 1572872 | tf_op jit(solution)/shard_map/ppermute | solution.py:262
  111.3 41.6 %copy-start = (f32[16,4096]{1,0:T(8,128)S(1)}, f32[16,4096]{1,0:T(8,128)}, u32[]{:S(2)}) copy-start(f32[16,4096]{1,0:T(8,128)} %mod_ref.3) | copy-start | bytes 786436
  111.3 41.6 %copy-start.1 = (bf16[64,4096]{1,0:T(8,128)(2,1)S(1)}, bf16[64,4096]{1,0:T(8,128)(2,1)}, u32[]{:S(2)}) copy-start(bf16[64,4096]{1,0:T(8,128)(2,1)} %state_ref.1) | copy-start | bytes 1572868
  111.3 41.6 %copy-start.2 = (bf16[64,4096]{1,0:T(8,128)(2,1)S(1)}, bf16[64,4096]{1,0:T(8,128)(2,1)}, u32[]{:S(2)}) copy-start(bf16[64,4096]{1,0:T(8,128)(2,1)} %fresh_ref.1) | copy-start | bytes 1572868
  114.3 38.6 %all-to-all-start.1 = ((bf16[32,64,128]{2,1,0:T(8,128)(2,1)}), bf16[32,64,128]{2,1,0:T(8,128)(2,1)S(1)}, u32[]{:S(2)}, u32[]{:S(2)}) async-start(bf16[32,64,128]{2,1,0:T(8,128)(2,1)} %bitcast.1), calls=%async_computation.1 | async-start | bytes 1048576 | tf_op jit(solution)/shard_map/all_to_all | solution.py:268
  153.3 12.6 %collective-permute-start.2 = (bf16[64,4096]{1,0:T(8,128)(2,1)S(1)}, bf16[64,4096]{1,0:T(8,128)(2,1)S(1)}, u32[]{:S(2)}, u32[]{:S(2)}) collective-permute-start(bf16[64,4096]{1,0:T(8,128)(2,1)S(1)} %shard_map.101), channel_id=1, source_target_pairs={{0,32},{32,64},{64,96},{96,128},{128,160},{160,192},{192,224},{224... | collective-permute-start | bytes 1572872 | tf_op jit(solution)/shard_map/ppermute | solution.py:271

commit v5 on v4

--- a/solution.py
+++ b/solution.py
@@ -78,13 +78,10 @@
     return odd if far else 1 - odd
 
 
-def own_kernel(far, qkv_ref, sums_ref, peak_ref, *refs):
-    value_ref = refs[-1]
+def own_kernel(far, qkv_ref, sums_ref, peak_ref, value_ref):
     frame_tok = peak_ref.shape[0]
     first = pl.multiple_of(frame_of(far) * frame_tok, frame_tok)
     own = pl.ds(first, frame_tok)
-    if not far:
-        refs[0][...] = qkv_ref[own, HEAD_DIM:]
     value_ref[:, :HEAD_DIM] = qkv_ref[own, 2 * HEAD_DIM :]
     value_ref[:, HEAD_DIM:] = jnp.ones((frame_tok, HEAD_DIM), jnp.bfloat16)
     for index in range(frame_tok // BLOCK):
@@ -107,8 +104,6 @@
         jax.ShapeDtypeStruct((frame_tok, 2 * HEAD_DIM), jnp.float32),
         jax.ShapeDtypeStruct((frame_tok, HEAD_DIM), jnp.float32),
     ]
-    if not far:
-        shapes.append(jax.ShapeDtypeStruct((frame_tok, 2 * HEAD_DIM), qkv.dtype))
     return pl.pallas_call(
         functools.partial(own_kernel, far),
         in_specs=[VMEM],
@@ -176,28 +171,37 @@
     other_frame(final, False, ws_ref, qkv_ref, halo_ref, sums_ref, peak_ref, key_ref, value_ref, store)
 
 
-def far_kernel(final, ws_ref, qkv_ref, halo_ref, sums_ref, peak_ref, near_ref, out_ref, key_ref, value_ref):
+def far_kernel(final, ws_ref, qkv_ref, halo_ref, sums_ref, peak_ref, near_ref, out_ref, key_ref, value_ref, held_ref, sem_ref):
     frame_tok = near_ref.shape[0]
     first = frame_of(True) * frame_tok
+    rest = pl.ds(pl.multiple_of(frame_of(False) * frame_tok, frame_tok), frame_tok)
+    copies = [pltpu.make_async_copy(near_ref, out_ref.at[rest], sem_ref.at[0])]
+    copies[0].start()
 
     def store(begin, result):
-        out_ref[pl.ds(pl.multiple_of(first + begin, BLOCK), BLOCK), :] = result
-
-    out_ref[pl.ds(pl.multiple_of(frame_of(False) * frame_tok, frame_tok), frame_tok), :] = near_ref[...]
+        rows = pl.ds(begin, BLOCK)
+        held_ref[rows, :] = result
+        there = out_ref.at[pl.ds(pl.multiple_of(first + begin, BLOCK), BLOCK)]
+        copies.append(pltpu.make_async_copy(held_ref.at[rows], there, sem_ref.at[len(copies)]))
+        copies[-1].start()
+
     other_frame(final, True, ws_ref, qkv_ref, halo_ref, sums_ref, peak_ref, key_ref, value_ref, store)
-
-
-def other_part(kernel, rows, window_start, qkv, *others):
+    for copy in copies:
+        copy.wait()
+
+
+def other_part(far, final, window_start, qkv, *others):
     frame_tok = qkv.shape[0] // FRAMES
-    return pl.pallas_call(
-        kernel,
+    out = jax.ShapeDtypeStruct((FRAMES * frame_tok if far else frame_tok, HEAD_DIM), qkv.dtype)
+    scratch = [pltpu.VMEM((frame_tok, HEAD_DIM), jnp.bfloat16), pltpu.VMEM((frame_tok, 2 * HEAD_DIM), jnp.bfloat16)]
+    if far:
+        scratch += [pltpu.VMEM((frame_tok, HEAD_DIM), jnp.bfloat16), pltpu.SemaphoreType.DMA((1 + frame_tok // BLOCK,))]
+    return pl.pallas_call(
+        functools.partial(far_kernel if far else near_kernel, final),
         in_specs=[SMEM] + [VMEM] * (1 + len(others)),
-        out_specs=VMEM,
-        out_shape=jax.ShapeDtypeStruct((rows, HEAD_DIM), qkv.dtype),
-        scratch_shapes=[
-            pltpu.VMEM((frame_tok, HEAD_DIM), jnp.bfloat16),
-            pltpu.VMEM((frame_tok, 2 * HEAD_DIM), jnp.bfloat16),
-        ],
+        out_specs=HBM if far else VMEM,
+        out_shape=out,
+        scratch_shapes=scratch,
         compiler_params=pltpu.CompilerParams(vmem_limit_bytes=LIMIT),
         cost_estimate=part_cost(frame_tok),
     )(window_start, qkv, *others)
@@ -257,13 +261,13 @@
     facing = lax.dynamic_slice(qkv, (start, HEAD_DIM), (frame_tok + MORE, 2 * HEAD_DIM))
     pairs = [(i, i + 1) for i in range(1, sections - 1, 2)]
     far = lax.ppermute(facing, "section", pairs + [(j, i) for i, j in pairs])
-    near_sums, near_peak, facing = own_part(False, qkv)
+    facing = lax.dynamic_slice(qkv, (frame_of(False) * frame_tok, HEAD_DIM), (frame_tok, 2 * HEAD_DIM))
     pairs = [(i, i + 1) for i in range(0, sections - 1, 2)]
     near = lax.ppermute(facing, "section", pairs + [(j, i) for i, j in pairs])
+    near_sums, near_peak = own_part(False, qkv)
     far_sums, far_peak = own_part(True, qkv)
-    kernels = [functools.partial(kernel, sections - 1) for kernel in (near_kernel, far_kernel)]
-    near_out = other_part(kernels[0], frame_tok, window_start, qkv, near, near_sums, near_peak)
-    attended = other_part(kernels[1], FRAMES * frame_tok, window_start, qkv, far, far_sums, far_peak, near_out)
+    near_out = other_part(False, sections - 1, window_start, qkv, near, near_sums, near_peak)
+    attended = other_part(True, sections - 1, window_start, qkv, far, far_sums, far_peak, near_out)
     attended = attended.reshape(feat // HEAD_DIM, tok_dev, HEAD_DIM)
     attended = lax.all_to_all(attended, "seq", split_axis=0, concat_axis=0, tiled=True)
     update = functools.partial(update_kernel, sections - 1)

time: 167 us -> 167 us (level)
  transfers between devices with their start and end apart: 5 -> 5, of which waited for: 5 -> 4; matrix products, arithmetic and copies ran while one was open for 0% -> 0% of each run, Pallas kernels for 4% -> 4%
where the time goes in v5:
time: 167 us
  waiting for transfers between devices  123 us (74%)
  starting transfers between devices  28.6 us (17%)
  Pallas kernels  12.4 us (7%)
    all_to_all x1, waiting for transfers between devices, per_device(): qkv = lax.all_to_all(packed, 'seq', split_axis=0, concat_axis=0, tiled=True)  78.6 us
    all_to_all x1, waiting for transfers between devices, per_device(): lax.all_to_all(attended, 'seq', split_axis=0, concat_axis=0, tiled=True)  33.7 us
    all_to_all x1, starting transfers between devices, per_device(): qkv = lax.all_to_all(packed, 'seq', split_axis=0, concat_axis=0, tiled=True)  16.9 us
    ppermute x1, waiting for transfers between devices, per_device(): lax.ppermute(passed, 'section', [(i, (i + 1) % sections) for i in range(s...  9.62 us
    pallas_call x2, Pallas kernels, other_part(): pl.pallas_call(functools.partial(far_kernel if far else near_kernel, fina...  5.03 us
    all_to_all x1, starting transfers between devices, per_device(): lax.all_to_all(attended, 'seq', split_axis=0, concat_axis=0, tiled=True)  4.28 us
    ppermute x1, starting transfers between devices, per_device(): far = lax.ppermute(facing, 'section', pairs + [(j, i) for i, j in pairs])  3.6 us
    pallas_call x2, Pallas kernels, own_part(): pl.pallas_call(functools.partial(own_kernel, far), in_specs=[VMEM], out_s...  3.52 us
  transfers between devices with their start and end apart: 5, of which 4 were waited for; matrix products, arithmetic and copies ran while one was open for 0% of the time, Pallas kernels for 4%

profile of v5, /device:TPU:34, one launch (start us, length us, event | category | flops | bytes accessed | tf_op | source)
XLA Modules:
  0.0 166.6 jit_solution(2473611031745948691)
XLA Ops:
  0.6 2.4 %shard_map.95 = bf16[32,64,384]{2,1,0:T(8,128)(2,1)} custom-call(bf16[64,4096]{1,0:T(8,128)(2,1)} %q_ref.1, bf16[64,4096]{1,0:T(8,128)(2,1)} %k_ref.1, bf16[64,4096]{1,0:T(8,128)(2,1)} %v_ref.1), custom_call_target="tpu_custom_call" | custom-call | tf_op jit(solution)/shard_map/pallas_call | solution.py:57
  3.0 16.9 %all-to-all-start = ((bf16[32,64,384]{2,1,0:T(8,128)(2,1)}), bf16[32,64,384]{2,1,0:T(8,128)(2,1)S(1)}, u32[]{:S(2)}, u32[]{:S(2)}) async-start(bf16[32,64,384]{2,1,0:T(8,128)(2,1)} %shard_map.95), calls=%async_computation | async-start | bytes 3145728 | tf_op jit(solution)/shard_map/all_to_all | solution.py:258
  20.0 78.6 %all-to-all-done = bf16[32,64,384]{2,1,0:T(8,128)(2,1)S(1)} async-done(((bf16[32,64,384]{2,1,0:T(8,128)(2,1)}), bf16[32,64,384]{2,1,0:T(8,128)(2,1)S(1)}, u32[]{:S(2)}, u32[]{:S(2)}) %all-to-all-start) | async-done | bytes 1572896 | tf_op jit(solution)/shard_map/all_to_all | solution.py:258
  98.6 3.6 %collective-permute-start = (bf16[1040,256]{1,0:T(8,128)(2,1)S(1)}, bf16[1040,256]{1,0:T(8,128)(2,1)S(1)}, u32[]{:S(2)}, u32[]{:S(2)}) collective-permute-start(bf16[1040,256]{1,0:T(8,128)(2,1)S(1)} %constant_dynamic-slice_fusion.1), channel_id=1, source_target_pairs={{32,64},{96,128},{160,192},{224,256},{288,320},{352,384},{416,448}... | collective-permute-start | bytes 1597448 | tf_op jit(solution)/shard_map/ppermute | solution.py:263
  102.2 0.0 copy-start.3
  102.3 1.9 %collective-permute-start.1 = (bf16[1024,256]{1,0:T(8,128)(2,1)S(1)}, bf16[1024,256]{1,0:T(8,128)(2,1)S(1)}, u32[]{:S(2)}, u32[]{:S(2)}) collective-permute-start(bf16[1024,256]{1,0:T(8,128)(2,1)S(1)} %constant_dynamic-slice_fusion), channel_id=1, source_target_pairs={{0,32},{64,96},{128,160},{192,224},{256,288},{320,352},{384,416},{... | collective-permute-start | bytes 1572872 | tf_op jit(solution)/shard_map/ppermute | solution.py:266
  104.2 1.8 %shard_map.97 = (f32[1024,256]{1,0:T(8,128)S(1)}, f32[1024,128]{1,0:T(8,128)S(1)}) custom-call(bf16[2048,384]{1,0:T(8,128)(2,1)S(1)} %bitcast.4), custom_call_target="tpu_custom_call" | custom-call | flops 1024 | bytes 1024 | tf_op jit(solution)/shard_map/pallas_call | solution.py:107
  106.0 1.8 %shard_map.96 = (f32[1024,256]{1,0:T(8,128)S(1)}, f32[1024,128]{1,0:T(8,128)S(1)}) custom-call(bf16[2048,384]{1,0:T(8,128)(2,1)S(1)} %bitcast.5), custom_call_target="tpu_custom_call" | custom-call | flops 1024 | bytes 1024 | tf_op jit(solution)/shard_map/pallas_call | solution.py:107
  107.7 0.0 collective-permute-done.1.halo_ref
  107.7 0.0 copy-done.3
  107.7 2.2 %shard_map.98.near_ref = bf16[1024,128]{1,0:T(8,128)(2,1)S(1)} custom-call(s32[1,2]{1,0:T(1,128)S(1)} %copy-done.3, bf16[2048,384]{1,0:T(8,128)(2,1)S(1)} %bitcast.6, bf16[1024,256]{1,0:T(8,128)(2,1)S(1)} %collective-permute-done.1.halo_ref, f32[1024,256]{1,0:T(8,128)S(1)} %get-tuple-element.8.sums_ref, f32[1024,128]{1,0:T(8,128)S(1)} %get-tuple-element.9.peak_ref), custom_call_target="tpu_custom_call" | custom-call | flops 1024 | bytes 1024 | tf_op jit(solution)/shard_map/pallas_call | solution.py:199
  109.9 1.4 collective-permute-done.halo_ref
  111.3 0.0 copy-start
  111.3 0.0 copy-start.1
  111.3 0.0 copy-start.2
  111.3 2.9 %shard_map.99 = bf16[2048,128]{1,0:T(8,128)(2,1)} custom-call(s32[1,2]{1,0:T(1,128)S(1)} %copy-done.3, bf16[2048,384]{1,0:T(8,128)(2,1)S(1)} %bitcast.7, bf16[1040,256]{1,0:T(8,128)(2,1)S(1)} %collective-permute-done.halo_ref, f32[1024,256]{1,0:T(8,128)S(1)} %get-tuple-element.6.sums_ref, f32[1024,128]{1,0:T(8,128)S(1)} %get-tuple-element.7.peak_ref, ...), custom_call_target="tpu_custom_call" | custom-call | flops 1024 | bytes 1024 | tf_op jit(solution)/shard_map/pallas_call | solution.py:199
  114.2 4.3 %all-to-all-start.1 = ((bf16[32,64,128]{2,1,0:T(8,128)(2,1)}), bf16[32,64,128]{2,1,0:T(8,128)(2,1)S(1)}, u32[]{:S(2)}, u32[]{:S(2)}) async-start(bf16[32,64,128]{2,1,0:T(8,128)(2,1)} %bitcast.1), calls=%async_computation.1 | async-start | bytes 1048576 | tf_op jit(solution)/shard_map/all_to_all | solution.py:272
  119.1 33.7 %all-to-all-done.1.att_ref = bf16[32,64,128]{2,1,0:T(8,128)(2,1)S(1)} async-done(((bf16[32,64,128]{2,1,0:T(8,128)(2,1)}), bf16[32,64,128]{2,1,0:T(8,128)(2,1)S(1)}, u32[]{:S(2)}, u32[]{:S(2)}) %all-to-all-start.1) | async-done | bytes 524320 | tf_op jit(solution)/shard_map/all_to_all | solution.py:272
  152.8 0.0 copy-done
  152.8 0.0 copy-done.1
  152.8 0.0 copy-done.2
  152.8 0.4 shard_map.101
  153.2 1.9 %collective-permute-start.2 = (bf16[64,4096]{1,0:T(8,128)(2,1)S(1)}, bf16[64,4096]{1,0:T(8,128)(2,1)S(1)}, u32[]{:S(2)}, u32[]{:S(2)}) collective-permute-start(bf16[64,4096]{1,0:T(8,128)(2,1)S(1)} %shard_map.101), channel_id=1, source_target_pairs={{0,32},{32,64},{64,96},{96,128},{128,160},{160,192},{192,224},{224... | collective-permute-start | bytes 1572872 | tf_op jit(solution)/shard_map/ppermute | solution.py:275
  155.1 1.1 shard_map.100
  156.2 9.6 %collective-permute-done.2 = bf16[64,4096]{1,0:T(8,128)(2,1)S(1)} collective-permute-done((bf16[64,4096]{1,0:T(8,128)(2,1)S(1)}, bf16[64,4096]{1,0:T(8,128)(2,1)S(1)}, u32[]{:S(2)}, u32[]{:S(2)}) %collective-permute-start.2) | collective-permute-done | bytes 524320 | tf_op jit(solution)/shard_map/ppermute | solution.py:275
  165.8 0.8 copy.12
  (2 shorter events, 0.1 us)
Async XLA Ops:
  3.0 95.5 %all-to-all-start = ((bf16[32,64,384]{2,1,0:T(8,128)(2,1)}), bf16[32,64,384]{2,1,0:T(8,128)(2,1)S(1)}, u32[]{:S(2)}, u32[]{:S(2)}) async-start(bf16[32,64,384]{2,1,0:T(8,128)(2,1)} %shard_map.95), calls=%async_computation | async-start | bytes 3145728 | tf_op jit(solution)/shard_map/all_to_all | solution.py:258
  98.6 12.7 %collective-permute-start = (bf16[1040,256]{1,0:T(8,128)(2,1)S(1)}, bf16[1040,256]{1,0:T(8,128)(2,1)S(1)}, u32[]{:S(2)}, u32[]{:S(2)}) collective-permute-start(bf16[1040,256]{1,0:T(8,128)(2,1)S(1)} %constant_dynamic-slice_fusion.1), channel_id=1, source_target_pairs={{32,64},{96,128},{160,192},{224,256},{288,320},{352,384},{416,448}... | collective-permute-start | bytes 1597448 | tf_op jit(solution)/shard_map/ppermute | solution.py:263
  102.2 5.5 %copy-start.3 = (s32[1,2]{1,0:T(1,128)S(1)}, s32[1,2]{1,0:T(1,128)}, u32[]{:S(2)}) copy-start(s32[1,2]{1,0:T(1,128)} %ws_ref.3) | copy-start | bytes 28
  102.3 5.5 %collective-permute-start.1 = (bf16[1024,256]{1,0:T(8,128)(2,1)S(1)}, bf16[1024,256]{1,0:T(8,128)(2,1)S(1)}, u32[]{:S(2)}, u32[]{:S(2)}) collective-permute-start(bf16[1024,256]{1,0:T(8,128)(2,1)S(1)} %constant_dynamic-slice_fusion), channel_id=1, source_target_pairs={{0,32},{64,96},{128,160},{192,224},{256,288},{320,352},{384,416},{... | collective-permute-start | bytes 1572872 | tf_op jit(solution)/shard_map/ppermute | solution.py:266
  111.3 41.5 %copy-start = (f32[16,4096]{1,0:T(8,128)S(1)}, f32[16,4096]{1,0:T(8,128)}, u32[]{:S(2)}) copy-start(f32[16,4096]{1,0:T(8,128)} %mod_ref.3) | copy-start | bytes 786436
  111.3 41.5 %copy-start.1 = (bf16[64,4096]{1,0:T(8,128)(2,1)S(1)}, bf16[64,4096]{1,0:T(8,128)(2,1)}, u32[]{:S(2)}) copy-start(bf16[64,4096]{1,0:T(8,128)(2,1)} %state_ref.1) | copy-start | bytes 1572868
  111.3 41.5 %copy-start.2 = (bf16[64,4096]{1,0:T(8,128)(2,1)S(1)}, bf16[64,4096]{1,0:T(8,128)(2,1)}, u32[]{:S(2)}) copy-start(bf16[64,4096]{1,0:T(8,128)(2,1)} %fresh_ref.1) | copy-start | bytes 1572868
  114.2 38.6 %all-to-all-start.1 = ((bf16[32,64,128]{2,1,0:T(8,128)(2,1)}), bf16[32,64,128]{2,1,0:T(8,128)(2,1)S(1)}, u32[]{:S(2)}, u32[]{:S(2)}) async-start(bf16[32,64,128]{2,1,0:T(8,128)(2,1)} %bitcast.1), calls=%async_computation.1 | async-start | bytes 1048576 | tf_op jit(solution)/shard_map/all_to_all | solution.py:272
  153.2 12.6 %collective-permute-start.2 = (bf16[64,4096]{1,0:T(8,128)(2,1)S(1)}, bf16[64,4096]{1,0:T(8,128)(2,1)S(1)}, u32[]{:S(2)}, u32[]{:S(2)}) collective-permute-start(bf16[64,4096]{1,0:T(8,128)(2,1)S(1)} %shard_map.101), channel_id=1, source_target_pairs={{0,32},{32,64},{64,96},{96,128},{128,160},{160,192},{192,224},{224... | collective-permute-start | bytes 1572872 | tf_op jit(solution)/shard_map/ppermute | solution.py:275

commit v6 on v5

--- a/solution.py
+++ b/solution.py
@@ -12,7 +12,7 @@
 NSTEPS = 16
 SCALE = 1.4426950408889634 / HEAD_DIM**0.5
 BLOCK = 256
-CHUNKS = 2
+CHUNKS = 4
 MORE = 16
 VMEM = pl.BlockSpec(memory_space=pltpu.VMEM)
 HBM = pl.BlockSpec(memory_space=pltpu.HBM)
@@ -26,27 +26,22 @@
     return 5.0 * share / (1.0 + 4.0 * share)
 
 
-def pack_kernel(q_ref, k_ref, v_ref, out_ref, held_ref, packed_ref, in_sem, out_sem):
+def pack_kernel(q_ref, k_ref, v_ref, out_ref, packed_ref, in_sem, out_sem):
     heads = out_ref.shape[0]
     group = heads // CHUNKS
-    copies = []
+    for head in range(heads):
+        cols = slice(head * HEAD_DIM, (head + 1) * HEAD_DIM)
+        for part, ref in enumerate((q_ref, k_ref, v_ref)):
+            there = packed_ref.at[head, :, part * HEAD_DIM : (part + 1) * HEAD_DIM]
+            pltpu.make_async_copy(ref.at[:, cols], there, in_sem.at[head // group]).start()
+    leaving = []
     for chunk in range(CHUNKS):
-        cols = slice(chunk * group * HEAD_DIM, (chunk + 1) * group * HEAD_DIM)
-        for part, ref in enumerate((q_ref, k_ref, v_ref)):
-            copy = pltpu.make_async_copy(ref.at[:, cols], held_ref.at[part, :, cols], in_sem.at[chunk, part])
-            copy.start()
-            copies.append(copy)
-    for chunk in range(CHUNKS):
-        mine = slice(chunk * group, (chunk + 1) * group)
-        for part in range(3):
-            copies[3 * chunk + part].wait()
-            for head in range(chunk * group, (chunk + 1) * group):
-                cols = slice(head * HEAD_DIM, (head + 1) * HEAD_DIM)
-                packed_ref[head, :, part * HEAD_DIM : (part + 1) * HEAD_DIM] = held_ref[part, :, cols]
-        copy = pltpu.make_async_copy(packed_ref.at[mine], out_ref.at[mine], out_sem.at[chunk])
-        copy.start()
-        copies.append(copy)
-    for copy in copies[3 * CHUNKS :]:
+        mine = packed_ref.at[chunk * group : (chunk + 1) * group]
+        pltpu.make_async_copy(mine, mine, in_sem.at[chunk]).wait()
+        there = out_ref.at[chunk * group : (chunk + 1) * group]
+        leaving.append(pltpu.make_async_copy(mine, there, out_sem.at[chunk]))
+        leaving[-1].start()
+    for copy in leaving:
         copy.wait()
 
 
@@ -60,9 +55,8 @@
         out_specs=HBM,
         out_shape=jax.ShapeDtypeStruct(shape, queries.dtype),
         scratch_shapes=[
-            pltpu.VMEM((3, tok, feat), queries.dtype),
             pltpu.VMEM(shape, queries.dtype),
-            pltpu.SemaphoreType.DMA((CHUNKS, 3)),
+            pltpu.SemaphoreType.DMA((CHUNKS,)),
             pltpu.SemaphoreType.DMA((CHUNKS,)),
         ],
         compiler_params=pltpu.CompilerParams(vmem_limit_bytes=WHOLE),
@@ -78,9 +72,9 @@
     return odd if far else 1 - odd
 
 
-def own_kernel(far, qkv_ref, sums_ref, peak_ref, value_ref):
+def own_kernel(qkv_ref, sums_ref, peak_ref, value_ref):
     frame_tok = peak_ref.shape[0]
-    first = pl.multiple_of(frame_of(far) * frame_tok, frame_tok)
+    first = pl.multiple_of(frame_of(True) * frame_tok, frame_tok)
     own = pl.ds(first, frame_tok)
     value_ref[:, :HEAD_DIM] = qkv_ref[own, 2 * HEAD_DIM :]
     value_ref[:, HEAD_DIM:] = jnp.ones((frame_tok, HEAD_DIM), jnp.bfloat16)
@@ -98,14 +92,14 @@
     return pl.CostEstimate(flops=frame_tok, bytes_accessed=frame_tok, transcendentals=0)
 
 
-def own_part(far, qkv):
+def own_part(qkv):
     frame_tok = qkv.shape[0] // FRAMES
     shapes = [
         jax.ShapeDtypeStruct((frame_tok, 2 * HEAD_DIM), jnp.float32),
         jax.ShapeDtypeStruct((frame_tok, HEAD_DIM), jnp.float32),
     ]
     return pl.pallas_call(
-        functools.partial(own_kernel, far),
+        own_kernel,
         in_specs=[VMEM],
         out_specs=[VMEM] * len(shapes),
         out_shape=shapes,
@@ -115,13 +109,13 @@
     )(qkv)
 
 
-def other_frame(final, far, ws_ref, qkv_ref, halo_ref, sums_ref, peak_ref, key_ref, value_ref, store):
+def other_frame(final, far, ws_ref, qkv_ref, halo_ref, key_ref, value_ref):
     frame_tok = qkv_ref.shape[0] // FRAMES
     position = lax.axis_index("section")
     frame = frame_of(far)
     outside = ws_ref[0, frame] == frame - 1
     exists = jnp.where(frame == 0, position > 0, position < final)
-    own = pl.multiple_of(frame * frame_tok, frame_tok)
+    own = pl.ds(pl.multiple_of(frame * frame_tok, frame_tok), frame_tok)
     other = pl.ds(pl.multiple_of((1 - frame) * frame_tok, frame_tok), frame_tok)
     k_cols, v_cols = slice(HEAD_DIM, 2 * HEAD_DIM), slice(2 * HEAD_DIM, 3 * HEAD_DIM)
     value_ref[:, HEAD_DIM:] = jnp.ones((frame_tok, HEAD_DIM), jnp.bfloat16)
@@ -139,11 +133,46 @@
 
     @pl.when(jnp.logical_and(outside, jnp.logical_not(exists)))
     def _():
-        key_ref[...] = qkv_ref[pl.ds(own, frame_tok), k_cols]
+        key_ref[...] = qkv_ref[own, k_cols]
         value_ref[...] = jnp.zeros((frame_tok, 2 * HEAD_DIM), jnp.bfloat16)
 
+
+def near_kernel(final, ws_ref, qkv_ref, halo_ref, out_ref, key_ref, value_ref):
+    frame_tok = out_ref.shape[0]
+    first = pl.multiple_of(frame_of(False) * frame_tok, frame_tok)
+    own, rest = pl.ds(first, frame_tok), pl.ds(frame_tok, frame_tok)
+    key_ref[:frame_tok] = qkv_ref[own, HEAD_DIM : 2 * HEAD_DIM]
+    value_ref[:frame_tok, :HEAD_DIM] = qkv_ref[own, 2 * HEAD_DIM :]
+    value_ref[:frame_tok, HEAD_DIM:] = jnp.ones((frame_tok, HEAD_DIM), jnp.bfloat16)
+    other_frame(final, False, ws_ref, qkv_ref, halo_ref, key_ref.at[rest], value_ref.at[rest])
+
     def scores(index):
-        rows = pl.ds(pl.multiple_of(own + index * BLOCK, BLOCK), BLOCK)
+        rows = pl.ds(pl.multiple_of(first + index * BLOCK, BLOCK), BLOCK)
+        return scores_of(qkv_ref[rows, :HEAD_DIM], key_ref[...])
+
+    blocks = frame_tok // BLOCK
+    after = scores(0)
+    for index in range(blocks):
+        here = after
+        if index + 1 < blocks:
+            after = scores(index + 1)
+        peak = jnp.max(here, axis=-1, keepdims=True)
+        weights = jnp.exp2((here - peak) * SCALE).astype(jnp.bfloat16)
+        sums = jnp.dot(weights, value_ref[...], preferred_element_type=jnp.float32)
+        result = (sums[:, :HEAD_DIM] / sums[:, HEAD_DIM:]).astype(jnp.bfloat16)
+        out_ref[index * BLOCK : (index + 1) * BLOCK, :] = result
+
+
+def far_kernel(final, ws_ref, qkv_ref, halo_ref, sums_ref, peak_ref, near_ref, out_ref, key_ref, value_ref, held_ref, sem_ref):
+    frame_tok = near_ref.shape[0]
+    first = pl.multiple_of(frame_of(True) * frame_tok, frame_tok)
+    rest = pl.ds(pl.multiple_of(frame_of(False) * frame_tok, frame_tok), frame_tok)
+    copies = [pltpu.make_async_copy(near_ref, out_ref.at[rest], sem_ref.at[0])]
+    copies[0].start()
+    other_frame(final, True, ws_ref, qkv_ref, halo_ref, key_ref, value_ref)
+
+    def scores(index):
+        rows = pl.ds(pl.multiple_of(first + index * BLOCK, BLOCK), BLOCK)
         return scores_of(qkv_ref[rows, :HEAD_DIM], key_ref[...])
 
     blocks = frame_tok // BLOCK
@@ -161,39 +190,19 @@
         share = jnp.exp2((before - peak) * SCALE)
         mixed = sums[:, :HEAD_DIM] + sums_ref[rows, :HEAD_DIM] * share
         total = sums[:, HEAD_DIM:] + sums_ref[rows, HEAD_DIM:] * share
-        store(index * BLOCK, (mixed / total).astype(jnp.bfloat16))
-
-
-def near_kernel(final, ws_ref, qkv_ref, halo_ref, sums_ref, peak_ref, out_ref, key_ref, value_ref):
-    def store(begin, result):
-        out_ref[pl.ds(begin, BLOCK), :] = result
-
-    other_frame(final, False, ws_ref, qkv_ref, halo_ref, sums_ref, peak_ref, key_ref, value_ref, store)
-
-
-def far_kernel(final, ws_ref, qkv_ref, halo_ref, sums_ref, peak_ref, near_ref, out_ref, key_ref, value_ref, held_ref, sem_ref):
-    frame_tok = near_ref.shape[0]
-    first = frame_of(True) * frame_tok
-    rest = pl.ds(pl.multiple_of(frame_of(False) * frame_tok, frame_tok), frame_tok)
-    copies = [pltpu.make_async_copy(near_ref, out_ref.at[rest], sem_ref.at[0])]
-    copies[0].start()
-
-    def store(begin, result):
-        rows = pl.ds(begin, BLOCK)
-        held_ref[rows, :] = result
-        there = out_ref.at[pl.ds(pl.multiple_of(first + begin, BLOCK), BLOCK)]
-        copies.append(pltpu.make_async_copy(held_ref.at[rows], there, sem_ref.at[len(copies)]))
+        held_ref[rows, :] = (mixed / total).astype(jnp.bfloat16)
+        there = out_ref.at[pl.ds(pl.multiple_of(first + index * BLOCK, BLOCK), BLOCK)]
+        copies.append(pltpu.make_async_copy(held_ref.at[rows], there, sem_ref.at[1 + index]))
         copies[-1].start()
-
-    other_frame(final, True, ws_ref, qkv_ref, halo_ref, sums_ref, peak_ref, key_ref, value_ref, store)
     for copy in copies:
         copy.wait()
 
 
-def other_part(far, final, window_start, qkv, *others):
+def window_part(far, final, window_start, qkv, *others):
     frame_tok = qkv.shape[0] // FRAMES
     out = jax.ShapeDtypeStruct((FRAMES * frame_tok if far else frame_tok, HEAD_DIM), qkv.dtype)
-    scratch = [pltpu.VMEM((frame_tok, HEAD_DIM), jnp.bfloat16), pltpu.VMEM((frame_tok, 2 * HEAD_DIM), jnp.bfloat16)]
+    keys = frame_tok if far else FRAMES * frame_tok
+    scratch = [pltpu.VMEM((keys, HEAD_DIM), jnp.bfloat16), pltpu.VMEM((keys, 2 * HEAD_DIM), jnp.bfloat16)]
     if far:
         scratch += [pltpu.VMEM((frame_tok, HEAD_DIM), jnp.bfloat16), pltpu.SemaphoreType.DMA((1 + frame_tok // BLOCK,))]
     return pl.pallas_call(
@@ -264,10 +273,9 @@
     facing = lax.dynamic_slice(qkv, (frame_of(False) * frame_tok, HEAD_DIM), (frame_tok, 2 * HEAD_DIM))
     pairs = [(i, i + 1) for i in range(0, sections - 1, 2)]
     near = lax.ppermute(facing, "section", pairs + [(j, i) for i, j in pairs])
-    near_sums, near_peak = own_part(False, qkv)
-    far_sums, far_peak = own_part(True, qkv)
-    near_out = other_part(False, sections - 1, window_start, qkv, near, near_sums, near_peak)
-    attended = other_part(True, sections - 1, window_start, qkv, far, far_sums, far_peak, near_out)
+    sums, peak = own_part(qkv)
+    near_out = window_part(False, sections - 1, window_start, qkv, near)
+    attended = window_part(True, sections - 1, window_start, qkv, far, sums, peak, near_out)
     attended = attended.reshape(feat // HEAD_DIM, tok_dev, HEAD_DIM)
     attended = lax.all_to_all(attended, "seq", split_axis=0, concat_axis=0, tiled=True)
     update = functools.partial(update_kernel, sections - 1)

time: 167 us -> 166 us (level)
    pallas_call x4 -> x3, Pallas kernels: 8.55 us -> 8.04 us  [the longest x2 6.31 us: window_part(): pl.pallas_call(functools.partial(far_kernel if far else near_kernel, fina...]
  transfers between devices with their start and end apart: 5 -> 5, of which waited for: 4 -> 5; matrix products, arithmetic and copies ran while one was open for 0% -> 0% of each run, Pallas kernels for 4% -> 4%
where the time goes in v6:
time: 166 us
  waiting for transfers between devices  123 us (74%)
  starting transfers between devices  28.6 us (17%)
  Pallas kernels  11.8 us (7%)
    all_to_all x1, waiting for transfers between devices, per_device(): qkv = lax.all_to_all(packed, 'seq', split_axis=0, concat_axis=0, tiled=True)  78.6 us
    all_to_all x1, waiting for transfers between devices, per_device(): lax.all_to_all(attended, 'seq', split_axis=0, concat_axis=0, tiled=True)  33 us
    all_to_all x1, starting transfers between devices, per_device(): qkv = lax.all_to_all(packed, 'seq', split_axis=0, concat_axis=0, tiled=True)  16.9 us
    ppermute x1, waiting for transfers between devices, per_device(): lax.ppermute(passed, 'section', [(i, (i + 1) % sections) for i in range(s...  9.62 us
    pallas_call x2, Pallas kernels, window_part(): pl.pallas_call(functools.partial(far_kernel if far else near_kernel, fina...  6.31 us
    all_to_all x1, starting transfers between devices, per_device(): lax.all_to_all(attended, 'seq', split_axis=0, concat_axis=0, tiled=True)  4.28 us
    ppermute x1, starting transfers between devices, per_device(): far = lax.ppermute(facing, 'section', pairs + [(j, i) for i, j in pairs])  3.6 us
  transfers between devices with their start and end apart: 5, of which 5 were waited for; matrix products, arithmetic and copies ran while one was open for 0% of the time, Pallas kernels for 4%

profile of v6, /device:TPU:34, one launch (start us, length us, event | category | flops | bytes accessed | tf_op | source)
XLA Modules:
  0.0 165.8 jit_solution(15295052057451952917)
XLA Ops:
  0.6 2.2 %shard_map.95 = bf16[32,64,384]{2,1,0:T(8,128)(2,1)} custom-call(bf16[64,4096]{1,0:T(8,128)(2,1)} %q_ref.1, bf16[64,4096]{1,0:T(8,128)(2,1)} %k_ref.1, bf16[64,4096]{1,0:T(8,128)(2,1)} %v_ref.1), custom_call_target="tpu_custom_call" | custom-call | tf_op jit(solution)/shard_map/pallas_call | solution.py:52
  2.9 16.9 %all-to-all-start = ((bf16[32,64,384]{2,1,0:T(8,128)(2,1)}), bf16[32,64,384]{2,1,0:T(8,128)(2,1)S(1)}, u32[]{:S(2)}, u32[]{:S(2)}) async-start(bf16[32,64,384]{2,1,0:T(8,128)(2,1)} %shard_map.95), calls=%async_computation | async-start | bytes 3145728 | tf_op jit(solution)/shard_map/all_to_all | solution.py:267
  19.8 78.6 %all-to-all-done = bf16[32,64,384]{2,1,0:T(8,128)(2,1)S(1)} async-done(((bf16[32,64,384]{2,1,0:T(8,128)(2,1)}), bf16[32,64,384]{2,1,0:T(8,128)(2,1)S(1)}, u32[]{:S(2)}, u32[]{:S(2)}) %all-to-all-start) | async-done | bytes 1572896 | tf_op jit(solution)/shard_map/all_to_all | solution.py:267
  98.4 0.0 copy-start.3
  98.4 3.6 %collective-permute-start = (bf16[1040,256]{1,0:T(8,128)(2,1)S(1)}, bf16[1040,256]{1,0:T(8,128)(2,1)S(1)}, u32[]{:S(2)}, u32[]{:S(2)}) collective-permute-start(bf16[1040,256]{1,0:T(8,128)(2,1)S(1)} %constant_dynamic-slice_fusion.1), channel_id=1, source_target_pairs={{32,64},{96,128},{160,192},{224,256},{288,320},{352,384},{416,448}... | collective-permute-start | bytes 1597448 | tf_op jit(solution)/shard_map/ppermute | solution.py:272
  102.1 1.9 %collective-permute-start.1 = (bf16[1024,256]{1,0:T(8,128)(2,1)S(1)}, bf16[1024,256]{1,0:T(8,128)(2,1)S(1)}, u32[]{:S(2)}, u32[]{:S(2)}) collective-permute-start(bf16[1024,256]{1,0:T(8,128)(2,1)S(1)} %constant_dynamic-slice_fusion), channel_id=1, source_target_pairs={{0,32},{64,96},{128,160},{192,224},{256,288},{320,352},{384,416},{... | collective-permute-start | bytes 1572872 | tf_op jit(solution)/shard_map/ppermute | solution.py:275
  104.0 1.7 %shard_map.96 = (f32[1024,256]{1,0:T(8,128)S(1)}, f32[1024,128]{1,0:T(8,128)S(1)}) custom-call(bf16[2048,384]{1,0:T(8,128)(2,1)S(1)} %bitcast.4), custom_call_target="tpu_custom_call" | custom-call | flops 1024 | bytes 1024 | tf_op jit(solution)/shard_map/pallas_call | solution.py:101
  105.8 0.1 collective-permute-done.1.halo_ref
  105.9 0.0 copy-done.3
  105.9 3.5 %shard_map.97.near_ref = bf16[1024,128]{1,0:T(8,128)(2,1)S(1)} custom-call(s32[1,2]{1,0:T(1,128)S(1)} %copy-done.3, bf16[2048,384]{1,0:T(8,128)(2,1)S(1)} %bitcast.5, bf16[1024,256]{1,0:T(8,128)(2,1)S(1)} %collective-permute-done.1.halo_ref), custom_call_target="tpu_custom_call" | custom-call | flops 1024 | bytes 1024 | tf_op jit(solution)/shard_map/pallas_call | solution.py:208
  109.4 1.8 %collective-permute-done.halo_ref = bf16[1040,256]{1,0:T(8,128)(2,1)S(1)} collective-permute-done((bf16[1040,256]{1,0:T(8,128)(2,1)S(1)}, bf16[1040,256]{1,0:T(8,128)(2,1)S(1)}, u32[]{:S(2)}, u32[]{:S(2)}) %collective-permute-start) | collective-permute-done | bytes 532512 | tf_op jit(solution)/shard_map/ppermute | solution.py:272
  111.1 0.0 copy-start
  111.1 0.0 copy-start.1
  111.1 0.0 copy-start.2
  111.1 2.9 %shard_map.98 = bf16[2048,128]{1,0:T(8,128)(2,1)} custom-call(s32[1,2]{1,0:T(1,128)S(1)} %copy-done.3, bf16[2048,384]{1,0:T(8,128)(2,1)S(1)} %bitcast.6, bf16[1040,256]{1,0:T(8,128)(2,1)S(1)} %collective-permute-done.halo_ref, f32[1024,256]{1,0:T(8,128)S(1)} %get-tuple-element.4.sums_ref, f32[1024,128]{1,0:T(8,128)S(1)} %get-tuple-element.5.peak_ref, ...), custom_call_target="tpu_custom_call" | custom-call | flops 1024 | bytes 1024 | tf_op jit(solution)/shard_map/pallas_call | solution.py:208
  114.0 4.3 %all-to-all-start.1 = ((bf16[32,64,128]{2,1,0:T(8,128)(2,1)}), bf16[32,64,128]{2,1,0:T(8,128)(2,1)S(1)}, u32[]{:S(2)}, u32[]{:S(2)}) async-start(bf16[32,64,128]{2,1,0:T(8,128)(2,1)} %bitcast.1), calls=%async_computation.1 | async-start | bytes 1048576 | tf_op jit(solution)/shard_map/all_to_all | solution.py:280
  118.9 33.0 %all-to-all-done.1.att_ref = bf16[32,64,128]{2,1,0:T(8,128)(2,1)S(1)} async-done(((bf16[32,64,128]{2,1,0:T(8,128)(2,1)}), bf16[32,64,128]{2,1,0:T(8,128)(2,1)S(1)}, u32[]{:S(2)}, u32[]{:S(2)}) %all-to-all-start.1) | async-done | bytes 524320 | tf_op jit(solution)/shard_map/all_to_all | solution.py:280
  152.0 0.0 copy-done
  152.0 0.0 copy-done.1
  152.0 0.0 copy-done.2
  152.0 0.4 shard_map.100
  152.4 1.9 %collective-permute-start.2 = (bf16[64,4096]{1,0:T(8,128)(2,1)S(1)}, bf16[64,4096]{1,0:T(8,128)(2,1)S(1)}, u32[]{:S(2)}, u32[]{:S(2)}) collective-permute-start(bf16[64,4096]{1,0:T(8,128)(2,1)S(1)} %shard_map.100), channel_id=1, source_target_pairs={{0,32},{32,64},{64,96},{96,128},{128,160},{160,192},{192,224},{224... | collective-permute-start | bytes 1572872 | tf_op jit(solution)/shard_map/ppermute | solution.py:283
  154.3 1.1 shard_map.99
  155.4 9.6 %collective-permute-done.2 = bf16[64,4096]{1,0:T(8,128)(2,1)S(1)} collective-permute-done((bf16[64,4096]{1,0:T(8,128)(2,1)S(1)}, bf16[64,4096]{1,0:T(8,128)(2,1)S(1)}, u32[]{:S(2)}, u32[]{:S(2)}) %collective-permute-start.2) | collective-permute-done | bytes 524320 | tf_op jit(solution)/shard_map/ppermute | solution.py:283
  165.0 0.8 copy.12
  (2 shorter events, 0.1 us)
Async XLA Ops:
  2.9 95.5 %all-to-all-start = ((bf16[32,64,384]{2,1,0:T(8,128)(2,1)}), bf16[32,64,384]{2,1,0:T(8,128)(2,1)S(1)}, u32[]{:S(2)}, u32[]{:S(2)}) async-start(bf16[32,64,384]{2,1,0:T(8,128)(2,1)} %shard_map.95), calls=%async_computation | async-start | bytes 3145728 | tf_op jit(solution)/shard_map/all_to_all | solution.py:267
  98.4 7.5 %copy-start.3 = (s32[1,2]{1,0:T(1,128)S(1)}, s32[1,2]{1,0:T(1,128)}, u32[]{:S(2)}) copy-start(s32[1,2]{1,0:T(1,128)} %ws_ref.3) | copy-start | bytes 28
  98.4 12.7 %collective-permute-start = (bf16[1040,256]{1,0:T(8,128)(2,1)S(1)}, bf16[1040,256]{1,0:T(8,128)(2,1)S(1)}, u32[]{:S(2)}, u32[]{:S(2)}) collective-permute-start(bf16[1040,256]{1,0:T(8,128)(2,1)S(1)} %constant_dynamic-slice_fusion.1), channel_id=1, source_target_pairs={{32,64},{96,128},{160,192},{224,256},{288,320},{352,384},{416,448}... | collective-permute-start | bytes 1597448 | tf_op jit(solution)/shard_map/ppermute | solution.py:272
  102.1 3.8 %collective-permute-start.1 = (bf16[1024,256]{1,0:T(8,128)(2,1)S(1)}, bf16[1024,256]{1,0:T(8,128)(2,1)S(1)}, u32[]{:S(2)}, u32[]{:S(2)}) collective-permute-start(bf16[1024,256]{1,0:T(8,128)(2,1)S(1)} %constant_dynamic-slice_fusion), channel_id=1, source_target_pairs={{0,32},{64,96},{128,160},{192,224},{256,288},{320,352},{384,416},{... | collective-permute-start | bytes 1572872 | tf_op jit(solution)/shard_map/ppermute | solution.py:275
  111.1 40.8 %copy-start = (f32[16,4096]{1,0:T(8,128)S(1)}, f32[16,4096]{1,0:T(8,128)}, u32[]{:S(2)}) copy-start(f32[16,4096]{1,0:T(8,128)} %mod_ref.3) | copy-start | bytes 786436
  111.1 40.8 %copy-start.1 = (bf16[64,4096]{1,0:T(8,128)(2,1)S(1)}, bf16[64,4096]{1,0:T(8,128)(2,1)}, u32[]{:S(2)}) copy-start(bf16[64,4096]{1,0:T(8,128)(2,1)} %state_ref.1) | copy-start | bytes 1572868
  111.1 40.8 %copy-start.2 = (bf16[64,4096]{1,0:T(8,128)(2,1)S(1)}, bf16[64,4096]{1,0:T(8,128)(2,1)}, u32[]{:S(2)}) copy-start(bf16[64,4096]{1,0:T(8,128)(2,1)} %fresh_ref.1) | copy-start | bytes 1572868
  114.0 38.0 %all-to-all-start.1 = ((bf16[32,64,128]{2,1,0:T(8,128)(2,1)}), bf16[32,64,128]{2,1,0:T(8,128)(2,1)S(1)}, u32[]{:S(2)}, u32[]{:S(2)}) async-start(bf16[32,64,128]{2,1,0:T(8,128)(2,1)} %bitcast.1), calls=%async_computation.1 | async-start | bytes 1048576 | tf_op jit(solution)/shard_map/all_to_all | solution.py:280
  152.4 12.6 %collective-permute-start.2 = (bf16[64,4096]{1,0:T(8,128)(2,1)S(1)}, bf16[64,4096]{1,0:T(8,128)(2,1)S(1)}, u32[]{:S(2)}, u32[]{:S(2)}) collective-permute-start(bf16[64,4096]{1,0:T(8,128)(2,1)S(1)} %shard_map.100), channel_id=1, source_target_pairs={{0,32},{32,64},{64,96},{96,128},{128,160},{160,192},{192,224},{224... | collective-permute-start | bytes 1572872 | tf_op jit(solution)/shard_map/ppermute | solution.py:283

commit v7 on v6

--- a/solution.py
+++ b/solution.py
@@ -216,11 +216,12 @@
     )(window_start, qkv, *others)
 
 
-def velocity_of(step_ref, att_ref, mod_ref):
-    heads, tok, _ = att_ref.shape
+def velocity_of(step_ref, att_ref, mod_ref, begin, tok):
+    heads = att_ref.shape[0]
+    rows = slice(begin, begin + tok)
     squares = jnp.zeros((tok, HEAD_DIM), jnp.float32)
     for head in range(heads):
-        a = att_ref[head].astype(jnp.float32)
+        a = att_ref[head, rows].astype(jnp.float32)
         squares += a * a
     mean = jnp.sum(squares, axis=-1, keepdims=True) / (heads * HEAD_DIM)
     inverse = jnp.broadcast_to(1.0 / jnp.sqrt(mean + 1e-06), (tok, HEAD_DIM))
@@ -228,27 +229,29 @@
     for head in range(heads):
         cols = slice(head * HEAD_DIM, (head + 1) * HEAD_DIM)
         gain = jnp.sum(jnp.where(chosen, mod_ref[:, cols], 0.0), axis=0, keepdims=True)
-        yield cols, att_ref[head].astype(jnp.float32) * inverse * gain
-
-
-def update_kernel(final, step_ref, att_ref, mod_ref, state_ref, fresh_ref, passed_ref):
+        yield cols, att_ref[head, rows].astype(jnp.float32) * inverse * gain
+
+
+def update_kernel(final, begin, step_ref, att_ref, mod_ref, state_ref, fresh_ref, passed_ref):
+    tok = passed_ref.shape[0]
+    rows = slice(begin, begin + tok)
     now = jnp.full((1, HEAD_DIM), step_ref[0], jnp.int32)
     delta = level((now - 1).astype(jnp.float32)) - level(now.astype(jnp.float32))
-    for cols, moving in velocity_of(step_ref, att_ref, mod_ref):
-        passed_ref[:, cols] = (state_ref[:, cols].astype(jnp.float32) + delta * moving).astype(jnp.bfloat16)
+    for cols, moving in velocity_of(step_ref, att_ref, mod_ref, begin, tok):
+        passed_ref[:, cols] = (state_ref[rows, cols].astype(jnp.float32) + delta * moving).astype(jnp.bfloat16)
 
     @pl.when(lax.axis_index("section") == final)
     def _():
-        passed_ref[...] = fresh_ref[...]
+        passed_ref[...] = fresh_ref[rows]
 
 
 def velocity_kernel(step_ref, att_ref, mod_ref, velocity_ref):
-    for cols, moving in velocity_of(step_ref, att_ref, mod_ref):
+    for cols, moving in velocity_of(step_ref, att_ref, mod_ref, 0, velocity_ref.shape[0]):
         velocity_ref[:, cols] = moving.astype(jnp.bfloat16)
 
 
-def finish(kernel, timestep, attended, modulation, *others):
-    heads, tok, _ = attended.shape
+def finish(kernel, tok, timestep, attended, modulation, *others):
+    heads = attended.shape[0]
     return pl.pallas_call(
         kernel,
         in_specs=[SMEM] + [VMEM] * (2 + len(others)),
@@ -278,11 +281,15 @@
     attended = window_part(True, sections - 1, window_start, qkv, far, sums, peak, near_out)
     attended = attended.reshape(feat // HEAD_DIM, tok_dev, HEAD_DIM)
     attended = lax.all_to_all(attended, "seq", split_axis=0, concat_axis=0, tiled=True)
-    update = functools.partial(update_kernel, sections - 1)
-    passed = finish(update, timestep, attended, modulation, queue_state, fresh_state)
-    advanced = lax.ppermute(passed, "section", [(i, (i + 1) % sections) for i in range(sections)])
-    velocity = finish(velocity_kernel, timestep, attended, modulation)
-    return velocity, advanced
+    ring = [(i, (i + 1) % sections) for i in range(sections)]
+    half = tok_dev // 2
+    halves = []
+    for begin in (0, half):
+        update = functools.partial(update_kernel, sections - 1, begin)
+        passed = finish(update, half, timestep, attended, modulation, queue_state, fresh_state)
+        halves.append(lax.ppermute(passed, "section", ring))
+    velocity = finish(velocity_kernel, tok_dev, timestep, attended, modulation)
+    return velocity, jnp.concatenate(halves, axis=0)
 
 
 def solution(mesh):

time: 166 us -> 166 us (level)
  starting transfers between devices: 28.6 us -> 30.9 us
  waiting for transfers between devices: 123 us -> 121 us
    ppermute x1 -> x2, waiting for transfers between devices: 9.62 us -> 7.12 us  [per_device(): halves.append(lax.ppermute(passed, 'section', ring))]
    ppermute x1 -> x2, starting transfers between devices: 1.92 us -> 4.14 us  [per_device(): halves.append(lax.ppermute(passed, 'section', ring))]
  transfers between devices with their start and end apart: 5 -> 6, of which waited for: 5 -> 6; matrix products, arithmetic and copies ran while one was open for 0% -> 0% of each run, Pallas kernels for 4% -> 4%
where the time goes in v7:
time: 166 us
  waiting for transfers between devices  121 us (73%)
  starting transfers between devices  30.9 us (19%)
  Pallas kernels  11.8 us (7%)
    all_to_all x1, waiting for transfers between devices, per_device(): qkv = lax.all_to_all(packed, 'seq', split_axis=0, concat_axis=0, tiled=True)  78.6 us
    all_to_all x1, waiting for transfers between devices, per_device(): lax.all_to_all(attended, 'seq', split_axis=0, concat_axis=0, tiled=True)  33 us
    all_to_all x1, starting transfers between devices, per_device(): qkv = lax.all_to_all(packed, 'seq', split_axis=0, concat_axis=0, tiled=True)  16.9 us
    ppermute x2, waiting for transfers between devices, per_device(): halves.append(lax.ppermute(passed, 'section', ring))  7.12 us
    pallas_call x2, Pallas kernels, window_part(): pl.pallas_call(functools.partial(far_kernel if far else near_kernel, fina...  6.31 us
    all_to_all x1, starting transfers between devices, per_device(): lax.all_to_all(attended, 'seq', split_axis=0, concat_axis=0, tiled=True)  4.28 us
    ppermute x2, starting transfers between devices, per_device(): halves.append(lax.ppermute(passed, 'section', ring))  4.14 us
    ppermute x1, starting transfers between devices, per_device(): far = lax.ppermute(facing, 'section', pairs + [(j, i) for i, j in pairs])  3.6 us
  transfers between devices with their start and end apart: 6, of which 6 were waited for; matrix products, arithmetic and copies ran while one was open for 0% of the time, Pallas kernels for 4%

profile of v7, /device:TPU:34, one launch (start us, length us, event | category | flops | bytes accessed | tf_op | source)
XLA Modules:
  0.0 165.7 jit_solution(908668344159871687)
XLA Ops:
  0.6 2.2 %shard_map.95 = bf16[32,64,384]{2,1,0:T(8,128)(2,1)} custom-call(bf16[64,4096]{1,0:T(8,128)(2,1)} %q_ref.1, bf16[64,4096]{1,0:T(8,128)(2,1)} %k_ref.1, bf16[64,4096]{1,0:T(8,128)(2,1)} %v_ref.1), custom_call_target="tpu_custom_call" | custom-call | tf_op jit(solution)/shard_map/pallas_call | solution.py:52
  2.9 16.9 %all-to-all-start = ((bf16[32,64,384]{2,1,0:T(8,128)(2,1)}), bf16[32,64,384]{2,1,0:T(8,128)(2,1)S(1)}, u32[]{:S(2)}, u32[]{:S(2)}) async-start(bf16[32,64,384]{2,1,0:T(8,128)(2,1)} %shard_map.95), calls=%async_computation | async-start | bytes 3145728 | tf_op jit(solution)/shard_map/all_to_all | solution.py:270
  19.8 78.6 %all-to-all-done = bf16[32,64,384]{2,1,0:T(8,128)(2,1)S(1)} async-done(((bf16[32,64,384]{2,1,0:T(8,128)(2,1)}), bf16[32,64,384]{2,1,0:T(8,128)(2,1)S(1)}, u32[]{:S(2)}, u32[]{:S(2)}) %all-to-all-start) | async-done | bytes 1572896 | tf_op jit(solution)/shard_map/all_to_all | solution.py:270
  98.4 0.0 copy-start.3
  98.4 3.6 %collective-permute-start = (bf16[1040,256]{1,0:T(8,128)(2,1)S(1)}, bf16[1040,256]{1,0:T(8,128)(2,1)S(1)}, u32[]{:S(2)}, u32[]{:S(2)}) collective-permute-start(bf16[1040,256]{1,0:T(8,128)(2,1)S(1)} %constant_dynamic-slice_fusion.1), channel_id=1, source_target_pairs={{32,64},{96,128},{160,192},{224,256},{288,320},{352,384},{416,448}... | collective-permute-start | bytes 1597448 | tf_op jit(solution)/shard_map/ppermute | solution.py:275
  102.1 1.9 %collective-permute-start.1 = (bf16[1024,256]{1,0:T(8,128)(2,1)S(1)}, bf16[1024,256]{1,0:T(8,128)(2,1)S(1)}, u32[]{:S(2)}, u32[]{:S(2)}) collective-permute-start(bf16[1024,256]{1,0:T(8,128)(2,1)S(1)} %constant_dynamic-slice_fusion), channel_id=1, source_target_pairs={{0,32},{64,96},{128,160},{192,224},{256,288},{320,352},{384,416},{... | collective-permute-start | bytes 1572872 | tf_op jit(solution)/shard_map/ppermute | solution.py:278
  104.0 1.7 %shard_map.96 = (f32[1024,256]{1,0:T(8,128)S(1)}, f32[1024,128]{1,0:T(8,128)S(1)}) custom-call(bf16[2048,384]{1,0:T(8,128)(2,1)S(1)} %bitcast.4), custom_call_target="tpu_custom_call" | custom-call | flops 1024 | bytes 1024 | tf_op jit(solution)/shard_map/pallas_call | solution.py:101
  105.8 0.1 collective-permute-done.1.halo_ref
  105.9 0.0 copy-done.3
  105.9 3.5 %shard_map.97.near_ref = bf16[1024,128]{1,0:T(8,128)(2,1)S(1)} custom-call(s32[1,2]{1,0:T(1,128)S(1)} %copy-done.3, bf16[2048,384]{1,0:T(8,128)(2,1)S(1)} %bitcast.5, bf16[1024,256]{1,0:T(8,128)(2,1)S(1)} %collective-permute-done.1.halo_ref), custom_call_target="tpu_custom_call" | custom-call | flops 1024 | bytes 1024 | tf_op jit(solution)/shard_map/pallas_call | solution.py:208
  109.4 1.8 %collective-permute-done.halo_ref = bf16[1040,256]{1,0:T(8,128)(2,1)S(1)} collective-permute-done((bf16[1040,256]{1,0:T(8,128)(2,1)S(1)}, bf16[1040,256]{1,0:T(8,128)(2,1)S(1)}, u32[]{:S(2)}, u32[]{:S(2)}) %collective-permute-start) | collective-permute-done | bytes 532512 | tf_op jit(solution)/shard_map/ppermute | solution.py:275
  111.1 0.0 copy-start
  111.1 0.0 copy-start.1
  111.1 0.0 copy-start.2
  111.1 2.9 %shard_map.98 = bf16[2048,128]{1,0:T(8,128)(2,1)} custom-call(s32[1,2]{1,0:T(1,128)S(1)} %copy-done.3, bf16[2048,384]{1,0:T(8,128)(2,1)S(1)} %bitcast.6, bf16[1040,256]{1,0:T(8,128)(2,1)S(1)} %collective-permute-done.halo_ref, f32[1024,256]{1,0:T(8,128)S(1)} %get-tuple-element.4.sums_ref, f32[1024,128]{1,0:T(8,128)S(1)} %get-tuple-element.5.peak_ref, ...), custom_call_target="tpu_custom_call" | custom-call | flops 1024 | bytes 1024 | tf_op jit(solution)/shard_map/pallas_call | solution.py:208
  114.0 4.3 %all-to-all-start.1 = ((bf16[32,64,128]{2,1,0:T(8,128)(2,1)}), bf16[32,64,128]{2,1,0:T(8,128)(2,1)S(1)}, u32[]{:S(2)}, u32[]{:S(2)}) async-start(bf16[32,64,128]{2,1,0:T(8,128)(2,1)} %bitcast.1), calls=%async_computation.1 | async-start | bytes 1048576 | tf_op jit(solution)/shard_map/all_to_all | solution.py:283
  118.9 33.0 %all-to-all-done.1.att_ref = bf16[32,64,128]{2,1,0:T(8,128)(2,1)S(1)} async-done(((bf16[32,64,128]{2,1,0:T(8,128)(2,1)}), bf16[32,64,128]{2,1,0:T(8,128)(2,1)S(1)}, u32[]{:S(2)}, u32[]{:S(2)}) %all-to-all-start.1) | async-done | bytes 524320 | tf_op jit(solution)/shard_map/all_to_all | solution.py:283
  152.0 0.0 copy-done
  152.0 0.0 copy-done.1
  152.0 0.0 copy-done.2
  152.0 0.3 shard_map.100
  152.2 1.9 %collective-permute-start.2 = (bf16[32,4096]{1,0:T(8,128)(2,1)S(1)}, bf16[32,4096]{1,0:T(8,128)(2,1)S(1)}, u32[]{:S(2)}, u32[]{:S(2)}) collective-permute-start(bf16[32,4096]{1,0:T(8,128)(2,1)S(1)} %shard_map.100), channel_id=1, source_target_pairs={{0,32},{32,64},{64,96},{96,128},{128,160},{160,192},{192,224},{224... | collective-permute-start | bytes 786440 | tf_op jit(solution)/shard_map/ppermute | solution.py:290
  154.2 0.3 shard_map.101
  154.4 2.2 %collective-permute-start.3 = (bf16[32,4096]{1,0:T(8,128)(2,1)S(1)}, bf16[32,4096]{1,0:T(8,128)(2,1)S(1)}, u32[]{:S(2)}, u32[]{:S(2)}) collective-permute-start(bf16[32,4096]{1,0:T(8,128)(2,1)S(1)} %shard_map.101), channel_id=1, source_target_pairs={{0,32},{32,64},{64,96},{96,128},{128,160},{160,192},{192,224},{224... | collective-permute-start | bytes 786440 | tf_op jit(solution)/shard_map/ppermute | solution.py:290
  156.7 1.1 shard_map.99
  157.7 4.3 %collective-permute-done.2 = bf16[32,4096]{1,0:T(8,128)(2,1)S(1)} collective-permute-done((bf16[32,4096]{1,0:T(8,128)(2,1)S(1)}, bf16[32,4096]{1,0:T(8,128)(2,1)S(1)}, u32[]{:S(2)}, u32[]{:S(2)}) %collective-permute-start.2) | collective-permute-done | bytes 262176 | tf_op jit(solution)/shard_map/ppermute | solution.py:290
  162.1 2.8 %collective-permute-done.3 = bf16[32,4096]{1,0:T(8,128)(2,1)S(1)} collective-permute-done((bf16[32,4096]{1,0:T(8,128)(2,1)S(1)}, bf16[32,4096]{1,0:T(8,128)(2,1)S(1)}, u32[]{:S(2)}, u32[]{:S(2)}) %collective-permute-start.3) | collective-permute-done | bytes 262176 | tf_op jit(solution)/shard_map/ppermute | solution.py:290
  164.9 0.8 pad_maximum_fusion
  (2 shorter events, 0.1 us)
Async XLA Ops:
  2.9 95.5 %all-to-all-start = ((bf16[32,64,384]{2,1,0:T(8,128)(2,1)}), bf16[32,64,384]{2,1,0:T(8,128)(2,1)S(1)}, u32[]{:S(2)}, u32[]{:S(2)}) async-start(bf16[32,64,384]{2,1,0:T(8,128)(2,1)} %shard_map.95), calls=%async_computation | async-start | bytes 3145728 | tf_op jit(solution)/shard_map/all_to_all | solution.py:270
  98.4 7.5 %copy-start.3 = (s32[1,2]{1,0:T(1,128)S(1)}, s32[1,2]{1,0:T(1,128)}, u32[]{:S(2)}) copy-start(s32[1,2]{1,0:T(1,128)} %ws_ref.3) | copy-start | bytes 28
  98.4 12.7 %collective-permute-start = (bf16[1040,256]{1,0:T(8,128)(2,1)S(1)}, bf16[1040,256]{1,0:T(8,128)(2,1)S(1)}, u32[]{:S(2)}, u32[]{:S(2)}) collective-permute-start(bf16[1040,256]{1,0:T(8,128)(2,1)S(1)} %constant_dynamic-slice_fusion.1), channel_id=1, source_target_pairs={{32,64},{96,128},{160,192},{224,256},{288,320},{352,384},{416,448}... | collective-permute-start | bytes 1597448 | tf_op jit(solution)/shard_map/ppermute | solution.py:275
  102.1 3.8 %collective-permute-start.1 = (bf16[1024,256]{1,0:T(8,128)(2,1)S(1)}, bf16[1024,256]{1,0:T(8,128)(2,1)S(1)}, u32[]{:S(2)}, u32[]{:S(2)}) collective-permute-start(bf16[1024,256]{1,0:T(8,128)(2,1)S(1)} %constant_dynamic-slice_fusion), channel_id=1, source_target_pairs={{0,32},{64,96},{128,160},{192,224},{256,288},{320,352},{384,416},{... | collective-permute-start | bytes 1572872 | tf_op jit(solution)/shard_map/ppermute | solution.py:278
  111.1 40.8 %copy-start = (f32[16,4096]{1,0:T(8,128)S(1)}, f32[16,4096]{1,0:T(8,128)}, u32[]{:S(2)}) copy-start(f32[16,4096]{1,0:T(8,128)} %mod_ref.5) | copy-start | bytes 786436
  111.1 40.8 %copy-start.1 = (bf16[64,4096]{1,0:T(8,128)(2,1)S(1)}, bf16[64,4096]{1,0:T(8,128)(2,1)}, u32[]{:S(2)}) copy-start(bf16[64,4096]{1,0:T(8,128)(2,1)} %state_ref.3) | copy-start | bytes 1572868
  111.1 40.8 %copy-start.2 = (bf16[64,4096]{1,0:T(8,128)(2,1)S(1)}, bf16[64,4096]{1,0:T(8,128)(2,1)}, u32[]{:S(2)}) copy-start(bf16[64,4096]{1,0:T(8,128)(2,1)} %fresh_ref.3) | copy-start | bytes 1572868
  114.0 38.0 %all-to-all-start.1 = ((bf16[32,64,128]{2,1,0:T(8,128)(2,1)}), bf16[32,64,128]{2,1,0:T(8,128)(2,1)S(1)}, u32[]{:S(2)}, u32[]{:S(2)}) async-start(bf16[32,64,128]{2,1,0:T(8,128)(2,1)} %bitcast.1), calls=%async_computation.1 | async-start | bytes 1048576 | tf_op jit(solution)/shard_map/all_to_all | solution.py:283
  152.2 9.8 %collective-permute-start.2 = (bf16[32,4096]{1,0:T(8,128)(2,1)S(1)}, bf16[32,4096]{1,0:T(8,128)(2,1)S(1)}, u32[]{:S(2)}, u32[]{:S(2)}) collective-permute-start(bf16[32,4096]{1,0:T(8,128)(2,1)S(1)} %shard_map.100), channel_id=1, source_target_pairs={{0,32},{32,64},{64,96},{96,128},{128,160},{160,192},{192,224},{224... | collective-permute-start | bytes 786440 | tf_op jit(solution)/shard_map/ppermute | solution.py:290
  154.4 10.4 %collective-permute-start.3 = (bf16[32,4096]{1,0:T(8,128)(2,1)S(1)}, bf16[32,4096]{1,0:T(8,128)(2,1)S(1)}, u32[]{:S(2)}, u32[]{:S(2)}) collective-permute-start(bf16[32,4096]{1,0:T(8,128)(2,1)S(1)} %shard_map.101), channel_id=1, source_target_pairs={{0,32},{32,64},{64,96},{96,128},{128,160},{160,192},{192,224},{224... | collective-permute-start | bytes 786440 | tf_op jit(solution)/shard_map/ppermute | solution.py:290

commit v8 on v6

--- a/solution.py
+++ b/solution.py
@@ -12,6 +12,7 @@
 NSTEPS = 16
 SCALE = 1.4426950408889634 / HEAD_DIM**0.5
 BLOCK = 256
+FAR_BLOCK = 512
 CHUNKS = 4
 MORE = 16
 VMEM = pl.BlockSpec(memory_space=pltpu.VMEM)
@@ -172,16 +173,16 @@
     other_frame(final, True, ws_ref, qkv_ref, halo_ref, key_ref, value_ref)
 
     def scores(index):
-        rows = pl.ds(pl.multiple_of(first + index * BLOCK, BLOCK), BLOCK)
+        rows = pl.ds(pl.multiple_of(first + index * FAR_BLOCK, FAR_BLOCK), FAR_BLOCK)
         return scores_of(qkv_ref[rows, :HEAD_DIM], key_ref[...])
 
-    blocks = frame_tok // BLOCK
+    blocks = frame_tok // FAR_BLOCK
     after = scores(0)
     for index in range(blocks):
         here = after
         if index + 1 < blocks:
             after = scores(index + 1)
-        rows = pl.ds(index * BLOCK, BLOCK)
+        rows = pl.ds(index * FAR_BLOCK, FAR_BLOCK)
         before = peak_ref[rows, :]
         peak = jnp.maximum(jnp.broadcast_to(jnp.max(here, axis=-1, keepdims=True), before.shape), before)
         spread = jnp.concatenate([peak] * (frame_tok // HEAD_DIM), axis=1)
@@ -191,7 +192,7 @@
         mixed = sums[:, :HEAD_DIM] + sums_ref[rows, :HEAD_DIM] * share
         total = sums[:, HEAD_DIM:] + sums_ref[rows, HEAD_DIM:] * share
         held_ref[rows, :] = (mixed / total).astype(jnp.bfloat16)
-        there = out_ref.at[pl.ds(pl.multiple_of(first + index * BLOCK, BLOCK), BLOCK)]
+        there = out_ref.at[pl.ds(pl.multiple_of(first + index * FAR_BLOCK, FAR_BLOCK), FAR_BLOCK)]
         copies.append(pltpu.make_async_copy(held_ref.at[rows], there, sem_ref.at[1 + index]))
         copies[-1].start()
     for copy in copies:
@@ -204,7 +205,7 @@
     keys = frame_tok if far else FRAMES * frame_tok
     scratch = [pltpu.VMEM((keys, HEAD_DIM), jnp.bfloat16), pltpu.VMEM((keys, 2 * HEAD_DIM), jnp.bfloat16)]
     if far:
-        scratch += [pltpu.VMEM((frame_tok, HEAD_DIM), jnp.bfloat16), pltpu.SemaphoreType.DMA((1 + frame_tok // BLOCK,))]
+        scratch += [pltpu.VMEM((frame_tok, HEAD_DIM), jnp.bfloat16), pltpu.SemaphoreType.DMA((1 + frame_tok // FAR_BLOCK,))]
     return pl.pallas_call(
         functools.partial(far_kernel if far else near_kernel, final),
         in_specs=[SMEM] + [VMEM] * (1 + len(others)),

time: 166 us -> 166 us (level)
  no operation moved by 1% of the time
where the time goes in v8:
time: 166 us
  waiting for transfers between devices  123 us (74%)
  starting transfers between devices  28.6 us (17%)
  Pallas kernels  11.7 us (7%)
    all_to_all x1, waiting for transfers between devices, per_device(): qkv = lax.all_to_all(packed, 'seq', split_axis=0, concat_axis=0, tiled=True)  78.6 us
    all_to_all x1, waiting for transfers between devices, per_device(): lax.all_to_all(attended, 'seq', split_axis=0, concat_axis=0, tiled=True)  33 us
    all_to_all x1, starting transfers between devices, per_device(): qkv = lax.all_to_all(packed, 'seq', split_axis=0, concat_axis=0, tiled=True)  16.9 us
    ppermute x1, waiting for transfers between devices, per_device(): lax.ppermute(passed, 'section', [(i, (i + 1) % sections) for i in range(s...  9.62 us
    pallas_call x2, Pallas kernels, window_part(): pl.pallas_call(functools.partial(far_kernel if far else near_kernel, fina...  6.26 us
    all_to_all x1, starting transfers between devices, per_device(): lax.all_to_all(attended, 'seq', split_axis=0, concat_axis=0, tiled=True)  4.27 us
    ppermute x1, starting transfers between devices, per_device(): far = lax.ppermute(facing, 'section', pairs + [(j, i) for i, j in pairs])  3.6 us
  transfers between devices with their start and end apart: 5, of which 5 were waited for; matrix products, arithmetic and copies ran while one was open for 0% of the time, Pallas kernels for 4%

profile of v8, /device:TPU:34, one launch (start us, length us, event | category | flops | bytes accessed | tf_op | source)
XLA Modules:
  0.0 165.8 jit_solution(341197028452233571)
XLA Ops:
  0.6 2.2 %shard_map.95 = bf16[32,64,384]{2,1,0:T(8,128)(2,1)} custom-call(bf16[64,4096]{1,0:T(8,128)(2,1)} %q_ref.1, bf16[64,4096]{1,0:T(8,128)(2,1)} %k_ref.1, bf16[64,4096]{1,0:T(8,128)(2,1)} %v_ref.1), custom_call_target="tpu_custom_call" | custom-call | tf_op jit(solution)/shard_map/pallas_call | solution.py:53
  2.9 16.9 %all-to-all-start = ((bf16[32,64,384]{2,1,0:T(8,128)(2,1)}), bf16[32,64,384]{2,1,0:T(8,128)(2,1)S(1)}, u32[]{:S(2)}, u32[]{:S(2)}) async-start(bf16[32,64,384]{2,1,0:T(8,128)(2,1)} %shard_map.95), calls=%async_computation | async-start | bytes 3145728 | tf_op jit(solution)/shard_map/all_to_all | solution.py:268
  19.8 78.6 %all-to-all-done = bf16[32,64,384]{2,1,0:T(8,128)(2,1)S(1)} async-done(((bf16[32,64,384]{2,1,0:T(8,128)(2,1)}), bf16[32,64,384]{2,1,0:T(8,128)(2,1)S(1)}, u32[]{:S(2)}, u32[]{:S(2)}) %all-to-all-start) | async-done | bytes 1572896 | tf_op jit(solution)/shard_map/all_to_all | solution.py:268
  98.4 0.0 copy-start.3
  98.4 3.6 %collective-permute-start = (bf16[1040,256]{1,0:T(8,128)(2,1)S(1)}, bf16[1040,256]{1,0:T(8,128)(2,1)S(1)}, u32[]{:S(2)}, u32[]{:S(2)}) collective-permute-start(bf16[1040,256]{1,0:T(8,128)(2,1)S(1)} %constant_dynamic-slice_fusion.1), channel_id=1, source_target_pairs={{32,64},{96,128},{160,192},{224,256},{288,320},{352,384},{416,448}... | collective-permute-start | bytes 1597448 | tf_op jit(solution)/shard_map/ppermute | solution.py:273
  102.1 1.9 %collective-permute-start.1 = (bf16[1024,256]{1,0:T(8,128)(2,1)S(1)}, bf16[1024,256]{1,0:T(8,128)(2,1)S(1)}, u32[]{:S(2)}, u32[]{:S(2)}) collective-permute-start(bf16[1024,256]{1,0:T(8,128)(2,1)S(1)} %constant_dynamic-slice_fusion), channel_id=1, source_target_pairs={{0,32},{64,96},{128,160},{192,224},{256,288},{320,352},{384,416},{... | collective-permute-start | bytes 1572872 | tf_op jit(solution)/shard_map/ppermute | solution.py:276
  104.0 1.7 %shard_map.96 = (f32[1024,256]{1,0:T(8,128)S(1)}, f32[1024,128]{1,0:T(8,128)S(1)}) custom-call(bf16[2048,384]{1,0:T(8,128)(2,1)S(1)} %bitcast.4), custom_call_target="tpu_custom_call" | custom-call | flops 1024 | bytes 1024 | tf_op jit(solution)/shard_map/pallas_call | solution.py:102
  105.8 0.1 collective-permute-done.1.halo_ref
  105.9 0.0 copy-done.3
  105.9 3.5 %shard_map.97.near_ref = bf16[1024,128]{1,0:T(8,128)(2,1)S(1)} custom-call(s32[1,2]{1,0:T(1,128)S(1)} %copy-done.3, bf16[2048,384]{1,0:T(8,128)(2,1)S(1)} %bitcast.5, bf16[1024,256]{1,0:T(8,128)(2,1)S(1)} %collective-permute-done.1.halo_ref), custom_call_target="tpu_custom_call" | custom-call | flops 1024 | bytes 1024 | tf_op jit(solution)/shard_map/pallas_call | solution.py:209
  109.4 1.8 %collective-permute-done.halo_ref = bf16[1040,256]{1,0:T(8,128)(2,1)S(1)} collective-permute-done((bf16[1040,256]{1,0:T(8,128)(2,1)S(1)}, bf16[1040,256]{1,0:T(8,128)(2,1)S(1)}, u32[]{:S(2)}, u32[]{:S(2)}) %collective-permute-start) | collective-permute-done | bytes 532512 | tf_op jit(solution)/shard_map/ppermute | solution.py:273
  111.1 0.0 copy-start
  111.1 0.0 copy-start.1
  111.1 0.0 copy-start.2
  111.1 2.8 %shard_map.98 = bf16[2048,128]{1,0:T(8,128)(2,1)} custom-call(s32[1,2]{1,0:T(1,128)S(1)} %copy-done.3, bf16[2048,384]{1,0:T(8,128)(2,1)S(1)} %bitcast.6, bf16[1040,256]{1,0:T(8,128)(2,1)S(1)} %collective-permute-done.halo_ref, f32[1024,256]{1,0:T(8,128)S(1)} %get-tuple-element.4.sums_ref, f32[1024,128]{1,0:T(8,128)S(1)} %get-tuple-element.5.peak_ref, ...), custom_call_target="tpu_custom_call" | custom-call | flops 1024 | bytes 1024 | tf_op jit(solution)/shard_map/pallas_call | solution.py:209
  114.0 4.3 %all-to-all-start.1 = ((bf16[32,64,128]{2,1,0:T(8,128)(2,1)}), bf16[32,64,128]{2,1,0:T(8,128)(2,1)S(1)}, u32[]{:S(2)}, u32[]{:S(2)}) async-start(bf16[32,64,128]{2,1,0:T(8,128)(2,1)} %bitcast.1), calls=%async_computation.1 | async-start | bytes 1048576 | tf_op jit(solution)/shard_map/all_to_all | solution.py:281
  118.9 33.0 %all-to-all-done.1.att_ref = bf16[32,64,128]{2,1,0:T(8,128)(2,1)S(1)} async-done(((bf16[32,64,128]{2,1,0:T(8,128)(2,1)}), bf16[32,64,128]{2,1,0:T(8,128)(2,1)S(1)}, u32[]{:S(2)}, u32[]{:S(2)}) %all-to-all-start.1) | async-done | bytes 524320 | tf_op jit(solution)/shard_map/all_to_all | solution.py:281
  151.9 0.0 copy-done
  151.9 0.0 copy-done.1
  151.9 0.0 copy-done.2
  151.9 0.4 shard_map.100
  152.4 1.9 %collective-permute-start.2 = (bf16[64,4096]{1,0:T(8,128)(2,1)S(1)}, bf16[64,4096]{1,0:T(8,128)(2,1)S(1)}, u32[]{:S(2)}, u32[]{:S(2)}) collective-permute-start(bf16[64,4096]{1,0:T(8,128)(2,1)S(1)} %shard_map.100), channel_id=1, source_target_pairs={{0,32},{32,64},{64,96},{96,128},{128,160},{160,192},{192,224},{224... | collective-permute-start | bytes 1572872 | tf_op jit(solution)/shard_map/ppermute | solution.py:284
  154.3 1.1 shard_map.99
  155.3 9.6 %collective-permute-done.2 = bf16[64,4096]{1,0:T(8,128)(2,1)S(1)} collective-permute-done((bf16[64,4096]{1,0:T(8,128)(2,1)S(1)}, bf16[64,4096]{1,0:T(8,128)(2,1)S(1)}, u32[]{:S(2)}, u32[]{:S(2)}) %collective-permute-start.2) | collective-permute-done | bytes 524320 | tf_op jit(solution)/shard_map/ppermute | solution.py:284
  165.0 0.8 copy.12
  (2 shorter events, 0.1 us)
Async XLA Ops:
  2.9 95.5 %all-to-all-start = ((bf16[32,64,384]{2,1,0:T(8,128)(2,1)}), bf16[32,64,384]{2,1,0:T(8,128)(2,1)S(1)}, u32[]{:S(2)}, u32[]{:S(2)}) async-start(bf16[32,64,384]{2,1,0:T(8,128)(2,1)} %shard_map.95), calls=%async_computation | async-start | bytes 3145728 | tf_op jit(solution)/shard_map/all_to_all | solution.py:268
  98.4 7.5 %copy-start.3 = (s32[1,2]{1,0:T(1,128)S(1)}, s32[1,2]{1,0:T(1,128)}, u32[]{:S(2)}) copy-start(s32[1,2]{1,0:T(1,128)} %ws_ref.3) | copy-start | bytes 28
  98.4 12.7 %collective-permute-start = (bf16[1040,256]{1,0:T(8,128)(2,1)S(1)}, bf16[1040,256]{1,0:T(8,128)(2,1)S(1)}, u32[]{:S(2)}, u32[]{:S(2)}) collective-permute-start(bf16[1040,256]{1,0:T(8,128)(2,1)S(1)} %constant_dynamic-slice_fusion.1), channel_id=1, source_target_pairs={{32,64},{96,128},{160,192},{224,256},{288,320},{352,384},{416,448}... | collective-permute-start | bytes 1597448 | tf_op jit(solution)/shard_map/ppermute | solution.py:273
  102.1 3.8 %collective-permute-start.1 = (bf16[1024,256]{1,0:T(8,128)(2,1)S(1)}, bf16[1024,256]{1,0:T(8,128)(2,1)S(1)}, u32[]{:S(2)}, u32[]{:S(2)}) collective-permute-start(bf16[1024,256]{1,0:T(8,128)(2,1)S(1)} %constant_dynamic-slice_fusion), channel_id=1, source_target_pairs={{0,32},{64,96},{128,160},{192,224},{256,288},{320,352},{384,416},{... | collective-permute-start | bytes 1572872 | tf_op jit(solution)/shard_map/ppermute | solution.py:276
  111.1 40.8 %copy-start = (f32[16,4096]{1,0:T(8,128)S(1)}, f32[16,4096]{1,0:T(8,128)}, u32[]{:S(2)}) copy-start(f32[16,4096]{1,0:T(8,128)} %mod_ref.3) | copy-start | bytes 786436
  111.1 40.8 %copy-start.1 = (bf16[64,4096]{1,0:T(8,128)(2,1)S(1)}, bf16[64,4096]{1,0:T(8,128)(2,1)}, u32[]{:S(2)}) copy-start(bf16[64,4096]{1,0:T(8,128)(2,1)} %state_ref.1) | copy-start | bytes 1572868
  111.1 40.8 %copy-start.2 = (bf16[64,4096]{1,0:T(8,128)(2,1)S(1)}, bf16[64,4096]{1,0:T(8,128)(2,1)}, u32[]{:S(2)}) copy-start(bf16[64,4096]{1,0:T(8,128)(2,1)} %fresh_ref.1) | copy-start | bytes 1572868
  114.0 38.0 %all-to-all-start.1 = ((bf16[32,64,128]{2,1,0:T(8,128)(2,1)}), bf16[32,64,128]{2,1,0:T(8,128)(2,1)S(1)}, u32[]{:S(2)}, u32[]{:S(2)}) async-start(bf16[32,64,128]{2,1,0:T(8,128)(2,1)} %bitcast.1), calls=%async_computation.1 | async-start | bytes 1048576 | tf_op jit(solution)/shard_map/all_to_all | solution.py:281
  152.4 12.6 %collective-permute-start.2 = (bf16[64,4096]{1,0:T(8,128)(2,1)S(1)}, bf16[64,4096]{1,0:T(8,128)(2,1)S(1)}, u32[]{:S(2)}, u32[]{:S(2)}) collective-permute-start(bf16[64,4096]{1,0:T(8,128)(2,1)S(1)} %shard_map.100), channel_id=1, source_target_pairs={{0,32},{32,64},{64,96},{96,128},{128,160},{160,192},{192,224},{224... | collective-permute-start | bytes 1572872 | tf_op jit(solution)/shard_map/ppermute | solution.py:284

commit v9 on v6

--- a/solution.py
+++ b/solution.py
@@ -216,7 +216,7 @@
     )(window_start, qkv, *others)
 
 
-def velocity_of(step_ref, att_ref, mod_ref):
+def velocity_of(att_ref, gain_ref):
     heads, tok, _ = att_ref.shape
     squares = jnp.zeros((tok, HEAD_DIM), jnp.float32)
     for head in range(heads):
@@ -224,17 +224,15 @@
         squares += a * a
     mean = jnp.sum(squares, axis=-1, keepdims=True) / (heads * HEAD_DIM)
     inverse = jnp.broadcast_to(1.0 / jnp.sqrt(mean + 1e-06), (tok, HEAD_DIM))
-    chosen = lax.broadcasted_iota(jnp.int32, (NSTEPS, HEAD_DIM), 0) == step_ref[0]
     for head in range(heads):
         cols = slice(head * HEAD_DIM, (head + 1) * HEAD_DIM)
-        gain = jnp.sum(jnp.where(chosen, mod_ref[:, cols], 0.0), axis=0, keepdims=True)
-        yield cols, att_ref[head].astype(jnp.float32) * inverse * gain
-
-
-def update_kernel(final, step_ref, att_ref, mod_ref, state_ref, fresh_ref, passed_ref):
+        yield cols, att_ref[head].astype(jnp.float32) * inverse * gain_ref[:1, cols]
+
+
+def update_kernel(final, step_ref, att_ref, gain_ref, state_ref, fresh_ref, passed_ref):
     now = jnp.full((1, HEAD_DIM), step_ref[0], jnp.int32)
     delta = level((now - 1).astype(jnp.float32)) - level(now.astype(jnp.float32))
-    for cols, moving in velocity_of(step_ref, att_ref, mod_ref):
+    for cols, moving in velocity_of(att_ref, gain_ref):
         passed_ref[:, cols] = (state_ref[:, cols].astype(jnp.float32) + delta * moving).astype(jnp.bfloat16)
 
     @pl.when(lax.axis_index("section") == final)
@@ -242,9 +240,24 @@
         passed_ref[...] = fresh_ref[...]
 
 
-def velocity_kernel(step_ref, att_ref, mod_ref, velocity_ref):
-    for cols, moving in velocity_of(step_ref, att_ref, mod_ref):
+def velocity_kernel(step_ref, att_ref, gain_ref, velocity_ref):
+    for cols, moving in velocity_of(att_ref, gain_ref):
         velocity_ref[:, cols] = moving.astype(jnp.bfloat16)
+
+
+def gain_kernel(step_ref, mod_ref, gain_ref):
+    chosen = lax.broadcasted_iota(jnp.int32, mod_ref.shape, 0) == step_ref[0]
+    row = jnp.sum(jnp.where(chosen, mod_ref[...], 0.0), axis=0, keepdims=True)
+    gain_ref[...] = jnp.broadcast_to(row, gain_ref.shape)
+
+
+def gain_of(timestep, modulation):
+    return pl.pallas_call(
+        gain_kernel,
+        in_specs=[SMEM, VMEM],
+        out_specs=VMEM,
+        out_shape=jax.ShapeDtypeStruct((8, modulation.shape[1]), modulation.dtype),
+    )(timestep, modulation)
 
 
 def finish(kernel, timestep, attended, modulation, *others):
@@ -278,10 +291,11 @@
     attended = window_part(True, sections - 1, window_start, qkv, far, sums, peak, near_out)
     attended = attended.reshape(feat // HEAD_DIM, tok_dev, HEAD_DIM)
     attended = lax.all_to_all(attended, "seq", split_axis=0, concat_axis=0, tiled=True)
+    gain = gain_of(timestep, modulation)
     update = functools.partial(update_kernel, sections - 1)
-    passed = finish(update, timestep, attended, modulation, queue_state, fresh_state)
+    passed = finish(update, timestep, attended, gain, queue_state, fresh_state)
     advanced = lax.ppermute(passed, "section", [(i, (i + 1) % sections) for i in range(sections)])
-    velocity = finish(velocity_kernel, timestep, attended, modulation)
+    velocity = finish(velocity_kernel, timestep, attended, gain)
     return velocity, advanced
 
 

time: 166 us -> 167 us (level)
  waiting for transfers between devices: 123 us -> 121 us
    all_to_all x1, waiting for transfers between devices: 33 us -> 31.4 us  [per_device(): lax.all_to_all(attended, 'seq', split_axis=0, concat_axis=0, tiled=True)]
  transfers between devices with their start and end apart: 5 -> 5, of which waited for: 5 -> 5; matrix products, arithmetic and copies ran while one was open for 0% -> 0% of each run, Pallas kernels for 4% -> 5%
where the time goes in v9:
time: 167 us
  waiting for transfers between devices  121 us (72%)
  starting transfers between devices  28.8 us (17%)
  Pallas kernels  13.4 us (8%)
  local copies, waits for them, and re-layouts  1.8 us (1%)
    all_to_all x1, waiting for transfers between devices, per_device(): qkv = lax.all_to_all(packed, 'seq', split_axis=0, concat_axis=0, tiled=True)  78.6 us
    all_to_all x1, waiting for transfers between devices, per_device(): lax.all_to_all(attended, 'seq', split_axis=0, concat_axis=0, tiled=True)  31.4 us
    all_to_all x1, starting transfers between devices, per_device(): qkv = lax.all_to_all(packed, 'seq', split_axis=0, concat_axis=0, tiled=True)  16.9 us
    ppermute x1, waiting for transfers between devices, per_device(): lax.ppermute(passed, 'section', [(i, (i + 1) % sections) for i in range(s...  9.63 us
    pallas_call x2, Pallas kernels, window_part(): pl.pallas_call(functools.partial(far_kernel if far else near_kernel, fina...  6.32 us
    all_to_all x1, starting transfers between devices, per_device(): lax.all_to_all(attended, 'seq', split_axis=0, concat_axis=0, tiled=True)  4.4 us
    ppermute x1, starting transfers between devices, per_device(): far = lax.ppermute(facing, 'section', pairs + [(j, i) for i, j in pairs])  3.6 us
  transfers between devices with their start and end apart: 5, of which 5 were waited for; matrix products, arithmetic and copies ran while one was open for 0% of the time, Pallas kernels for 5%

profile of v9, /device:TPU:34, one launch (start us, length us, event | category | flops | bytes accessed | tf_op | source)
XLA Modules:
  0.0 166.8 jit_solution(7225902934772595833)
XLA Ops:
  0.6 2.2 %shard_map.95 = bf16[32,64,384]{2,1,0:T(8,128)(2,1)} custom-call(bf16[64,4096]{1,0:T(8,128)(2,1)} %q_ref.1, bf16[64,4096]{1,0:T(8,128)(2,1)} %k_ref.1, bf16[64,4096]{1,0:T(8,128)(2,1)} %v_ref.1), custom_call_target="tpu_custom_call" | custom-call | tf_op jit(solution)/shard_map/pallas_call | solution.py:52
  2.9 16.9 %all-to-all-start = ((bf16[32,64,384]{2,1,0:T(8,128)(2,1)}), bf16[32,64,384]{2,1,0:T(8,128)(2,1)S(1)}, u32[]{:S(2)}, u32[]{:S(2)}) async-start(bf16[32,64,384]{2,1,0:T(8,128)(2,1)} %shard_map.95), calls=%async_computation | async-start | bytes 3145728 | tf_op jit(solution)/shard_map/all_to_all | solution.py:280
  19.8 78.6 %all-to-all-done = bf16[32,64,384]{2,1,0:T(8,128)(2,1)S(1)} async-done(((bf16[32,64,384]{2,1,0:T(8,128)(2,1)}), bf16[32,64,384]{2,1,0:T(8,128)(2,1)S(1)}, u32[]{:S(2)}, u32[]{:S(2)}) %all-to-all-start) | async-done | bytes 1572896 | tf_op jit(solution)/shard_map/all_to_all | solution.py:280
  98.4 0.0 copy-start.3
  98.4 3.6 %collective-permute-start = (bf16[1040,256]{1,0:T(8,128)(2,1)S(1)}, bf16[1040,256]{1,0:T(8,128)(2,1)S(1)}, u32[]{:S(2)}, u32[]{:S(2)}) collective-permute-start(bf16[1040,256]{1,0:T(8,128)(2,1)S(1)} %constant_dynamic-slice_fusion.1), channel_id=1, source_target_pairs={{32,64},{96,128},{160,192},{224,256},{288,320},{352,384},{416,448}... | collective-permute-start | bytes 1597448 | tf_op jit(solution)/shard_map/ppermute | solution.py:285
  102.1 1.9 %collective-permute-start.1 = (bf16[1024,256]{1,0:T(8,128)(2,1)S(1)}, bf16[1024,256]{1,0:T(8,128)(2,1)S(1)}, u32[]{:S(2)}, u32[]{:S(2)}) collective-permute-start(bf16[1024,256]{1,0:T(8,128)(2,1)S(1)} %constant_dynamic-slice_fusion), channel_id=1, source_target_pairs={{0,32},{64,96},{128,160},{192,224},{256,288},{320,352},{384,416},{... | collective-permute-start | bytes 1572872 | tf_op jit(solution)/shard_map/ppermute | solution.py:288
  104.0 1.7 %shard_map.96 = (f32[1024,256]{1,0:T(8,128)S(1)}, f32[1024,128]{1,0:T(8,128)S(1)}) custom-call(bf16[2048,384]{1,0:T(8,128)(2,1)S(1)} %bitcast.4), custom_call_target="tpu_custom_call" | custom-call | flops 1024 | bytes 1024 | tf_op jit(solution)/shard_map/pallas_call | solution.py:101
  105.8 0.1 collective-permute-done.1.halo_ref
  105.9 0.0 copy-done.3
  105.9 3.5 %shard_map.97.near_ref = bf16[1024,128]{1,0:T(8,128)(2,1)S(1)} custom-call(s32[1,2]{1,0:T(1,128)S(1)} %copy-done.3, bf16[2048,384]{1,0:T(8,128)(2,1)S(1)} %bitcast.5, bf16[1024,256]{1,0:T(8,128)(2,1)S(1)} %collective-permute-done.1.halo_ref), custom_call_target="tpu_custom_call" | custom-call | flops 1024 | bytes 1024 | tf_op jit(solution)/shard_map/pallas_call | solution.py:208
  109.4 1.8 %collective-permute-done.halo_ref = bf16[1040,256]{1,0:T(8,128)(2,1)S(1)} collective-permute-done((bf16[1040,256]{1,0:T(8,128)(2,1)S(1)}, bf16[1040,256]{1,0:T(8,128)(2,1)S(1)}, u32[]{:S(2)}, u32[]{:S(2)}) %collective-permute-start) | collective-permute-done | bytes 532512 | tf_op jit(solution)/shard_map/ppermute | solution.py:285
  111.1 2.9 %shard_map.98 = bf16[2048,128]{1,0:T(8,128)(2,1)} custom-call(s32[1,2]{1,0:T(1,128)S(1)} %copy-done.3, bf16[2048,384]{1,0:T(8,128)(2,1)S(1)} %bitcast.6, bf16[1040,256]{1,0:T(8,128)(2,1)S(1)} %collective-permute-done.halo_ref, f32[1024,256]{1,0:T(8,128)S(1)} %get-tuple-element.4.sums_ref, f32[1024,128]{1,0:T(8,128)S(1)} %get-tuple-element.5.peak_ref, ...), custom_call_target="tpu_custom_call" | custom-call | flops 1024 | bytes 1024 | tf_op jit(solution)/shard_map/pallas_call | solution.py:208
  114.0 0.0 copy-start.1
  114.0 0.0 copy-start.2
  114.0 4.4 %all-to-all-start.1 = ((bf16[32,64,128]{2,1,0:T(8,128)(2,1)}), bf16[32,64,128]{2,1,0:T(8,128)(2,1)S(1)}, u32[]{:S(2)}, u32[]{:S(2)}) async-start(bf16[32,64,128]{2,1,0:T(8,128)(2,1)} %bitcast.1), calls=%async_computation.1 | async-start | bytes 1048576 | tf_op jit(solution)/shard_map/all_to_all | solution.py:293
  119.1 1.7 shard_map.99.gain_ref
  120.7 31.4 %all-to-all-done.1.att_ref = bf16[32,64,128]{2,1,0:T(8,128)(2,1)S(1)} async-done(((bf16[32,64,128]{2,1,0:T(8,128)(2,1)}), bf16[32,64,128]{2,1,0:T(8,128)(2,1)S(1)}, u32[]{:S(2)}, u32[]{:S(2)}) %all-to-all-start.1) | async-done | bytes 524320 | tf_op jit(solution)/shard_map/all_to_all | solution.py:293
  152.1 0.0 copy-done.1
  152.1 0.0 copy-done.2
  152.1 0.0 copy-start
  152.1 0.9 copy-done
  153.0 0.4 shard_map.101
  153.4 1.9 %collective-permute-start.2 = (bf16[64,4096]{1,0:T(8,128)(2,1)S(1)}, bf16[64,4096]{1,0:T(8,128)(2,1)S(1)}, u32[]{:S(2)}, u32[]{:S(2)}) collective-permute-start(bf16[64,4096]{1,0:T(8,128)(2,1)S(1)} %shard_map.101), channel_id=1, source_target_pairs={{0,32},{32,64},{64,96},{96,128},{128,160},{160,192},{192,224},{224... | collective-permute-start | bytes 1572872 | tf_op jit(solution)/shard_map/ppermute | solution.py:297
  155.3 1.0 shard_map.100
  156.4 9.6 %collective-permute-done.2 = bf16[64,4096]{1,0:T(8,128)(2,1)S(1)} collective-permute-done((bf16[64,4096]{1,0:T(8,128)(2,1)S(1)}, bf16[64,4096]{1,0:T(8,128)(2,1)S(1)}, u32[]{:S(2)}, u32[]{:S(2)}) %collective-permute-start.2) | collective-permute-done | bytes 524320 | tf_op jit(solution)/shard_map/ppermute | solution.py:297
  166.0 0.8 copy.12
  (2 shorter events, 0.1 us)
Async XLA Ops:
  2.9 95.5 %all-to-all-start = ((bf16[32,64,384]{2,1,0:T(8,128)(2,1)}), bf16[32,64,384]{2,1,0:T(8,128)(2,1)S(1)}, u32[]{:S(2)}, u32[]{:S(2)}) async-start(bf16[32,64,384]{2,1,0:T(8,128)(2,1)} %shard_map.95), calls=%async_computation | async-start | bytes 3145728 | tf_op jit(solution)/shard_map/all_to_all | solution.py:280
  98.4 7.5 %copy-start.3 = (s32[1,2]{1,0:T(1,128)S(1)}, s32[1,2]{1,0:T(1,128)}, u32[]{:S(2)}) copy-start(s32[1,2]{1,0:T(1,128)} %ws_ref.3) | copy-start | bytes 28
  98.4 12.7 %collective-permute-start = (bf16[1040,256]{1,0:T(8,128)(2,1)S(1)}, bf16[1040,256]{1,0:T(8,128)(2,1)S(1)}, u32[]{:S(2)}, u32[]{:S(2)}) collective-permute-start(bf16[1040,256]{1,0:T(8,128)(2,1)S(1)} %constant_dynamic-slice_fusion.1), channel_id=1, source_target_pairs={{32,64},{96,128},{160,192},{224,256},{288,320},{352,384},{416,448}... | collective-permute-start | bytes 1597448 | tf_op jit(solution)/shard_map/ppermute | solution.py:285
  102.1 3.8 %collective-permute-start.1 = (bf16[1024,256]{1,0:T(8,128)(2,1)S(1)}, bf16[1024,256]{1,0:T(8,128)(2,1)S(1)}, u32[]{:S(2)}, u32[]{:S(2)}) collective-permute-start(bf16[1024,256]{1,0:T(8,128)(2,1)S(1)} %constant_dynamic-slice_fusion), channel_id=1, source_target_pairs={{0,32},{64,96},{128,160},{192,224},{256,288},{320,352},{384,416},{... | collective-permute-start | bytes 1572872 | tf_op jit(solution)/shard_map/ppermute | solution.py:288
  114.0 38.1 %copy-start.1 = (bf16[64,4096]{1,0:T(8,128)(2,1)S(1)}, bf16[64,4096]{1,0:T(8,128)(2,1)}, u32[]{:S(2)}) copy-start(bf16[64,4096]{1,0:T(8,128)(2,1)} %state_ref.1) | copy-start | bytes 1572868
  114.0 38.1 %copy-start.2 = (bf16[64,4096]{1,0:T(8,128)(2,1)S(1)}, bf16[64,4096]{1,0:T(8,128)(2,1)}, u32[]{:S(2)}) copy-start(bf16[64,4096]{1,0:T(8,128)(2,1)} %fresh_ref.1) | copy-start | bytes 1572868
  114.0 38.1 %all-to-all-start.1 = ((bf16[32,64,128]{2,1,0:T(8,128)(2,1)}), bf16[32,64,128]{2,1,0:T(8,128)(2,1)S(1)}, u32[]{:S(2)}, u32[]{:S(2)}) async-start(bf16[32,64,128]{2,1,0:T(8,128)(2,1)} %bitcast.1), calls=%async_computation.1 | async-start | bytes 1048576 | tf_op jit(solution)/shard_map/all_to_all | solution.py:293
  152.1 0.9 copy-start
  153.4 12.6 %collective-permute-start.2 = (bf16[64,4096]{1,0:T(8,128)(2,1)S(1)}, bf16[64,4096]{1,0:T(8,128)(2,1)S(1)}, u32[]{:S(2)}, u32[]{:S(2)}) collective-permute-start(bf16[64,4096]{1,0:T(8,128)(2,1)S(1)} %shard_map.101), channel_id=1, source_target_pairs={{0,32},{32,64},{64,96},{96,128},{128,160},{160,192},{192,224},{224... | collective-permute-start | bytes 1572872 | tf_op jit(solution)/shard_map/ppermute | solution.py:297
